TPU v7x, 512 devices: a whole 4x4x16 slice. The times are simulated.
512 devices in a mesh: occ: 16 (over y_lo, x, core), vir: 32 (over z, y_hi).
Axes of the slice: x: 4, y: 4 (y_hi: 2, y_lo: 2; y = y_hi * 2 + y_lo), z: 16, core: 2. Of those that a mesh axis runs over, the one named last changes fastest.
Arguments:
- amps: bfloat16 [16384, 3072], P('occ', 'vir'), may hold values from -6 to 6
- ints: bfloat16 [3072, 16384], P(None, 'vir'), may hold values from -0.109375 to 0.109375
- amp_mask: int32 [512, 6], P('occ'), may hold values 0 or 1
- keep_mask: int32 [512, 32], P('occ', 'vir'), may hold values 0 or 1
- owners: int32 [512, 1], P('occ'), may hold values from 0 to 15; in each aligned block of 32 rows (0 to 31, 32 to 63, ...) at most 4 rows name the same one
- occ_energy: bfloat16 [16384], P('occ'), may hold values from -2 to -0.5
- vir_energy: float32 [16384], P('vir'), may hold values from 0.5 to 3
- mix: bfloat16 [16, 32, 32], P('occ'), may hold values from -4 to 4
Outputs:
- owned: bfloat16 [1024, 32, 16384], P('occ', None, 'vir')
Inputs may be any that keep to these rules, and one draw needn't show every extreme that they name: `owners`: in the row tiles of one index of occ no owner appears more than 4 times; in every draw some owner appears exactly 4 times in some device's tiles.
All inputs are finite; a program needn't handle non-finite values. No bound on the sum of `amp_mask` or of `keep_mask` on one device may be relied on, other than what follows from the above.
Results may differ from a plain program's by a relative error of at most 0.0049.
Values may be sent and summed in bfloat16 or wider, within the bound.
No kernel may reach another device: no remote copies, remote signals or barrier semaphores. Data moves between devices by JAX's collectives and lax.ppermute only.
A program may use at most 64 MiB of HBM per device.

v0:
```python
import jax
import jax.numpy as jnp
from jax import lax
from jax.sharding import Mesh
from jax.sharding import PartitionSpec as P

VIR = ("vir_0", "vir_1")


def gathered_by_axis(x, axes, dim):
    result = x
    for number in range(len(axes) - 1, -1, -1):
        result = lax.all_gather(result, axes[number], axis=dim, tiled=True)
    return result


def shards(amps, ints, amp_mask, keep_mask, owners, occ_energy, vir_energy, mix):
    tiles_dev, k_tiles = amp_mask.shape
    row_count, k_width = amps.shape
    tile_rows = row_count // tiles_dev
    col_count = ints.shape[1]
    owner_count = lax.axis_size("occ")
    capacity = max(2, 2 * tiles_dev // owner_count)
    slot_count = owner_count * capacity
    k_first = lax.axis_index(VIR) * k_width
    column_tile = (k_first + jnp.arange(k_width, dtype=jnp.int32)) // (ints.shape[0] // k_tiles)
    select = (column_tile[None, :] == jnp.arange(k_tiles, dtype=jnp.int32)[:, None]).astype(
        jnp.float32
    )
    col_mask = jnp.dot(amp_mask.astype(jnp.float32), select).astype(jnp.bfloat16)
    masked = amps.reshape(tiles_dev, tile_rows, k_width) * col_mask[:, None, :]
    destination = owners[:, 0]
    same_owner = destination[:, None] == destination[None, :]
    earlier = jnp.arange(tiles_dev)[:, None] > jnp.arange(tiles_dev)[None, :]
    position = jnp.sum((same_owner & earlier).astype(jnp.int32), axis=1)
    slot_index = destination * capacity + position
    routing = (slot_index[None, :] == jnp.arange(slot_count, dtype=jnp.int32)[:, None]).astype(
        jnp.bfloat16
    )
    send_energy = jnp.dot(
        routing, occ_energy.reshape(tiles_dev, tile_rows), preferred_element_type=jnp.float32
    ).astype(jnp.bfloat16)
    keep_flag = keep_mask.astype(jnp.bfloat16)
    weight = mix[0]
    ladder = jnp.dot(
        gathered_by_axis(masked.reshape(row_count, k_width), VIR, 1),
        ints,
        preferred_element_type=jnp.float32,
    )
    kept_tiles = ladder.astype(jnp.bfloat16).reshape(tiles_dev, tile_rows * col_count) * keep_flag
    send_tiles = jnp.dot(routing, kept_tiles, preferred_element_type=jnp.float32).astype(
        jnp.bfloat16
    )
    tiles_in = lax.all_to_all(
        send_tiles.reshape(owner_count, capacity, tile_rows, col_count),
        "occ",
        split_axis=0,
        concat_axis=0,
        tiled=True,
    )
    energy_in = lax.all_to_all(
        send_energy.reshape(owner_count, capacity, tile_rows),
        "occ",
        split_axis=0,
        concat_axis=0,
        tiled=True,
    )
    mixed_rows = jnp.einsum("ij,oajc->oaic", weight, tiles_in, preferred_element_type=jnp.float32)
    denominator = vir_energy - energy_in.astype(jnp.float32)[..., None]
    owned = (mixed_rows / denominator).astype(jnp.bfloat16)
    owned = owned.reshape(slot_count, tile_rows, col_count)
    return owned


def solution(mesh):
    split = Mesh(mesh.devices.reshape(mesh.shape["occ"], 16, 2), ("occ", "vir_0", "vir_1"))
    in_specs = (
        P("occ", VIR),
        P(None, VIR),
        P("occ", None),
        P("occ", VIR),
        P("occ", None),
        P("occ"),
        P(VIR),
        P("occ", None, None),
    )
    out_specs = P("occ", None, VIR)
    return jax.shard_map(
        shards, mesh=split, in_specs=in_specs, out_specs=out_specs, check_vma=False
    )
```

profile of v0, /device:TPU:1, one launch (start us, length us, event | category | flops | bytes accessed | tf_op | source)
XLA Modules:
  0.0 167.9 jit_solution(12814308627202270587)
XLA Ops:
  6.5 0.0 copy-start
  6.5 0.0 all-gather.2.cloned.1.call-start
  6.6 1.0 fusion.1
  7.6 0.8 copy.19
  8.4 1.1 mul.43
  9.5 7.6 %all_gather.6 = bf16[1024,192]{0,1:T(8,128)(2,1)} all-gather(bf16[1024,96]{0,1:T(8,128)(2,1)S(1)} %mul.43), channel_id=1, replica_groups=mesh['occ'=16,'vir_0'=16,'vir_1'=2] {'vir_1'}, dimensions={1}, use_global_device_ids=true | all-gather | bytes 589824 | tf_op jit(solution)/shard_map/all_gather | solution.py:13
  17.1 0.0 all-gather.2.cloned.1.call-update
  17.1 0.8 reshape.51
  17.9 0.9 convert_reduce_fusion
  18.8 0.7 multiply_add_fusion
  19.4 0.2 convolution_convert_fusion.3
  19.6 0.7 copy.20
  20.3 10.6 %all-to-all-start.1 = ((bf16[16,4,32]{2,1,0:T(4,128)(2,1)}), bf16[16,4,32]{2,1,0:T(4,128)(2,1)S(1)}, u32[]{:S(2)}, u32[]{:S(2)}) async-start(bf16[16,4,32]{2,1,0:T(4,128)(2,1)} %bitcast.8), calls=%async_computation.1 | async-start | bytes 32768 | tf_op jit(solution)/shard_map/all_to_all | solution.py:61
  30.9 0.7 convert_bitcast_fusion
  31.5 76.5 %all-gather.2.cloned.1.call-done = bf16[1024,3072]{0,1:T(8,128)(2,1)} async-done(((bf16[1024,192]{0,1:T(8,128)(2,1)}), bf16[1024,3072]{0,1:T(8,128)(2,1)}) %all-gather.2.cloned.1.call-update) | async-done | bytes 6291472 | tf_op jit(solution)/shard_map/all_gather | solution.py:13
  108.1 0.0 copy-done
  108.1 7.2 %convolution_convert_fusion.1 = bf16[1024,512]{1,0:T(8,128)(2,1)} fusion(bf16[1024,3072]{0,1:T(8,128)(2,1)} %all-gather.2.cloned.1.call-done, bf16[3072,512]{1,0:T(8,128)(2,1)S(1)} %copy-done), kind=kOutput, calls=%fused_computation.3 | convolution fusion | flops 3221749760 | bytes 10485760 | tf_op jit(solution)/shard_map/dot_general | solution.py:45
  115.3 2.3 %reshape.49 = bf16[32,16384]{1,0:T(8,128)(2,1)} reshape(bf16[1024,512]{1,0:T(8,128)(2,1)} %convolution_convert_fusion.1) | data formatting | bytes 2097152 | tf_op jit(solution)/shard_map/reshape | solution.py:50
  117.6 2.0 %convolution_convert_fusion = bf16[64,16384]{1,0:T(8,128)(2,1)S(1)} fusion(bf16[32,16384]{1,0:T(8,128)(2,1)} %reshape.49, bf16[32]{0:T(256)(128)(2,1)S(1)} %convert_bitcast_fusion, s32[32]{0:T(128)S(1)} %multiply_add_fusion), kind=kOutput, calls=%fused_computation | convolution fusion | flops 68683776 | bytes 3145920 | tf_op jit(solution)/shard_map/dot_general | solution.py:51
  119.6 2.1 %copy.22 = bf16[8,8,32,512]{3,2,1,0:T(8,128)(2,1)} copy(bf16[8,8,32,512]{3,1,2,0:T(8,128)(2,1)S(1)} %bitcast.28) | data formatting | bytes 4194304
  121.7 0.0 copy-start.1
  121.7 0.0 copy-start.2
  121.7 0.0 all-to-all-done.1
  121.7 8.0 %all-to-all-start = ((bf16[16,4,32,512]{3,2,1,0:T(8,128)(2,1)}), bf16[16,4,32,512]{3,2,1,0:T(8,128)(2,1)}, u32[]{:S(2)}, u32[]{:S(2)}) async-start(bf16[16,4,32,512]{3,2,1,0:T(8,128)(2,1)} %bitcast.27), calls=%async_computation | async-start | bytes 4194304 | tf_op jit(solution)/shard_map/all_to_all | solution.py:54
  129.7 27.7 %all-to-all-done = bf16[16,4,32,512]{3,2,1,0:T(8,128)(2,1)} async-done(((bf16[16,4,32,512]{3,2,1,0:T(8,128)(2,1)}), bf16[16,4,32,512]{3,2,1,0:T(8,128)(2,1)}, u32[]{:S(2)}, u32[]{:S(2)}) %all-to-all-start) | async-done | bytes 2097184 | tf_op jit(solution)/shard_map/all_to_all | solution.py:54
  157.4 0.0 copy-done.1
  157.4 0.0 copy-done.2
  157.4 3.7 %fusion = bf16[16,4,32,512]{3,2,1,0:T(8,128)(2,1)} fusion(bf16[16,4,32,512]{3,2,1,0:T(8,128)(2,1)} %all-to-all-done, f32[16,4,32]{2,1,0:T(4,128)S(1)} %convert_element_type.40, f32[512]{0:T(512)S(1)} %copy-done.2, bf16[1,32,32]{2,1,0:T(8,128)(2,1)S(1)} %copy-done.1), kind=kOutput, calls=%fused_computation.2 | convolution fusion | flops 70254592 | bytes 4206592 | tf_op jit(solution)/shard_map/ij,oajc->oaic/dot_general | solution.py:68
  (3 shorter events, 0.1 us)
Async XLA Ops:
  6.5 101.5 %copy-start = (bf16[3072,512]{1,0:T(8,128)(2,1)S(1)}, bf16[3072,512]{1,0:T(8,128)(2,1)}, u32[]{:S(2)}) copy-start(bf16[3072,512]{1,0:T(8,128)(2,1)} %param.9) | copy-start | bytes 9437188
  6.5 101.5 %all-gather.2.cloned.1.call-start = ((), (), s32[]{:S(2)}) async-start(), calls=%async_computation.2 | async-start | bytes 6684672 | tf_op jit(solution)/shard_map/all_gather | solution.py:13
  20.3 101.3 %all-to-all-start.1 = ((bf16[16,4,32]{2,1,0:T(4,128)(2,1)}), bf16[16,4,32]{2,1,0:T(4,128)(2,1)S(1)}, u32[]{:S(2)}, u32[]{:S(2)}) async-start(bf16[16,4,32]{2,1,0:T(4,128)(2,1)} %bitcast.8), calls=%async_computation.1 | async-start | bytes 32768 | tf_op jit(solution)/shard_map/all_to_all | solution.py:61
  121.7 35.7 %copy-start.1 = (bf16[1,32,32]{2,1,0:T(8,128)(2,1)S(1)}, bf16[1,32,32]{2,1,0:T(8,128)(2,1)}, u32[]{:S(2)}) copy-start(bf16[1,32,32]{2,1,0:T(8,128)(2,1)} %param.15) | copy-start | bytes 6148
  121.7 35.7 %copy-start.2 = (f32[512]{0:T(512)S(1)}, f32[512]{0:T(512)}, u32[]{:S(2)}) copy-start(f32[512]{0:T(512)} %param.14) | copy-start | bytes 6148
  121.7 35.7 %all-to-all-start = ((bf16[16,4,32,512]{3,2,1,0:T(8,128)(2,1)}), bf16[16,4,32,512]{3,2,1,0:T(8,128)(2,1)}, u32[]{:S(2)}, u32[]{:S(2)}) async-start(bf16[16,4,32,512]{3,2,1,0:T(8,128)(2,1)} %bitcast.27), calls=%async_computation | async-start | bytes 4194304 | tf_op jit(solution)/shard_map/all_to_all | solution.py:54
Sparse Core Ops, SparseCore 0:
  17.2 90.8 all-gather.1
where the time goes:
time: 168 us
  waiting for transfers between devices  104 us (62%)
  starting transfers between devices  18.6 us (11%)
  matrix products  14 us (8%)
  between operations  13.4 us (8%)
  blocking collectives  7.56 us (4%)
  local copies, waits for them, and re-layouts  6.73 us (4%)
  other arithmetic  3.32 us (2%)
    all_gather x1, waiting for transfers between devices, gathered_by_axis(): result = lax.all_gather(result, axes[number], axis=dim, tiled=True)  76.5 us
    all_to_all x1, waiting for transfers between devices, shards(): lax.all_to_all(send_tiles.reshape(owner_count, capacity, tile_rows, col_c...  27.7 us
    all_to_all x1, starting transfers between devices, shards(): lax.all_to_all(send_energy.reshape(owner_count, capacity, tile_rows), 'oc...  10.6 us
    all_to_all x1, starting transfers between devices, shards(): lax.all_to_all(send_tiles.reshape(owner_count, capacity, tile_rows, col_c...  8.02 us
    all_gather x1, blocking collectives, gathered_by_axis(): result = lax.all_gather(result, axes[number], axis=dim, tiled=True)  7.56 us
    dot_general x1, matrix products, shards(): jnp.dot(gathered_by_axis(masked.reshape(row_count, k_width), VIR, 1), int...  7.2 us
    dot_general x1, matrix products, shards(): jnp.einsum('ij,oajc->oaic', weight, tiles_in, preferred_element_type=jnp....  3.65 us
  transfers between devices with their start and end apart: 3, of which 2 were waited for; matrix products, arithmetic and copies ran while one was open for 10% of the time, Pallas kernels for 0%

commit v1 on v0

v1 whole, which is shorter than its diff:
```python
import jax
import jax.numpy as jnp
from jax import lax
from jax.experimental import pallas as pl
from jax.experimental.pallas import tpu as pltpu
from jax.sharding import Mesh
from jax.sharding import PartitionSpec as P

OCC = ("ylo", "x", "core")
VIR = ("z", "yhi")
F32 = jnp.float32
BF16 = jnp.bfloat16
I32 = jnp.int32


def iota(shape, dim):
    return lax.broadcasted_iota(I32, shape, dim)


def dot(a, b, da=1, db=0):
    return lax.dot_general(a, b, (((da,), (db,)), ((), ())), preferred_element_type=F32)


def encode(v):
    a = jnp.abs(v)
    small = a < 2.0**-60
    b = jnp.where(small, a * 2.0**60, a)
    e = jnp.floor(jnp.log2(jnp.maximum(b, 2.0**-70)))
    q = b * jnp.exp2(7.0 - e)
    up = q >= 255.5
    down = q < 127.5
    q = q * jnp.where(up, 0.5, jnp.where(down, 2.0, 1.0))
    e = e + jnp.where(up, 1.0, jnp.where(down, -1.0, 0.0)) - jnp.where(small, 60.0, 0.0)
    code = (e + 127.0) * 128.0 + (jnp.floor(q + 0.5) - 128.0)
    code = jnp.where(a < 2.0**-126, 0.0, code)
    return jnp.where(v < 0.0, -code, code).astype(I32)


def decode(c):
    c = c.astype(I32)
    m = jnp.abs(c)
    f = ((m & 127) + 128).astype(F32) * (1.0 / 128.0)
    v = f * jnp.exp2((m >> 7).astype(F32) - 127.0)
    v = jnp.where(m == 0, 0.0, v)
    return jnp.where(c < 0, -v, v).astype(BF16)


def prep_kernel(tile_k, kfirst, amps_ref, owners_ref, mask_ref, keep_ref, energy_ref, code_ref, slot_ref, meta_ref):
    k_width, rows = amps_ref.shape
    tiles, k_tiles = mask_ref.shape
    owners = meta_ref.shape[0]
    tile_rows = rows // tiles
    half = rows // 2
    own = owners_ref[...].astype(F32)
    i = iota((tiles, tiles), 0)
    j = iota((tiles, tiles), 1)
    own_row = jnp.sum(jnp.where(i == j, own, 0.0), axis=0, keepdims=True)
    earlier = jnp.where((own_row == own) & (j < i), 1.0, 0.0)
    before = jnp.where(own_row < own, 1.0, 0.0)
    k = jnp.sum(earlier, axis=1, keepdims=True)
    rank = jnp.sum(before, axis=1, keepdims=True) + k
    place = own * 2.0 + jnp.where(k >= 2.0, 1.0, 0.0)
    slot_ref[...] = jnp.sum(
        jnp.where(rank == j.astype(F32), place, 0.0), axis=0, keepdims=True
    ).astype(I32)
    lane = iota((tiles, 128), 1)
    keep = keep_ref[...].astype(F32)
    cols = jnp.where(
        lane == 0, rank, jnp.where(lane == 1, own, jnp.where(lane == 2, k, keep))
    ).astype(BF16)
    spread = jnp.where(iota((rows, tiles), 0) // tile_rows == iota((rows, tiles), 1), 1.0, 0.0).astype(BF16)
    per_row = dot(spread, cols)
    per_col = dot(cols, spread, 0, 1)
    column_tile = (kfirst[0] + iota((k_width, k_tiles), 0)) // tile_k
    select = jnp.where(column_tile == iota((k_width, k_tiles), 1), 1.0, 0.0).astype(BF16)
    present = dot(select, mask_ref[...].astype(F32).astype(BF16), 1, 1).astype(BF16)
    present = dot(present, spread, 1, 1)
    masked = jnp.where(present > 0.5, amps_ref[...].astype(F32), 0.0).astype(BF16)
    r = per_row[:, 0:1].astype(I32)
    target = (r % 2) * half + (r // 2) * tile_rows + iota((rows, 1), 0) % tile_rows
    moved = jnp.where(target == iota((rows, rows), 1), 1.0, 0.0).astype(BF16)
    code = encode(dot(masked, moved))
    code_ref[0] = code[:, :half].astype(jnp.int16)
    code_ref[1] = code[:, half:].astype(jnp.int16)
    energy = jnp.where(per_col[3:4] > 0.5, energy_ref[...].astype(F32), 0.0)
    to = per_col[1:2].astype(I32) * tile_rows + iota((1, rows), 1) % tile_rows
    big = iota((owners * tile_rows, rows), 0)
    sent = jnp.where(big == to, energy, 0.0).astype(BF16)
    position = jnp.where(per_row[:, 2:3].astype(I32) == iota((rows, 128), 1), 1.0, 0.0).astype(BF16)
    meta = dot(sent, position)
    start = jnp.sum(
        jnp.where(own_row < (iota((owners * tile_rows, tiles), 0) // tile_rows).astype(F32), 1.0, 0.0),
        axis=1,
        keepdims=True,
    ).astype(I32)
    odd = (start % 2).astype(F32)
    meta = jnp.where(iota(meta.shape, 1) == 4, odd, meta)
    meta_ref[...] = meta.astype(BF16).reshape(meta_ref.shape)


def prep(kfirst, tile_k, amps_t, owners, amp_mask, keep_mask, energy, owner_count):
    k_width, rows = amps_t.shape
    tile_rows = rows // amp_mask.shape[0]
    vmem = pl.BlockSpec(memory_space=pltpu.VMEM)

    def kernel(*refs):
        prep_kernel(tile_k, *refs)

    return pl.pallas_call(
        kernel,
        out_shape=(
            jax.ShapeDtypeStruct((2, k_width, rows // 2), jnp.int16),
            jax.ShapeDtypeStruct((1, amp_mask.shape[0]), I32),
            jax.ShapeDtypeStruct((owner_count, tile_rows, 128), BF16),
        ),
        in_specs=[pl.BlockSpec(memory_space=pltpu.SMEM)] + [vmem] * 5,
        out_specs=(vmem, vmem, vmem),
        compiler_params=pltpu.CompilerParams(vmem_limit_bytes=32 << 20),
        name="prep",
    )(kfirst, amps_t, owners, amp_mask, keep_mask, energy)


def place_tiles(slot, h, acc, out_ref):
    tile_rows = out_ref.shape[3]
    for n in range(acc.shape[0] // tile_rows):
        at = slot[0, 2 * n + h]
        out_ref[0, at // 2, at % 2] = acc[n * tile_rows : (n + 1) * tile_rows].astype(BF16)


def near_kernel(slot, where, code_ref, ints_ref, amps_ref, out_ref, acc_ref):
    step = pl.program_id(0)
    a = decode(code_ref[...]).T
    amps_ref[...] = a
    part = dot(a, ints_ref[...])

    @pl.when(step == 0)
    def _():
        acc_ref[...] = part

    @pl.when(step > 0)
    def _():
        acc_ref[...] += part

    @pl.when(step == pl.num_programs(0) - 1)
    def _():
        place_tiles(slot, where[0], acc_ref, out_ref)


def near(slot, where, code, ints, owner_count, tile_rows):
    depth, rows = code.shape
    width = ints.shape[1]
    steps = 4
    block = depth // steps
    return pl.pallas_call(
        near_kernel,
        out_shape=(
            jax.ShapeDtypeStruct((rows, depth), BF16),
            jax.ShapeDtypeStruct((2, owner_count, 2, tile_rows, width), BF16),
        ),
        grid_spec=pltpu.PrefetchScalarGridSpec(
            num_scalar_prefetch=2,
            grid=(steps,),
            in_specs=[
                pl.BlockSpec((block, rows), lambda s, *_: (s, 0)),
                pl.BlockSpec((block, width), lambda s, *_: (s, 0)),
            ],
            out_specs=(
                pl.BlockSpec((rows, block), lambda s, *_: (0, s)),
                pl.BlockSpec(
                    (1, owner_count, 2, tile_rows, width), lambda s, slot, where: (where[0], 0, 0, 0, 0)
                ),
            ),
            scratch_shapes=[pltpu.VMEM((rows, width), F32)],
        ),
        compiler_params=pltpu.CompilerParams(vmem_limit_bytes=40 << 20),
        cost_estimate=pl.CostEstimate(
            flops=2 * rows * depth * width, bytes_accessed=11 << 20, transcendentals=rows * depth
        ),
        name="near",
    )(slot, where, code, ints)


def far_kernel(slot, where, a0_ref, a1_ref, mine_ref, other_ref, _, out_ref):
    acc = dot(a0_ref[...], mine_ref[...]) + dot(a1_ref[...], other_ref[...])
    place_tiles(slot, where[0], acc, out_ref)


def far(slot, where, amps, mine, other, send):
    rows, depth = amps.shape
    width = mine.shape[1]
    owner_count, tile_rows = send.shape[1], send.shape[3]
    return pl.pallas_call(
        far_kernel,
        out_shape=jax.ShapeDtypeStruct(send.shape, BF16),
        grid_spec=pltpu.PrefetchScalarGridSpec(
            num_scalar_prefetch=2,
            grid=(1,),
            in_specs=[
                pl.BlockSpec((rows, depth // 2), lambda s, slot, where: (0, where[1])),
                pl.BlockSpec((rows, depth // 2), lambda s, slot, where: (0, 1 - where[1])),
                pl.BlockSpec(mine.shape, lambda s, *_: (0, 0)),
                pl.BlockSpec(mine.shape, lambda s, *_: (0, 0)),
                pl.BlockSpec(memory_space=pl.ANY),
            ],
            out_specs=pl.BlockSpec(
                (1, owner_count, 2, tile_rows, width), lambda s, slot, where: (1 - where[0], 0, 0, 0, 0)
            ),
        ),
        input_output_aliases={6: 0},
        compiler_params=pltpu.CompilerParams(vmem_limit_bytes=40 << 20),
        cost_estimate=pl.CostEstimate(
            flops=2 * rows * depth * width, bytes_accessed=8 << 20, transcendentals=0
        ),
        name="far",
    )(slot, where, amps, amps, mine, other, send)


def update_kernel(recv_ref, meta_ref, mix_ref, vir_ref, out_ref):
    meta = meta_ref[0].astype(F32)
    odd = meta[0:1, 4:5] > 0.5
    weight = mix_ref[0]
    energies = vir_ref[...]
    for k in range(4):
        energy = meta[:, k : k + 1]
        tile = jnp.where(odd, recv_ref[(k + 1) % 2, 0, k // 2].astype(F32), recv_ref[k % 2, 0, k // 2].astype(F32))
        tile = jnp.where(energy != 0.0, tile, 0.0).astype(BF16)
        out_ref[k] = (dot(weight, tile) / (energies - energy)).astype(BF16)


def update(recv, meta, mix, vir_energy):
    _, owner_count, two, tile_rows, width = recv.shape
    return pl.pallas_call(
        update_kernel,
        out_shape=jax.ShapeDtypeStruct((owner_count * 4, tile_rows, width), BF16),
        grid=(owner_count,),
        in_specs=[
            pl.BlockSpec((2, 1, two, tile_rows, width), lambda s: (0, s, 0, 0, 0)),
            pl.BlockSpec((1, tile_rows, 128), lambda s: (s, 0, 0)),
            pl.BlockSpec(mix.shape, lambda s: (0, 0, 0)),
            pl.BlockSpec((1, width), lambda s: (0, 0)),
        ],
        out_specs=pl.BlockSpec((4, tile_rows, width), lambda s: (s, 0, 0)),
        name="update",
    )(recv, meta, mix, vir_energy)


def shards(amps, ints, amp_mask, keep_mask, owners, occ_energy, vir_energy, mix):
    tiles_dev, k_tiles = amp_mask.shape
    rows, k_width = amps.shape
    tile_rows = rows // tiles_dev
    depth, width = ints.shape
    owner_count = lax.axis_size(OCC)
    h = lax.axis_index("yhi").astype(I32)
    c = lax.axis_index("core").astype(I32)
    kfirst = (lax.axis_index(VIR) * k_width).astype(I32).reshape(1)
    where = jnp.stack([h, c])
    code, slot, meta = prep(
        kfirst, depth // k_tiles, amps.T, owners, amp_mask, keep_mask, occ_energy.reshape(1, rows), owner_count
    )
    code = lax.all_to_all(code, "yhi", 0, 0, tiled=True)
    part = lax.dynamic_slice(ints, (c * (depth // 2), 0), (depth // 2, width))
    mine = lax.ppermute(part, ("ylo", "yhi"), [(n, 3 - n) for n in range(4)])
    other = lax.ppermute(mine, "core", [(0, 1), (1, 0)])
    meta = lax.all_to_all(meta, OCC, 0, 0, tiled=True)
    code = lax.all_gather(code.reshape(2 * k_width, rows // 2), "z", axis=0, tiled=True)
    decoded, send = near(slot, where, code, ints, owner_count, tile_rows)
    send = far(slot, where, decoded, mine, other, send)
    recv = lax.all_to_all(
        send.reshape(2 * owner_count, 2, tile_rows, width), ("yhi",) + OCC, 0, 0, tiled=True
    )
    recv = recv.reshape(2, owner_count, 2, tile_rows, width)
    return update(recv, meta, mix, vir_energy.reshape(1, width))


def solution(mesh):
    split = Mesh(mesh.devices.reshape(2, 4, 2, 16, 2), OCC + VIR)
    in_specs = (
        P(OCC, VIR),
        P(None, VIR),
        P(OCC, None),
        P(OCC, VIR),
        P(OCC, None),
        P(OCC),
        P(VIR),
        P(OCC, None, None),
    )
    return jax.shard_map(
        shards, mesh=split, in_specs=in_specs, out_specs=P(OCC, None, VIR), check_vma=False
    )
```

time: 168 us -> 171 us (1.018)
  blocking collectives: 7.56 us -> 95.4 us
  waiting for transfers between devices: 104 us -> 26 us
  Pallas kernels: 0 us -> 24.9 us
  matrix products: 14 us -> 0 us
  between operations: 13.4 us -> 0.14 us
  other arithmetic: 3.32 us -> 0.08 us
  local copies, waits for them, and re-layouts: 6.73 us -> 3.77 us
    all_gather x1 -> x0, waiting for transfers between devices: 76.5 us -> none  [gathered_by_axis(): result = lax.all_gather(result, axes[number], axis=dim, tiled=True)]
    all_gather x1, blocking collectives: 7.56 us -> 52.4 us  [shards(): lax.all_gather(code.reshape(2 * k_width, rows // 2), 'z', axis=0, tiled=T...]
    all_to_all x0 -> x1, blocking collectives: none -> 43 us  [shards(): lax.all_to_all(send.reshape(2 * owner_count, 2, tile_rows, width), ('yhi'...]
    all_to_all x2, waiting for transfers between devices: 27.7 us -> 0.01 us  [the longest x1 0.01 us: shards(): meta = lax.all_to_all(meta, OCC, 0, 0, tiled=True)]
    ppermute x0 -> x2, waiting for transfers between devices: none -> 26 us  [the longest x1 26 us: shards(): mine = lax.ppermute(part, ('ylo', 'yhi'), [(n, 3 - n) for n in range(4)])]
    pallas_call x0 -> x4, Pallas kernels: none -> 24.9 us  [the longest x1 11.2 us: update(): pl.pallas_call(update_kernel, out_shape=jax.ShapeDtypeStruct((owner_count...]
    dot_general x5 -> x0, matrix products: 14 us -> none  [the longest x1 7.2 us: shards(): jnp.dot(gathered_by_axis(masked.reshape(row_count, k_width), VIR, 1), int...]
    ppermute x0 -> x2, starting transfers between devices: none -> 12.2 us  [the longest x1 6.71 us: shards(): other = lax.ppermute(mine, 'core', [(0, 1), (1, 0)])]
  transfers between devices with their start and end apart: 3 -> 4, of which waited for: 2 -> 1; matrix products, arithmetic and copies ran while one was open for 10% -> 0% of each run, Pallas kernels for 0% -> 8%
where the time goes in v1:
time: 171 us; the launch traced here: 170 us
  blocking collectives  95.4 us (56%)
  waiting for transfers between devices  26 us (15%)
  Pallas kernels  24.9 us (15%)
  starting transfers between devices  20.1 us (12%)
  local copies, waits for them, and re-layouts  3.77 us (2%)
    all_gather x1, blocking collectives, shards(): lax.all_gather(code.reshape(2 * k_width, rows // 2), 'z', axis=0, tiled=T...  52.4 us
    all_to_all x1, blocking collectives, shards(): lax.all_to_all(send.reshape(2 * owner_count, 2, tile_rows, width), ('yhi'...  43 us
    ppermute x1, waiting for transfers between devices, shards(): mine = lax.ppermute(part, ('ylo', 'yhi'), [(n, 3 - n) for n in range(4)])  26 us
    pallas_call x1, Pallas kernels, update(): pl.pallas_call(update_kernel, out_shape=jax.ShapeDtypeStruct((owner_count...  11.2 us
    ppermute x1, starting transfers between devices, shards(): other = lax.ppermute(mine, 'core', [(0, 1), (1, 0)])  6.71 us
    pallas_call x1, Pallas kernels, near(): pl.pallas_call(near_kernel, out_shape=(jax.ShapeDtypeStruct((rows, depth)...  6.55 us
    ppermute x1, starting transfers between devices, shards(): mine = lax.ppermute(part, ('ylo', 'yhi'), [(n, 3 - n) for n in range(4)])  5.47 us
    all_to_all x1, starting transfers between devices, shards(): meta = lax.all_to_all(meta, OCC, 0, 0, tiled=True)  4.44 us
  transfers between devices with their start and end apart: 4, of which 1 were waited for; matrix products, arithmetic and copies ran while one was open for 0% of the time, Pallas kernels for 8%

profile of v1, /device:TPU:1, one launch (start us, length us, event | category | flops | bytes accessed | tf_op | source)
XLA Modules:
  0.0 170.4 jit_solution(5479574666757212032)
XLA Ops:
  0.0 0.0 copy-start.5
  0.0 0.0 copy-start.3
  0.0 0.0 copy-start.6
  0.0 0.0 copy-start.4
  0.0 0.0 copy-start.1
  0.0 1.6 constant_dynamic-slice_fusion
  1.6 5.5 %collective-permute-start = (bf16[1536,512]{1,0:T(8,128)(2,1)S(1)}, bf16[1536,512]{1,0:T(8,128)(2,1)}, u32[]{:S(2)}, u32[]{:S(2)}) collective-permute-start(bf16[1536,512]{1,0:T(8,128)(2,1)S(1)} %constant_dynamic-slice_fusion), channel_id=1, source_target_pairs={{0,257},{1,256},{256,1},{257,0},{2,259},{3,258},{258,3},{259,2},{4... | collective-permute-start | bytes 4718600 | tf_op jit(solution)/shard_map/ppermute | solution.py:262
  7.1 0.0 copy-done.5
  7.1 0.1 copy.10.refs_2_
  7.2 0.0 copy-done.3
  7.2 0.1 copy.11.refs_3_
  7.3 0.0 copy-done.6
  7.3 0.1 copy.12.refs_4_
  7.4 0.0 copy-done.4
  7.4 0.0 copy-done.1
  7.4 2.9 %prep.1 = (s16[2,96,512]{2,1,0:T(8,128)(2,1)}, s32[1,32]{1,0:T(1,128)S(1)}, bf16[16,32,128]{2,1,0:T(8,128)(2,1)}) custom-call(s32[1]{0:T(128)} %bitcast.refs_0_, bf16[96,1024]{1,0:T(8,128)(2,1)S(1)} %bitcast.9, s32[32,1]{1,0:T(8,128)S(1)} %copy.10.refs_2_, s32[32,6]{1,0:T(8,128)S(1)} %copy.11.refs_3_, s32[32,1]{1,0:T(8,128)S(1)} %copy.12.refs_4_, ...), custom_call_target="tpu_custom_call" | custom-call | tf_op jit(solution)/shard_map/prep/pallas_call | solution.py:109
  10.3 3.4 %all-to-all-start = ((s16[2,96,512]{2,1,0:T(8,128)(2,1)}), s16[2,96,512]{2,1,0:T(8,128)(2,1)S(1)}, u32[]{:S(2)}, u32[]{:S(2)}) async-start(s16[2,96,512]{2,1,0:T(8,128)(2,1)} %get-tuple-element.11), calls=%async_computation | async-start | bytes 393216 | tf_op jit(solution)/shard_map/all_to_all | solution.py:260
  13.7 0.1 pad_add_fusion.where
  13.8 26.0 %collective-permute-done.mine_ref = bf16[1536,512]{1,0:T(8,128)(2,1)} collective-permute-done((bf16[1536,512]{1,0:T(8,128)(2,1)S(1)}, bf16[1536,512]{1,0:T(8,128)(2,1)}, u32[]{:S(2)}, u32[]{:S(2)}) %collective-permute-start) | collective-permute-done | bytes 1572896 | tf_op jit(solution)/shard_map/ppermute | solution.py:262
  39.8 6.7 %collective-permute-start.1 = (bf16[1536,512]{1,0:T(8,128)(2,1)}, bf16[1536,512]{1,0:T(8,128)(2,1)}, u32[]{:S(2)}, u32[]{:S(2)}) collective-permute-start(bf16[1536,512]{1,0:T(8,128)(2,1)} %collective-permute-done.mine_ref), channel_id=1, source_target_pairs={{0,32},{32,0},{1,33},{33,1},{2,34},{34,2},{3,35},{35,3},{4,36},{36... | collective-permute-start | bytes 4718600 | tf_op jit(solution)/shard_map/ppermute | solution.py:263
  46.6 0.0 all-to-all-done
  46.6 4.4 %all-to-all-start.2 = ((bf16[16,32,128]{2,1,0:T(8,128)(2,1)}), bf16[16,32,128]{2,1,0:T(8,128)(2,1)S(1)}, u32[]{:S(2)}, u32[]{:S(2)}) async-start(bf16[16,32,128]{2,1,0:T(8,128)(2,1)} %get-tuple-element.14), calls=%async_computation.2 | async-start | bytes 262144 | tf_op jit(solution)/shard_map/all_to_all | solution.py:264
  51.0 52.4 %all-gather.1.code_ref = s16[3072,512]{1,0:T(8,128)(2,1)S(1)} all-gather(s16[192,512]{1,0:T(8,128)(2,1)S(1)} %bitcast.11), channel_id=1, replica_groups=mesh['ylo'=2,'x'=4,'core'=2,'z'=16,'yhi'=2] {'z'}, dimensions={0}, use_global_device_ids=true | all-gather | bytes 3342336 | tf_op jit(solution)/shard_map/all_gather | solution.py:265
  103.5 0.0 copy-start
  103.5 1.9 %copy-done = bf16[3072,512]{1,0:T(8,128)(2,1)S(1)} copy-done((bf16[3072,512]{1,0:T(8,128)(2,1)S(1)}, bf16[3072,512]{1,0:T(8,128)(2,1)}, u32[]{:S(2)}) %copy-start) | copy-done | bytes 3145752
  105.3 6.5 %near.1 = (bf16[512,3072]{1,0:T(8,128)(2,1)S(1)}, bf16[2,16,2,32,512]{4,3,2,1,0:T(8,128)(2,1)S(1)}) custom-call(s32[1,32]{1,0:T(1,128)S(1)} %get-tuple-element.10.slot, s32[2]{0:T(128)S(1)} %pad_add_fusion.where, s16[3072,512]{1,0:T(8,128)(2,1)S(1)} %all-gather.1.code_ref, bf16[3072,512]{1,0:T(8,128)(2,1)S(1)} %copy-done), custom_call_target="tpu_custom_call" | custom-call | flops 1610612736 | bytes 11534336 | tf_op jit(solution)/shard_map/near/pallas_call | solution.py:154
  111.9 0.0 collective-permute-done.1.other_ref
  111.9 4.3 %far.1 = bf16[2,16,2,32,512]{4,3,2,1,0:T(8,128)(2,1)S(1)} custom-call(s32[1,32]{1,0:T(1,128)S(1)} %get-tuple-element.10.slot, s32[2]{0:T(128)S(1)} %pad_add_fusion.where, bf16[512,3072]{1,0:T(8,128)(2,1)S(1)} %get-tuple-element.12.a0_ref.a1_ref, bf16[512,3072]{1,0:T(8,128)(2,1)S(1)} %get-tuple-element.12.a0_ref.a1_ref, ...), custom_call_target="tpu_custom_call", output_to_operand_aliasing={{}: (6, {})} | custom-call | flops 1610612736 | bytes 8388608 | tf_op jit(solution)/shard_map/far/pallas_call | solution.py:192
  116.2 0.0 all-to-all-done.2.meta_ref
  116.2 0.0 copy-start.2
  116.2 43.0 %all_to_all.15 = bf16[32,2,32,512]{3,2,1,0:T(8,128)(2,1)} all-to-all(bf16[32,2,32,512]{3,2,1,0:T(8,128)(2,1)S(1)} %bitcast.8), channel_id=1, replica_groups=mesh['ylo'=2,'x'=4,'core'=2,'z'=16,'yhi'=2] {'yhi','ylo','x','core'}, dimensions={0} | all-to-all | bytes 4194304 | tf_op jit(solution)/shard_map/all_to_all | solution.py:268
  159.2 0.0 copy-done.2
  159.2 11.2 %update.1 = bf16[64,32,512]{2,1,0:T(8,128)(2,1)} custom-call(bf16[2,16,2,32,512]{4,3,2,1,0:T(8,128)(2,1)} %bitcast.10, bf16[16,32,128]{2,1,0:T(8,128)(2,1)} %copy-done.2, bf16[1,32,32]{2,1,0:T(8,128)(2,1)} %mix_ref.1, f32[1,512]{1,0:T(1,128)} %bitcast.12), custom_call_target="tpu_custom_call" | custom-call | tf_op jit(solution)/shard_map/update/pallas_call | solution.py:232
  (1 shorter events, 0.0 us)
Async XLA Ops:
  0.0 7.1 %copy-start.5 = (s32[32,1]{0,1:T(1,128)S(1)}, s32[32,1]{0,1:T(1,128)}, u32[]{:S(2)}) copy-start(s32[32,1]{0,1:T(1,128)} %param.12) | copy-start | bytes 388
  0.0 7.2 %copy-start.3 = (s32[32,6]{0,1:T(8,128)S(1)}, s32[32,6]{0,1:T(8,128)}, u32[]{:S(2)}) copy-start(s32[32,6]{0,1:T(8,128)} %param.10) | copy-start | bytes 2308
  0.0 7.3 %copy-start.6 = (s32[32,1]{0,1:T(1,128)S(1)}, s32[32,1]{0,1:T(1,128)}, u32[]{:S(2)}) copy-start(s32[32,1]{0,1:T(1,128)} %param.11) | copy-start | bytes 388
  0.0 7.4 %copy-start.4 = (bf16[1024]{0:T(1024)(128)(2,1)S(1)}, bf16[1024]{0:T(1024)(128)(2,1)}, u32[]{:S(2)}) copy-start(bf16[1024]{0:T(1024)(128)(2,1)} %param.13) | copy-start | bytes 6148
  0.0 7.4 %copy-start.1 = (bf16[1024,96]{0,1:T(8,128)(2,1)S(1)}, bf16[1024,96]{0,1:T(8,128)(2,1)}, u32[]{:S(2)}) copy-start(bf16[1024,96]{0,1:T(8,128)(2,1)} %param.8) | copy-start | bytes 589828
  1.6 38.2 %collective-permute-start = (bf16[1536,512]{1,0:T(8,128)(2,1)S(1)}, bf16[1536,512]{1,0:T(8,128)(2,1)}, u32[]{:S(2)}, u32[]{:S(2)}) collective-permute-start(bf16[1536,512]{1,0:T(8,128)(2,1)S(1)} %constant_dynamic-slice_fusion), channel_id=1, source_target_pairs={{0,257},{1,256},{256,1},{257,0},{2,259},{3,258},{258,3},{259,2},{4... | collective-permute-start | bytes 4718600 | tf_op jit(solution)/shard_map/ppermute | solution.py:262
  10.3 36.3 %all-to-all-start = ((s16[2,96,512]{2,1,0:T(8,128)(2,1)}), s16[2,96,512]{2,1,0:T(8,128)(2,1)S(1)}, u32[]{:S(2)}, u32[]{:S(2)}) async-start(s16[2,96,512]{2,1,0:T(8,128)(2,1)} %get-tuple-element.11), calls=%async_computation | async-start | bytes 393216 | tf_op jit(solution)/shard_map/all_to_all | solution.py:260
  39.8 72.1 %collective-permute-start.1 = (bf16[1536,512]{1,0:T(8,128)(2,1)}, bf16[1536,512]{1,0:T(8,128)(2,1)}, u32[]{:S(2)}, u32[]{:S(2)}) collective-permute-start(bf16[1536,512]{1,0:T(8,128)(2,1)} %collective-permute-done.mine_ref), channel_id=1, source_target_pairs={{0,32},{32,0},{1,33},{33,1},{2,34},{34,2},{3,35},{35,3},{4,36},{36... | collective-permute-start | bytes 4718600 | tf_op jit(solution)/shard_map/ppermute | solution.py:263
  46.6 69.6 %all-to-all-start.2 = ((bf16[16,32,128]{2,1,0:T(8,128)(2,1)}), bf16[16,32,128]{2,1,0:T(8,128)(2,1)S(1)}, u32[]{:S(2)}, u32[]{:S(2)}) async-start(bf16[16,32,128]{2,1,0:T(8,128)(2,1)} %get-tuple-element.14), calls=%async_computation.2 | async-start | bytes 262144 | tf_op jit(solution)/shard_map/all_to_all | solution.py:264
  103.5 1.9 %copy-start = (bf16[3072,512]{1,0:T(8,128)(2,1)S(1)}, bf16[3072,512]{1,0:T(8,128)(2,1)}, u32[]{:S(2)}) copy-start(bf16[3072,512]{1,0:T(8,128)(2,1)} %ints_ref.1) | copy-start | bytes 9437188
  116.2 43.0 %copy-start.2 = (bf16[16,32,128]{2,1,0:T(8,128)(2,1)}, bf16[16,32,128]{2,1,0:T(8,128)(2,1)S(1)}, u32[]{:S(2)}) copy-start(bf16[16,32,128]{2,1,0:T(8,128)(2,1)S(1)} %all-to-all-done.2.meta_ref) | copy-start | bytes 393220

commit v2 on v1

--- a/solution.py
+++ b/solution.py
@@ -39,13 +39,18 @@
 def decode(c):
     c = c.astype(I32)
     m = jnp.abs(c)
-    f = ((m & 127) + 128).astype(F32) * (1.0 / 128.0)
-    v = f * jnp.exp2((m >> 7).astype(F32) - 127.0)
+    v = ((m & 127) | 128).astype(F32) * jnp.exp2((m >> 7).astype(F32) - 127.0)
     v = jnp.where(m == 0, 0.0, v)
     return jnp.where(c < 0, -v, v).astype(BF16)
 
 
-def prep_kernel(tile_k, kfirst, amps_ref, owners_ref, mask_ref, keep_ref, energy_ref, code_ref, slot_ref, meta_ref):
+def prep_kernel(
+    tile_k, where, amps_ref, owners_ref, mask_ref, keep_ref, energy_ref, ints_ref, code_ref, slot_ref, meta_ref, part_ref, sem
+):
+    half_depth = part_ref.shape[0]
+    first = pl.multiple_of(where[1] * half_depth, half_depth)
+    copy = pltpu.make_async_copy(ints_ref.at[pl.ds(first, half_depth)], part_ref, sem)
+    copy.start()
     k_width, rows = amps_ref.shape
     tiles, k_tiles = mask_ref.shape
     owners = meta_ref.shape[0]
@@ -71,7 +76,7 @@
     spread = jnp.where(iota((rows, tiles), 0) // tile_rows == iota((rows, tiles), 1), 1.0, 0.0).astype(BF16)
     per_row = dot(spread, cols)
     per_col = dot(cols, spread, 0, 1)
-    column_tile = (kfirst[0] + iota((k_width, k_tiles), 0)) // tile_k
+    column_tile = (where[2] + iota((k_width, k_tiles), 0)) // tile_k
     select = jnp.where(column_tile == iota((k_width, k_tiles), 1), 1.0, 0.0).astype(BF16)
     present = dot(select, mask_ref[...].astype(F32).astype(BF16), 1, 1).astype(BF16)
     present = dot(present, spread, 1, 1)
@@ -96,9 +101,11 @@
     odd = (start % 2).astype(F32)
     meta = jnp.where(iota(meta.shape, 1) == 4, odd, meta)
     meta_ref[...] = meta.astype(BF16).reshape(meta_ref.shape)
-
-
-def prep(kfirst, tile_k, amps_t, owners, amp_mask, keep_mask, energy, owner_count):
+    copy.wait()
+
+
+def prep(where, amps_t, owners, amp_mask, keep_mask, energy, ints, owner_count):
+    tile_k = ints.shape[0] // amp_mask.shape[1]
     k_width, rows = amps_t.shape
     tile_rows = rows // amp_mask.shape[0]
     vmem = pl.BlockSpec(memory_space=pltpu.VMEM)
@@ -112,19 +119,21 @@
             jax.ShapeDtypeStruct((2, k_width, rows // 2), jnp.int16),
             jax.ShapeDtypeStruct((1, amp_mask.shape[0]), I32),
             jax.ShapeDtypeStruct((owner_count, tile_rows, 128), BF16),
-        ),
-        in_specs=[pl.BlockSpec(memory_space=pltpu.SMEM)] + [vmem] * 5,
-        out_specs=(vmem, vmem, vmem),
-        compiler_params=pltpu.CompilerParams(vmem_limit_bytes=32 << 20),
+            jax.ShapeDtypeStruct((ints.shape[0] // 2, ints.shape[1]), BF16),
+        ),
+        in_specs=[pl.BlockSpec(memory_space=pltpu.SMEM)] + [vmem] * 5 + [pl.BlockSpec(memory_space=pltpu.HBM)],
+        out_specs=(vmem, vmem, vmem, pl.BlockSpec(memory_space=pltpu.HBM)),
+        scratch_shapes=[pltpu.SemaphoreType.DMA],
+        compiler_params=pltpu.CompilerParams(vmem_limit_bytes=62 << 20),
         name="prep",
-    )(kfirst, amps_t, owners, amp_mask, keep_mask, energy)
+    )(where, amps_t, owners, amp_mask, keep_mask, energy, ints)
 
 
 def place_tiles(slot, h, acc, out_ref):
     tile_rows = out_ref.shape[3]
     for n in range(acc.shape[0] // tile_rows):
         at = slot[0, 2 * n + h]
-        out_ref[0, at // 2, at % 2] = acc[n * tile_rows : (n + 1) * tile_rows].astype(BF16)
+        out_ref[0, at // 2, at % 2] = (acc[n * tile_rows : (n + 1) * tile_rows] * (1.0 / 128.0)).astype(BF16)
 
 
 def near_kernel(slot, where, code_ref, ints_ref, amps_ref, out_ref, acc_ref):
@@ -172,7 +181,7 @@
             ),
             scratch_shapes=[pltpu.VMEM((rows, width), F32)],
         ),
-        compiler_params=pltpu.CompilerParams(vmem_limit_bytes=40 << 20),
+        compiler_params=pltpu.CompilerParams(vmem_limit_bytes=58 << 20),
         cost_estimate=pl.CostEstimate(
             flops=2 * rows * depth * width, bytes_accessed=11 << 20, transcendentals=rows * depth
         ),
@@ -180,66 +189,102 @@
     )(slot, where, code, ints)
 
 
-def far_kernel(slot, where, a0_ref, a1_ref, mine_ref, other_ref, _, out_ref):
-    acc = dot(a0_ref[...], mine_ref[...]) + dot(a1_ref[...], other_ref[...])
-    place_tiles(slot, where[0], acc, out_ref)
+def far_kernel(slot, where, amps_ref, mine_ref, other_ref, _, out_ref, acc_ref):
+    step = pl.program_id(0)
+    last = pl.num_programs(0) - 1
+
+    @pl.when(step == 0)
+    def _():
+        acc_ref[...] = dot(amps_ref[...], mine_ref[...])
+
+    @pl.when((step > 0) & (step < 2))
+    def _():
+        acc_ref[...] += dot(amps_ref[...], mine_ref[...])
+
+    @pl.when(step >= 2)
+    def _():
+        acc_ref[...] += dot(amps_ref[...], other_ref[...])
+
+    @pl.when(step == last)
+    def _():
+        place_tiles(slot, where[0], acc_ref, out_ref)
 
 
 def far(slot, where, amps, mine, other, send):
     rows, depth = amps.shape
     width = mine.shape[1]
     owner_count, tile_rows = send.shape[1], send.shape[3]
+    block = depth // 4
     return pl.pallas_call(
         far_kernel,
         out_shape=jax.ShapeDtypeStruct(send.shape, BF16),
         grid_spec=pltpu.PrefetchScalarGridSpec(
             num_scalar_prefetch=2,
-            grid=(1,),
+            grid=(4,),
             in_specs=[
-                pl.BlockSpec((rows, depth // 2), lambda s, slot, where: (0, where[1])),
-                pl.BlockSpec((rows, depth // 2), lambda s, slot, where: (0, 1 - where[1])),
-                pl.BlockSpec(mine.shape, lambda s, *_: (0, 0)),
-                pl.BlockSpec(mine.shape, lambda s, *_: (0, 0)),
+                pl.BlockSpec(
+                    (rows, block),
+                    lambda s, slot, where: (0, jnp.where(s < 2, where[1], 1 - where[1]) * 2 + s % 2),
+                ),
+                pl.BlockSpec((block, width), lambda s, *_: (jnp.minimum(s, 1), 0)),
+                pl.BlockSpec((block, width), lambda s, *_: (jnp.maximum(s - 2, 0), 0)),
                 pl.BlockSpec(memory_space=pl.ANY),
             ],
             out_specs=pl.BlockSpec(
                 (1, owner_count, 2, tile_rows, width), lambda s, slot, where: (1 - where[0], 0, 0, 0, 0)
             ),
-        ),
-        input_output_aliases={6: 0},
-        compiler_params=pltpu.CompilerParams(vmem_limit_bytes=40 << 20),
+            scratch_shapes=[pltpu.VMEM((rows, width), F32)],
+        ),
+        input_output_aliases={5: 0},
+        compiler_params=pltpu.CompilerParams(vmem_limit_bytes=50 << 20),
         cost_estimate=pl.CostEstimate(
             flops=2 * rows * depth * width, bytes_accessed=8 << 20, transcendentals=0
         ),
         name="far",
-    )(slot, where, amps, amps, mine, other, send)
-
-
-def update_kernel(recv_ref, meta_ref, mix_ref, vir_ref, out_ref):
-    meta = meta_ref[0].astype(F32)
-    odd = meta[0:1, 4:5] > 0.5
-    weight = mix_ref[0]
-    energies = vir_ref[...]
-    for k in range(4):
-        energy = meta[:, k : k + 1]
-        tile = jnp.where(odd, recv_ref[(k + 1) % 2, 0, k // 2].astype(F32), recv_ref[k % 2, 0, k // 2].astype(F32))
-        tile = jnp.where(energy != 0.0, tile, 0.0).astype(BF16)
-        out_ref[k] = (dot(weight, tile) / (energies - energy)).astype(BF16)
+    )(slot, where, amps, mine, other, send)
+
+
+def update_kernel(recv_ref, meta_ref, mix_ref, vir_ref, out_ref, weight_ref):
+    tile_rows = mix_ref.shape[1]
+    tall = weight_ref.shape[0]
+    batch = meta_ref.shape[0]
+
+    @pl.when(pl.program_id(0) == 0)
+    def _():
+        copies = jnp.where(iota((tall, tile_rows), 0) % tile_rows == iota((tall, tile_rows), 1), 1.0, 0.0).astype(BF16)
+        wide = dot(dot(copies, mix_ref[0]).astype(BF16), copies, 1, 1)
+        same = iota((tall, tall), 0) // tile_rows == iota((tall, tall), 1) // tile_rows
+        weight_ref[...] = jnp.where(same, wide, 0.0).astype(BF16)
+
+    tiles, energies = [], []
+    for s in range(batch):
+        meta = meta_ref[s].astype(F32)
+        odd = meta[0:1, 4:5] > 0.5
+        for k in range(4):
+            energy = meta[:, k : k + 1]
+            tile = jnp.where(odd, recv_ref[(k + 1) % 2, s, k // 2].astype(F32), recv_ref[k % 2, s, k // 2].astype(F32))
+            tiles.append(jnp.where(energy != 0.0, tile, 0.0).astype(BF16))
+            energies.append(energy)
+    mixed = dot(weight_ref[...], jnp.concatenate(tiles, axis=0))
+    new = mixed / (vir_ref[...] - jnp.concatenate(energies, axis=0))
+    out_ref[...] = new.astype(BF16).reshape(out_ref.shape)
 
 
 def update(recv, meta, mix, vir_energy):
     _, owner_count, two, tile_rows, width = recv.shape
+    batch = 2
     return pl.pallas_call(
         update_kernel,
         out_shape=jax.ShapeDtypeStruct((owner_count * 4, tile_rows, width), BF16),
-        grid=(owner_count,),
+        grid=(owner_count // batch,),
         in_specs=[
-            pl.BlockSpec((2, 1, two, tile_rows, width), lambda s: (0, s, 0, 0, 0)),
-            pl.BlockSpec((1, tile_rows, 128), lambda s: (s, 0, 0)),
+            pl.BlockSpec((2, batch, two, tile_rows, width), lambda s: (0, s, 0, 0, 0)),
+            pl.BlockSpec((batch, tile_rows, 128), lambda s: (s, 0, 0)),
             pl.BlockSpec(mix.shape, lambda s: (0, 0, 0)),
             pl.BlockSpec((1, width), lambda s: (0, 0)),
         ],
-        out_specs=pl.BlockSpec((4, tile_rows, width), lambda s: (s, 0, 0)),
+        out_specs=pl.BlockSpec((batch * 4, tile_rows, width), lambda s: (s, 0, 0)),
+        scratch_shapes=[pltpu.VMEM((batch * 4 * tile_rows, batch * 4 * tile_rows), BF16)],
         name="update",
     )(recv, meta, mix, vir_energy)
 
@@ -252,17 +297,17 @@
     owner_count = lax.axis_size(OCC)
     h = lax.axis_index("yhi").astype(I32)
     c = lax.axis_index("core").astype(I32)
-    kfirst = (lax.axis_index(VIR) * k_width).astype(I32).reshape(1)
-    where = jnp.stack([h, c])
-    code, slot, meta = prep(
-        kfirst, depth // k_tiles, amps.T, owners, amp_mask, keep_mask, occ_energy.reshape(1, rows), owner_count
+    kfirst = (lax.axis_index(VIR) * k_width).astype(I32)
+    where = jnp.stack([h, c, kfirst])
+    code, slot, meta, part = prep(
+        where, amps.T, owners, amp_mask, keep_mask, occ_energy.reshape(1, rows), ints, owner_count
     )
     code = lax.all_to_all(code, "yhi", 0, 0, tiled=True)
-    part = lax.dynamic_slice(ints, (c * (depth // 2), 0), (depth // 2, width))
+    meta = lax.all_to_all(meta, OCC, 0, 0, tiled=True)
     mine = lax.ppermute(part, ("ylo", "yhi"), [(n, 3 - n) for n in range(4)])
+    code = lax.all_gather(code.reshape(2 * k_width, rows // 2), "z", axis=0, tiled=True)
+    mine, code = lax.optimization_barrier((mine, code))
     other = lax.ppermute(mine, "core", [(0, 1), (1, 0)])
-    meta = lax.all_to_all(meta, OCC, 0, 0, tiled=True)
-    code = lax.all_gather(code.reshape(2 * k_width, rows // 2), "z", axis=0, tiled=True)
     decoded, send = near(slot, where, code, ints, owner_count, tile_rows)
     send = far(slot, where, decoded, mine, other, send)
     recv = lax.all_to_all(

time: 171 us -> 194 us (1.13)
  Pallas kernels: 24.9 us -> 72.8 us
  waiting for transfers between devices: 26 us -> 0.36 us
  blocking collectives: 95.4 us -> 89.9 us
  starting transfers between devices: 20.1 us -> 24.5 us
    pallas_call x1, Pallas kernels: 2.86 us -> 50.5 us  [prep(): pl.pallas_call(kernel, out_shape=(jax.ShapeDtypeStruct((2, k_width, rows...]
    ppermute x1, waiting for transfers between devices: 26 us -> 0.01 us  [shards(): mine = lax.ppermute(part, ('ylo', 'yhi'), [(n, 3 - n) for n in range(4)])]
    all_to_all x1, blocking collectives: 43 us -> 34.4 us  [shards(): lax.all_to_all(send.reshape(2 * owner_count, 2, tile_rows, width), ('yhi'...]
    pallas_call x1, Pallas kernels: 11.2 us -> 7.25 us  [update(): pl.pallas_call(update_kernel, out_shape=jax.ShapeDtypeStruct((owner_count...]
    ppermute x1, starting transfers between devices: 6.71 us -> 10.2 us  [shards(): other = lax.ppermute(mine, 'core', [(0, 1), (1, 0)])]
    all_gather x1, blocking collectives: 52.4 us -> 55.5 us  [shards(): lax.all_gather(code.reshape(2 * k_width, rows // 2), 'z', axis=0, tiled=T...]
    pallas_call x1, Pallas kernels: 6.55 us -> 9.28 us  [near(): pl.pallas_call(near_kernel, out_shape=(jax.ShapeDtypeStruct((rows, depth)...]
    unnamed x17 -> x9, local copies, waits for them, and re-layouts: 2.17 us -> 4.04 us
where the time goes in v2:
time: 194 us
  blocking collectives  89.9 us (46%)
  Pallas kernels  72.8 us (38%)
  starting transfers between devices  24.5 us (13%)
  local copies, waits for them, and re-layouts  5.31 us (3%)
    all_gather x1, blocking collectives, shards(): lax.all_gather(code.reshape(2 * k_width, rows // 2), 'z', axis=0, tiled=T...  55.5 us
    pallas_call x1, Pallas kernels, prep(): pl.pallas_call(kernel, out_shape=(jax.ShapeDtypeStruct((2, k_width, rows...  50.5 us
    all_to_all x1, blocking collectives, shards(): lax.all_to_all(send.reshape(2 * owner_count, 2, tile_rows, width), ('yhi'...  34.4 us
    ppermute x1, starting transfers between devices, shards(): other = lax.ppermute(mine, 'core', [(0, 1), (1, 0)])  10.2 us
    pallas_call x1, Pallas kernels, near(): pl.pallas_call(near_kernel, out_shape=(jax.ShapeDtypeStruct((rows, depth)...  9.28 us
    pallas_call x1, Pallas kernels, update(): pl.pallas_call(update_kernel, out_shape=jax.ShapeDtypeStruct((owner_count...  7.25 us
    pallas_call x1, Pallas kernels, far(): pl.pallas_call(far_kernel, out_shape=jax.ShapeDtypeStruct(send.shape, BF1...  5.81 us
    all_to_all x1, starting transfers between devices, shards(): code = lax.all_to_all(code, 'yhi', 0, 0, tiled=True)  5.02 us
  transfers between devices with their start and end apart: 4, of which 1 were waited for; matrix products, arithmetic and copies ran while one was open for 0% of the time, Pallas kernels for 8%

profile of v2, /device:TPU:1, one launch (start us, length us, event | category | flops | bytes accessed | tf_op | source)
XLA Modules:
  0.0 193.6 jit_solution(3881850688907896264)
XLA Ops:
  0.0 1.3 copy.10.refs_2_
  1.3 1.4 copy.11.refs_3_
  2.7 1.3 copy.12.refs_4_
  4.0 1.3 reshape.15.refs_5_
  5.3 0.6 pad_add_fusion.refs_0_.where
  5.9 50.5 %prep.1 = (s16[2,96,512]{2,1,0:T(8,128)(2,1)}, s32[1,32]{1,0:T(1,128)}, bf16[16,32,128]{2,1,0:T(8,128)(2,1)}, bf16[1536,512]{1,0:T(8,128)(2,1)}) custom-call(s32[3]{0:T(128)} %pad_add_fusion.refs_0_.where, bf16[96,1024]{1,0:T(8,128)(2,1)} %bitcast.11, s32[32,1]{1,0:T(8,128)} %copy.10.refs_2_, s32[32,6]{1,0:T(8,128)} %copy.11.refs_3_, s32[32,1]{1,0:T(8,128)} %copy.12.refs_4_, ...), custom_call_target="tpu_custom_call" | custom-call | tf_op jit(solution)/shard_map/prep/pallas_call | solution.py:116
  56.4 5.0 %all-to-all-start = ((s16[2,96,512]{2,1,0:T(8,128)(2,1)}), s16[2,96,512]{2,1,0:T(8,128)(2,1)S(1)}, u32[]{:S(2)}, u32[]{:S(2)}) async-start(s16[2,96,512]{2,1,0:T(8,128)(2,1)} %get-tuple-element.15), calls=%async_computation | async-start | bytes 393216 | tf_op jit(solution)/shard_map/all_to_all | solution.py:305
  61.4 4.8 %collective-permute-start = (bf16[1536,512]{1,0:T(8,128)(2,1)}, bf16[1536,512]{1,0:T(8,128)(2,1)S(1)}, u32[]{:S(2)}, u32[]{:S(2)}) collective-permute-start(bf16[1536,512]{1,0:T(8,128)(2,1)} %get-tuple-element.14), channel_id=1, source_target_pairs={{0,257},{1,256},{256,1},{257,0},{2,259},{3,258},{258,3},{259,2},{4... | collective-permute-start | bytes 4718600 | tf_op jit(solution)/shard_map/ppermute | solution.py:307
  66.3 0.3 all-to-all-done
  66.6 55.5 %all-gather.1.code_ref = s16[3072,512]{1,0:T(8,128)(2,1)} all-gather(s16[192,512]{1,0:T(8,128)(2,1)S(1)} %bitcast.10), channel_id=1, replica_groups=mesh['ylo'=2,'x'=4,'core'=2,'z'=16,'yhi'=2] {'z'}, dimensions={0}, use_global_device_ids=true | all-gather | bytes 3342336 | tf_op jit(solution)/shard_map/all_gather | solution.py:308
  122.1 0.0 collective-permute-done.mine_ref
  122.1 10.2 %collective-permute-start.1 = (bf16[1536,512]{1,0:T(8,128)(2,1)S(1)}, bf16[1536,512]{1,0:T(8,128)(2,1)S(1)}, u32[]{:S(2)}, u32[]{:S(2)}) collective-permute-start(bf16[1536,512]{1,0:T(8,128)(2,1)S(1)} %collective-permute-done.mine_ref), channel_id=1, source_target_pairs={{0,32},{32,0},{1,33},{33,1},{2,34},{34,2},{3,35},{35,3},{4,36},{36... | collective-permute-start | bytes 4718600 | tf_op jit(solution)/shard_map/ppermute | solution.py:310
  132.4 4.4 %all-to-all-start.2 = ((bf16[16,32,128]{2,1,0:T(8,128)(2,1)}), bf16[16,32,128]{2,1,0:T(8,128)(2,1)S(1)}, u32[]{:S(2)}, u32[]{:S(2)}) async-start(bf16[16,32,128]{2,1,0:T(8,128)(2,1)} %get-tuple-element.20), calls=%async_computation.2 | async-start | bytes 262144 | tf_op jit(solution)/shard_map/all_to_all | solution.py:306
  136.8 0.0 copy-start
  136.8 0.0 copy-start.1
  136.8 9.3 %near.1 = (bf16[512,3072]{1,0:T(8,128)(2,1)}, bf16[2,16,2,32,512]{4,3,2,1,0:T(8,128)(2,1)}) custom-call(s32[1,32]{1,0:T(1,128)} %get-tuple-element.13.slot, s32[3]{0:T(128)} %pad_add_fusion.refs_0_.where, s16[3072,512]{1,0:T(8,128)(2,1)} %all-gather.1.code_ref, bf16[3072,512]{1,0:T(8,128)(2,1)} %ints_ref.1), custom_call_target="tpu_custom_call" | custom-call | flops 1610612736 | bytes 11534336 | tf_op jit(solution)/shard_map/near/pallas_call | solution.py:163
  146.1 0.0 collective-permute-done.1.other_ref
  146.1 0.0 copy-done
  146.1 0.0 copy-done.1
  146.1 5.8 %far.1 = bf16[2,16,2,32,512]{4,3,2,1,0:T(8,128)(2,1)} custom-call(s32[1,32]{1,0:T(1,128)S(1)} %copy-done.1, s32[3]{0:T(128)S(1)} %copy-done, bf16[512,3072]{1,0:T(8,128)(2,1)} %get-tuple-element.17.amps_ref, bf16[1536,512]{1,0:T(8,128)(2,1)S(1)} %collective-permute-done.mine_ref, ...), custom_call_target="tpu_custom_call", output_to_operand_aliasing={{}: (5, {})} | custom-call | flops 1610612736 | bytes 8388608 | tf_op jit(solution)/shard_map/far/pallas_call | solution.py:218
  151.9 0.0 all-to-all-done.2.meta_ref
  151.9 0.0 copy-start.2
  151.9 34.4 %all_to_all.15 = bf16[32,2,32,512]{3,2,1,0:T(8,128)(2,1)} all-to-all(bf16[32,2,32,512]{3,2,1,0:T(8,128)(2,1)} %bitcast.9), channel_id=1, replica_groups=mesh['ylo'=2,'x'=4,'core'=2,'z'=16,'yhi'=2] {'yhi','ylo','x','core'}, dimensions={0} | all-to-all | bytes 4194304 | tf_op jit(solution)/shard_map/all_to_all | solution.py:313
  186.3 0.0 copy-done.2
  186.3 7.3 %update.1 = bf16[64,32,512]{2,1,0:T(8,128)(2,1)} custom-call(bf16[2,16,2,32,512]{4,3,2,1,0:T(8,128)(2,1)} %bitcast.8, bf16[16,32,128]{2,1,0:T(8,128)(2,1)} %copy-done.2, bf16[1,32,32]{2,1,0:T(8,128)(2,1)} %mix_ref.1, f32[1,512]{1,0:T(1,128)} %bitcast.12), custom_call_target="tpu_custom_call" | custom-call | tf_op jit(solution)/shard_map/update/pallas_call | solution.py:276
Async XLA Ops:
  56.4 10.2 %all-to-all-start = ((s16[2,96,512]{2,1,0:T(8,128)(2,1)}), s16[2,96,512]{2,1,0:T(8,128)(2,1)S(1)}, u32[]{:S(2)}, u32[]{:S(2)}) async-start(s16[2,96,512]{2,1,0:T(8,128)(2,1)} %get-tuple-element.15), calls=%async_computation | async-start | bytes 393216 | tf_op jit(solution)/shard_map/all_to_all | solution.py:305
  61.4 60.7 %collective-permute-start = (bf16[1536,512]{1,0:T(8,128)(2,1)}, bf16[1536,512]{1,0:T(8,128)(2,1)S(1)}, u32[]{:S(2)}, u32[]{:S(2)}) collective-permute-start(bf16[1536,512]{1,0:T(8,128)(2,1)} %get-tuple-element.14), channel_id=1, source_target_pairs={{0,257},{1,256},{256,1},{257,0},{2,259},{3,258},{258,3},{259,2},{4... | collective-permute-start | bytes 4718600 | tf_op jit(solution)/shard_map/ppermute | solution.py:307
  122.1 24.0 %collective-permute-start.1 = (bf16[1536,512]{1,0:T(8,128)(2,1)S(1)}, bf16[1536,512]{1,0:T(8,128)(2,1)S(1)}, u32[]{:S(2)}, u32[]{:S(2)}) collective-permute-start(bf16[1536,512]{1,0:T(8,128)(2,1)S(1)} %collective-permute-done.mine_ref), channel_id=1, source_target_pairs={{0,32},{32,0},{1,33},{33,1},{2,34},{34,2},{3,35},{35,3},{4,36},{36... | collective-permute-start | bytes 4718600 | tf_op jit(solution)/shard_map/ppermute | solution.py:310
  132.4 19.6 %all-to-all-start.2 = ((bf16[16,32,128]{2,1,0:T(8,128)(2,1)}), bf16[16,32,128]{2,1,0:T(8,128)(2,1)S(1)}, u32[]{:S(2)}, u32[]{:S(2)}) async-start(bf16[16,32,128]{2,1,0:T(8,128)(2,1)} %get-tuple-element.20), calls=%async_computation.2 | async-start | bytes 262144 | tf_op jit(solution)/shard_map/all_to_all | solution.py:306
  136.8 9.3 %copy-start = (s32[3]{0:T(128)S(1)}, s32[3]{0:T(128)}, u32[]{:S(2)}) copy-start(s32[3]{0:T(128)} %pad_add_fusion.refs_0_.where) | copy-start | bytes 40
  136.8 9.3 %copy-start.1 = (s32[1,32]{1,0:T(1,128)S(1)}, s32[1,32]{1,0:T(1,128)}, u32[]{:S(2)}) copy-start(s32[1,32]{1,0:T(1,128)} %get-tuple-element.13.slot) | copy-start | bytes 388
  151.9 34.4 %copy-start.2 = (bf16[16,32,128]{2,1,0:T(8,128)(2,1)}, bf16[16,32,128]{2,1,0:T(8,128)(2,1)S(1)}, u32[]{:S(2)}) copy-start(bf16[16,32,128]{2,1,0:T(8,128)(2,1)S(1)} %all-to-all-done.2.meta_ref) | copy-start | bytes 393220

commit v3 on v1

v3 whole, which is shorter than its diff:
```python
import jax
import jax.numpy as jnp
from jax import lax
from jax.experimental import pallas as pl
from jax.experimental.pallas import tpu as pltpu
from jax.sharding import Mesh
from jax.sharding import PartitionSpec as P

OCC = ("ylo", "x", "core")
VIR = ("z", "yhi")
F32 = jnp.float32
BF16 = jnp.bfloat16
I32 = jnp.int32
NEAR_LIMIT = 32
FAR_LIMIT = 32


def iota(shape, dim):
    return lax.broadcasted_iota(I32, shape, dim)


def dot(a, b, da=1, db=0):
    return lax.dot_general(a, b, (((da,), (db,)), ((), ())), preferred_element_type=F32)


def encode(v):
    a = jnp.abs(v)
    small = a < 2.0**-60
    b = jnp.where(small, a * 2.0**60, a)
    e = jnp.floor(jnp.log2(jnp.maximum(b, 2.0**-70)))
    q = b * jnp.exp2(7.0 - e)
    up = q >= 255.5
    down = q < 127.5
    q = q * jnp.where(up, 0.5, jnp.where(down, 2.0, 1.0))
    e = e + jnp.where(up, 1.0, jnp.where(down, -1.0, 0.0)) - jnp.where(small, 60.0, 0.0)
    code = (e + 127.0) * 128.0 + (jnp.floor(q + 0.5) - 128.0)
    code = jnp.where(a < 2.0**-126, 0.0, code)
    return jnp.where(v < 0.0, -code, code).astype(I32)


def decode(c):
    c = c.astype(I32)
    m = jnp.abs(c)
    v = ((m & 127) | 128).astype(F32) * jnp.exp2((m >> 7).astype(F32) - 127.0)
    v = jnp.where(m == 0, 0.0, v)
    return jnp.where(c < 0, -v, v).astype(BF16)


def prep_kernel(
    tile_k, where, amps_ref, owners_ref, mask_ref, keep_ref, energy_ref, code_ref, slot_ref, meta_ref
):
    k_width, rows = amps_ref.shape
    tiles, k_tiles = mask_ref.shape
    owners = meta_ref.shape[0]
    tile_rows = rows // tiles
    half = rows // 2
    own = owners_ref[...].astype(F32)
    i = iota((tiles, tiles), 0)
    j = iota((tiles, tiles), 1)
    own_row = jnp.sum(jnp.where(i == j, own, 0.0), axis=0, keepdims=True)
    earlier = jnp.where((own_row == own) & (j < i), 1.0, 0.0)
    before = jnp.where(own_row < own, 1.0, 0.0)
    k = jnp.sum(earlier, axis=1, keepdims=True)
    rank = jnp.sum(before, axis=1, keepdims=True) + k
    place = own * 2.0 + jnp.where(k >= 2.0, 1.0, 0.0)
    slot_ref[...] = jnp.sum(
        jnp.where(rank == j.astype(F32), place, 0.0), axis=0, keepdims=True
    ).astype(I32)
    lane = iota((tiles, 128), 1)
    keep = keep_ref[...].astype(F32)
    cols = jnp.where(
        lane == 0, rank, jnp.where(lane == 1, own, jnp.where(lane == 2, k, keep))
    ).astype(BF16)
    spread = jnp.where(iota((rows, tiles), 0) // tile_rows == iota((rows, tiles), 1), 1.0, 0.0).astype(BF16)
    per_row = dot(spread, cols)
    per_col = dot(cols, spread, 0, 1)
    column_tile = (where[2] + iota((k_width, k_tiles), 0)) // tile_k
    select = jnp.where(column_tile == iota((k_width, k_tiles), 1), 1.0, 0.0).astype(BF16)
    present = dot(select, mask_ref[...].astype(F32).astype(BF16), 1, 1).astype(BF16)
    present = dot(present, spread, 1, 1)
    masked = jnp.where(present > 0.5, amps_ref[...].astype(F32), 0.0).astype(BF16)
    r = per_row[:, 0:1].astype(I32)
    target = (r % 2) * half + (r // 2) * tile_rows + iota((rows, 1), 0) % tile_rows
    moved = jnp.where(target == iota((rows, rows), 1), 1.0, 0.0).astype(BF16)
    code = encode(dot(masked, moved))
    code_ref[0] = code[:, :half].astype(jnp.int16)
    code_ref[1] = code[:, half:].astype(jnp.int16)
    energy = jnp.where(per_col[3:4] > 0.5, energy_ref[...].astype(F32), 0.0)
    to = per_col[1:2].astype(I32) * tile_rows + iota((1, rows), 1) % tile_rows
    big = iota((owners * tile_rows, rows), 0)
    sent = jnp.where(big == to, energy, 0.0).astype(BF16)
    position = jnp.where(per_row[:, 2:3].astype(I32) == iota((rows, 128), 1), 1.0, 0.0).astype(BF16)
    meta = dot(sent, position)
    start = jnp.sum(
        jnp.where(own_row < (iota((owners * tile_rows, tiles), 0) // tile_rows).astype(F32), 1.0, 0.0),
        axis=1,
        keepdims=True,
    ).astype(I32)
    odd = (start % 2).astype(F32)
    meta = jnp.where(iota(meta.shape, 1) == 4, odd, meta)
    meta_ref[...] = meta.astype(BF16).reshape(meta_ref.shape)


def prep(where, amps_t, owners, amp_mask, keep_mask, energy, tile_k, owner_count):
    k_width, rows = amps_t.shape
    tile_rows = rows // amp_mask.shape[0]
    vmem = pl.BlockSpec(memory_space=pltpu.VMEM)

    def kernel(*refs):
        prep_kernel(tile_k, *refs)

    return pl.pallas_call(
        kernel,
        out_shape=(
            jax.ShapeDtypeStruct((2, k_width, rows // 2), jnp.int16),
            jax.ShapeDtypeStruct((1, amp_mask.shape[0]), I32),
            jax.ShapeDtypeStruct((owner_count, tile_rows, 128), BF16),
        ),
        in_specs=[pl.BlockSpec(memory_space=pltpu.SMEM)] + [vmem] * 5,
        out_specs=(vmem, vmem, vmem),
        compiler_params=pltpu.CompilerParams(vmem_limit_bytes=24 << 20),
        name="prep",
    )(where, amps_t, owners, amp_mask, keep_mask, energy)


def place_tiles(slot, h, first, acc, out_ref, to):
    tile_rows = out_ref.shape[3]
    for n in range(acc.shape[0] // tile_rows):
        at = slot[0, 2 * (first + n) + h]
        tile = acc[n * tile_rows : (n + 1) * tile_rows] * (1.0 / 128.0)
        out_ref[to, at // 2, at % 2] = tile.astype(BF16)


def near_kernel(slot, where, code_ref, ints_ref, amps_ref, out_ref):
    depth, rows = code_ref.shape
    block = depth // 8
    for k in range(0, depth, block):
        amps_ref[:, k : k + block] = decode(code_ref[k : k + block]).T
    tall = rows // 4
    for r in range(0, rows, tall):
        acc = dot(amps_ref[r : r + tall], ints_ref[...])
        place_tiles(slot, where[0], r // out_ref.shape[3], acc, out_ref, where[0])


def near(slot, where, code, ints, owner_count, tile_rows):
    depth, rows = code.shape
    width = ints.shape[1]
    smem = pl.BlockSpec(memory_space=pltpu.SMEM)
    vmem = pl.BlockSpec(memory_space=pltpu.VMEM)
    return pl.pallas_call(
        near_kernel,
        out_shape=(
            jax.ShapeDtypeStruct((rows, depth), BF16),
            jax.ShapeDtypeStruct((2, owner_count, 2, tile_rows, width), BF16),
        ),
        in_specs=[smem, smem, vmem, vmem],
        out_specs=(vmem, vmem),
        compiler_params=pltpu.CompilerParams(vmem_limit_bytes=NEAR_LIMIT << 20),
        cost_estimate=pl.CostEstimate(
            flops=2 * rows * depth * width, bytes_accessed=11 << 20, transcendentals=rows * depth
        ),
        name="near",
    )(slot, where, code, ints)


def far_kernel(slot, where, amps_ref, mine_ref, other_ref, _, out_ref):
    rows = amps_ref.shape[0]
    half = mine_ref.shape[0]
    c = where[1]
    first = pl.multiple_of(c * half, half)
    second = pl.multiple_of((1 - c) * half, half)
    tall = rows // 4
    for r in range(0, rows, tall):
        acc = dot(amps_ref[r : r + tall, pl.ds(first, half)], mine_ref[...])
        acc += dot(amps_ref[r : r + tall, pl.ds(second, half)], other_ref[...])
        place_tiles(slot, where[0], r // out_ref.shape[3], acc, out_ref, 1 - where[0])


def far(slot, where, amps, mine, other, send):
    rows, depth = amps.shape
    width = mine.shape[1]
    smem = pl.BlockSpec(memory_space=pltpu.SMEM)
    vmem = pl.BlockSpec(memory_space=pltpu.VMEM)
    return pl.pallas_call(
        far_kernel,
        out_shape=jax.ShapeDtypeStruct(send.shape, BF16),
        in_specs=[smem, smem, vmem, vmem, vmem, vmem],
        out_specs=vmem,
        input_output_aliases={5: 0},
        compiler_params=pltpu.CompilerParams(vmem_limit_bytes=FAR_LIMIT << 20),
        cost_estimate=pl.CostEstimate(
            flops=2 * rows * depth * width, bytes_accessed=8 << 20, transcendentals=0
        ),
        name="far",
    )(slot, where, amps, mine, other, send)


def update_kernel(recv_ref, meta_ref, mix_ref, vir_ref, out_ref, weight_ref, new_ref, sems):
    tile_rows = mix_ref.shape[1]
    tall = weight_ref.shape[0]
    batch = tall // (4 * tile_rows)
    copies = jnp.where(iota((tall, tile_rows), 0) % tile_rows == iota((tall, tile_rows), 1), 1.0, 0.0).astype(BF16)
    wide = dot(dot(copies, mix_ref[0]).astype(BF16), copies, 1, 1)
    same = iota((tall, tall), 0) // tile_rows == iota((tall, tall), 1) // tile_rows
    weight_ref[...] = jnp.where(same, wide, 0.0).astype(BF16)
    writes = []
    for step in range(meta_ref.shape[0] // batch):
        tiles, energies = [], []
        for s in range(step * batch, (step + 1) * batch):
            meta = meta_ref[s].astype(F32)
            odd = meta[0:1, 4:5] > 0.5
            for k in range(4):
                energy = meta[:, k : k + 1]
                even_tile = recv_ref[k % 2, s, k // 2].astype(F32)
                odd_tile = recv_ref[(k + 1) % 2, s, k // 2].astype(F32)
                tile = jnp.where(odd, odd_tile, even_tile)
                tiles.append(jnp.where(energy != 0.0, tile, 0.0).astype(BF16))
                energies.append(energy)
        mixed = dot(weight_ref[...], jnp.concatenate(tiles, axis=0))
        new = mixed / (vir_ref[...] - jnp.concatenate(energies, axis=0))
        at = pl.ds(step * batch * 4, batch * 4)
        new_ref[at] = new.astype(BF16).reshape((batch * 4,) + new_ref.shape[1:])
        write = pltpu.make_async_copy(new_ref.at[at], out_ref.at[at], sems.at[step])
        write.start()
        writes.append(write)
    for write in writes:
        write.wait()


def update(recv, meta, mix, vir_energy):
    _, owner_count, two, tile_rows, width = recv.shape
    batch = 2
    vmem = pl.BlockSpec(memory_space=pltpu.VMEM)
    return pl.pallas_call(
        update_kernel,
        out_shape=jax.ShapeDtypeStruct((owner_count * 4, tile_rows, width), BF16),
        in_specs=[vmem] * 4,
        out_specs=pl.BlockSpec(memory_space=pl.ANY),
        scratch_shapes=[
            pltpu.VMEM((batch * 4 * tile_rows, batch * 4 * tile_rows), BF16),
            pltpu.VMEM((owner_count * 4, tile_rows, width), BF16),
            pltpu.SemaphoreType.DMA((owner_count // batch,)),
        ],
        compiler_params=pltpu.CompilerParams(vmem_limit_bytes=24 << 20),
        name="update",
    )(recv, meta, mix, vir_energy)


def shards(amps, ints, amp_mask, keep_mask, owners, occ_energy, vir_energy, mix):
    tiles_dev, k_tiles = amp_mask.shape
    rows, k_width = amps.shape
    tile_rows = rows // tiles_dev
    depth, width = ints.shape
    owner_count = lax.axis_size(OCC)
    h = lax.axis_index("yhi").astype(I32)
    c = lax.axis_index("core").astype(I32)
    kfirst = (lax.axis_index(VIR) * k_width).astype(I32)
    where = jnp.stack([h, c, kfirst])
    code, slot, meta = prep(
        where, amps.T, owners, amp_mask, keep_mask, occ_energy.reshape(1, rows), depth // k_tiles, owner_count
    )
    code, meta, ints_late = lax.optimization_barrier((code, meta, ints))
    code = lax.all_to_all(code, "yhi", 0, 0, tiled=True)
    meta = lax.all_to_all(meta, OCC, 0, 0, tiled=True)
    part = lax.dynamic_slice(ints_late, (c * (depth // 2), 0), (depth // 2, width))
    mine = lax.ppermute(part, ("ylo", "yhi"), [(n, 3 - n) for n in range(4)])
    code, meta = lax.optimization_barrier((code, meta))
    code = lax.all_gather(code.reshape(2 * k_width, rows // 2), "z", axis=0, tiled=True)
    mine, code = lax.optimization_barrier((mine, code))
    other = lax.ppermute(mine, "core", [(0, 1), (1, 0)])
    decoded, send = near(slot, where, code, ints, owner_count, tile_rows)
    send = far(slot, where, decoded, mine, other, send)
    recv = lax.all_to_all(
        send.reshape(2 * owner_count, 2, tile_rows, width), ("yhi",) + OCC, 0, 0, tiled=True
    )
    recv = recv.reshape(2, owner_count, 2, tile_rows, width)
    return update(recv, meta, mix, vir_energy.reshape(1, width))


def solution(mesh):
    split = Mesh(mesh.devices.reshape(2, 4, 2, 16, 2), OCC + VIR)
    in_specs = (
        P(OCC, VIR),
        P(None, VIR),
        P(OCC, None),
        P(OCC, VIR),
        P(OCC, None),
        P(OCC),
        P(VIR),
        P(OCC, None, None),
    )
    return jax.shard_map(
        shards, mesh=split, in_specs=in_specs, out_specs=P(OCC, None, VIR), check_vma=False
    )
```

time: 171 us -> 137 us (0.80)
  waiting for transfers between devices: 26 us -> 6.51 us
  Pallas kernels: 24.9 us -> 13.8 us
  blocking collectives: 95.4 us -> 84.7 us
  starting transfers between devices: 20.1 us -> 24.7 us
  local copies, waits for them, and re-layouts: 3.77 us -> 6.52 us
    ppermute x1, waiting for transfers between devices: 26 us -> 0.01 us  [shards(): mine = lax.ppermute(part, ('ylo', 'yhi'), [(n, 3 - n) for n in range(4)])]
    pallas_call x1, Pallas kernels: 11.2 us -> 2.43 us  [update(): pl.pallas_call(update_kernel, out_shape=jax.ShapeDtypeStruct((owner_count...]
    all_to_all x1, blocking collectives: 43 us -> 36.6 us  [shards(): lax.all_to_all(send.reshape(2 * owner_count, 2, tile_rows, width), ('yhi'...]
    all_to_all x1, starting transfers between devices: 4.44 us -> 9.74 us  [shards(): meta = lax.all_to_all(meta, OCC, 0, 0, tiled=True)]
    all_to_all x1, waiting for transfers between devices: 0.01 us -> 5.18 us  [shards(): code = lax.all_to_all(code, 'yhi', 0, 0, tiled=True)]
    all_gather x1, blocking collectives: 52.4 us -> 48.1 us  [shards(): lax.all_gather(code.reshape(2 * k_width, rows // 2), 'z', axis=0, tiled=T...]
    ppermute x1, starting transfers between devices: 5.47 us -> 2.17 us  [shards(): mine = lax.ppermute(part, ('ylo', 'yhi'), [(n, 3 - n) for n in range(4)])]
    pallas_call x1, Pallas kernels: 6.55 us -> 4.72 us  [near(): pl.pallas_call(near_kernel, out_shape=(jax.ShapeDtypeStruct((rows, depth)...]
  transfers between devices with their start and end apart: 4 -> 4, of which waited for: 1 -> 2; matrix products, arithmetic and copies ran while one was open for 0% -> 2% of each run, Pallas kernels for 8% -> 3%
where the time goes in v3:
time: 137 us; the launch traced here: 136 us
  blocking collectives  84.7 us (62%)
  starting transfers between devices  24.7 us (18%)
  Pallas kernels  13.8 us (10%)
  local copies, waits for them, and re-layouts  6.52 us (5%)
  waiting for transfers between devices  6.51 us (5%)
    all_gather x1, blocking collectives, shards(): lax.all_gather(code.reshape(2 * k_width, rows // 2), 'z', axis=0, tiled=T...  48.1 us
    all_to_all x1, blocking collectives, shards(): lax.all_to_all(send.reshape(2 * owner_count, 2, tile_rows, width), ('yhi'...  36.6 us
    all_to_all x1, starting transfers between devices, shards(): meta = lax.all_to_all(meta, OCC, 0, 0, tiled=True)  9.74 us
    ppermute x1, starting transfers between devices, shards(): other = lax.ppermute(mine, 'core', [(0, 1), (1, 0)])  7.75 us
    all_to_all x1, waiting for transfers between devices, shards(): code = lax.all_to_all(code, 'yhi', 0, 0, tiled=True)  5.18 us
    all_to_all x1, starting transfers between devices, shards(): code = lax.all_to_all(code, 'yhi', 0, 0, tiled=True)  5.01 us
    pallas_call x1, Pallas kernels, near(): pl.pallas_call(near_kernel, out_shape=(jax.ShapeDtypeStruct((rows, depth)...  4.72 us
    pallas_call x1, Pallas kernels, prep(): pl.pallas_call(kernel, out_shape=(jax.ShapeDtypeStruct((2, k_width, rows...  3.4 us
  transfers between devices with their start and end apart: 4, of which 2 were waited for; matrix products, arithmetic and copies ran while one was open for 2% of the time, Pallas kernels for 3%

profile of v3, /device:TPU:1, one launch (start us, length us, event | category | flops | bytes accessed | tf_op | source)
XLA Modules:
  0.0 136.3 jit_solution(11831860004561971500)
XLA Ops:
  0.0 0.7 copy.10.refs_2_
  0.7 0.8 copy.11.refs_3_
  1.5 0.7 copy.12.refs_4_
  2.2 0.7 reshape.15.refs_5_
  2.9 0.1 pad_add_fusion.refs_0_.where
  3.0 0.0 copy-start.1
  3.0 0.9 copy-done.1
  3.9 3.4 %prep.1 = (s16[2,96,512]{2,1,0:T(8,128)(2,1)}, s32[1,32]{1,0:T(1,128)S(1)}, bf16[16,32,128]{2,1,0:T(8,128)(2,1)}) custom-call(s32[3]{0:T(128)S(1)} %pad_add_fusion.refs_0_.where, bf16[96,1024]{1,0:T(8,128)(2,1)S(1)} %bitcast.10, s32[32,1]{1,0:T(8,128)S(1)} %copy.10.refs_2_, s32[32,6]{1,0:T(8,128)S(1)} %copy.11.refs_3_, s32[32,1]{1,0:T(8,128)S(1)} %copy.12.refs_4_, ...), custom_call_target="tpu_custom_call" | custom-call | tf_op jit(solution)/shard_map/prep/pallas_call | solution.py:112
  7.3 5.0 %all-to-all-start = ((s16[2,96,512]{2,1,0:T(8,128)(2,1)}), s16[2,96,512]{2,1,0:T(8,128)(2,1)S(1)}, u32[]{:S(2)}, u32[]{:S(2)}) async-start(s16[2,96,512]{2,1,0:T(8,128)(2,1)} %get-tuple-element.21), calls=%async_computation | async-start | bytes 393216 | tf_op jit(solution)/shard_map/all_to_all | solution.py:263
  12.3 5.2 %all-to-all-done = s16[2,96,512]{2,1,0:T(8,128)(2,1)S(1)} async-done(((s16[2,96,512]{2,1,0:T(8,128)(2,1)}), s16[2,96,512]{2,1,0:T(8,128)(2,1)S(1)}, u32[]{:S(2)}, u32[]{:S(2)}) %all-to-all-start) | async-done | bytes 196640 | tf_op jit(solution)/shard_map/all_to_all | solution.py:263
  17.5 9.7 %all-to-all-start.1 = ((bf16[16,32,128]{2,1,0:T(8,128)(2,1)}), bf16[16,32,128]{2,1,0:T(8,128)(2,1)S(1)}, u32[]{:S(2)}, u32[]{:S(2)}) async-start(bf16[16,32,128]{2,1,0:T(8,128)(2,1)} %get-tuple-element.22), calls=%async_computation.1 | async-start | bytes 262144 | tf_op jit(solution)/shard_map/all_to_all | solution.py:264
  27.3 2.7 %constant_dynamic-slice_fusion = bf16[1536,512]{1,0:T(8,128)(2,1)} fusion(bf16[3072,512]{1,0:T(8,128)(2,1)} %ints_ref.1, s32[]{:T(128)S(6)} %select_n.3), kind=kLoop, calls=%fused_computation.1 | loop fusion | bytes 3145732 | tf_op jit(solution)/shard_map/dynamic_slice | solution.py:265
  29.9 0.0 copy-start
  29.9 2.2 %collective-permute-start = (bf16[1536,512]{1,0:T(8,128)(2,1)}, bf16[1536,512]{1,0:T(8,128)(2,1)}, u32[]{:S(2)}, u32[]{:S(2)}) collective-permute-start(bf16[1536,512]{1,0:T(8,128)(2,1)} %constant_dynamic-slice_fusion), channel_id=1, source_target_pairs={{0,257},{1,256},{256,1},{257,0},{2,259},{3,258},{258,3},{259,2},{4... | collective-permute-start | bytes 4718600 | tf_op jit(solution)/shard_map/ppermute | solution.py:266
  32.1 1.3 all-to-all-done.1.meta_ref
  33.4 48.1 %all-gather.1.code_ref = s16[3072,512]{1,0:T(8,128)(2,1)S(1)} all-gather(s16[192,512]{1,0:T(8,128)(2,1)S(1)} %bitcast.12), channel_id=1, replica_groups=mesh['ylo'=2,'x'=4,'core'=2,'z'=16,'yhi'=2] {'z'}, dimensions={0}, use_global_device_ids=true | all-gather | bytes 3342336 | tf_op jit(solution)/shard_map/all_gather | solution.py:268
  81.6 0.0 collective-permute-done.mine_ref
  81.6 7.8 %collective-permute-start.1 = (bf16[1536,512]{1,0:T(8,128)(2,1)}, bf16[1536,512]{1,0:T(8,128)(2,1)S(1)}, u32[]{:S(2)}, u32[]{:S(2)}) collective-permute-start(bf16[1536,512]{1,0:T(8,128)(2,1)} %collective-permute-done.mine_ref), channel_id=1, source_target_pairs={{0,32},{32,0},{1,33},{33,1},{2,34},{34,2},{3,35},{35,3},{4,36},{36... | collective-permute-start | bytes 4718600 | tf_op jit(solution)/shard_map/ppermute | solution.py:270
  89.3 0.0 copy-done
  89.3 4.7 %near.1 = (bf16[512,3072]{1,0:T(8,128)(2,1)S(1)}, bf16[2,16,2,32,512]{4,3,2,1,0:T(8,128)(2,1)S(1)}) custom-call(s32[1,32]{1,0:T(1,128)S(1)} %get-tuple-element.17.slot, s32[3]{0:T(128)S(1)} %pad_add_fusion.refs_0_.where, s16[3072,512]{1,0:T(8,128)(2,1)S(1)} %all-gather.1.code_ref, bf16[3072,512]{1,0:T(8,128)(2,1)S(1)} %copy-done), custom_call_target="tpu_custom_call" | custom-call | flops 1610612736 | bytes 11534336 | tf_op jit(solution)/shard_map/near/pallas_call | solution.py:150
  94.1 0.0 collective-permute-done.1.other_ref
  94.1 3.2 %far.1 = bf16[2,16,2,32,512]{4,3,2,1,0:T(8,128)(2,1)S(1)} custom-call(s32[1,32]{1,0:T(1,128)S(1)} %get-tuple-element.17.slot, s32[3]{0:T(128)S(1)} %pad_add_fusion.refs_0_.where, bf16[512,3072]{1,0:T(8,128)(2,1)S(1)} %get-tuple-element.25.amps_ref, bf16[1536,512]{1,0:T(8,128)(2,1)} %collective-permute-done.mine_ref, ...), custom_call_target="tpu_custom_call", output_to_operand_aliasing={{}: (5, {})} | custom-call | flops 1610612736 | bytes 8388608 | tf_op jit(solution)/shard_map/far/pallas_call | solution.py:184
  97.3 0.0 copy-start.2
  97.3 0.0 copy-start.3
  97.3 36.6 %all_to_all.15 = bf16[32,2,32,512]{3,2,1,0:T(8,128)(2,1)S(1)} all-to-all(bf16[32,2,32,512]{3,2,1,0:T(8,128)(2,1)S(1)} %bitcast.9), channel_id=1, replica_groups=mesh['ylo'=2,'x'=4,'core'=2,'z'=16,'yhi'=2] {'yhi','ylo','x','core'}, dimensions={0} | all-to-all | bytes 4194304 | tf_op jit(solution)/shard_map/all_to_all | solution.py:273
  133.9 0.0 copy-done.2
  133.9 0.0 copy-done.3
  133.9 2.4 %update.1 = bf16[64,32,512]{2,1,0:T(8,128)(2,1)} custom-call(bf16[2,16,2,32,512]{4,3,2,1,0:T(8,128)(2,1)S(1)} %bitcast.8, bf16[16,32,128]{2,1,0:T(8,128)(2,1)S(1)} %all-to-all-done.1.meta_ref, bf16[1,32,32]{2,1,0:T(8,128)(2,1)S(1)} %copy-done.2, f32[1,512]{1,0:T(1,128)S(1)} %bitcast.11), custom_call_target="tpu_custom_call" | custom-call | tf_op jit(solution)/shard_map/update/pallas_call | solution.py:234
Async XLA Ops:
  3.0 0.9 copy-start.1
  7.3 10.2 %all-to-all-start = ((s16[2,96,512]{2,1,0:T(8,128)(2,1)}), s16[2,96,512]{2,1,0:T(8,128)(2,1)S(1)}, u32[]{:S(2)}, u32[]{:S(2)}) async-start(s16[2,96,512]{2,1,0:T(8,128)(2,1)} %get-tuple-element.21), calls=%async_computation | async-start | bytes 393216 | tf_op jit(solution)/shard_map/all_to_all | solution.py:263
  17.5 15.9 %all-to-all-start.1 = ((bf16[16,32,128]{2,1,0:T(8,128)(2,1)}), bf16[16,32,128]{2,1,0:T(8,128)(2,1)S(1)}, u32[]{:S(2)}, u32[]{:S(2)}) async-start(bf16[16,32,128]{2,1,0:T(8,128)(2,1)} %get-tuple-element.22), calls=%async_computation.1 | async-start | bytes 262144 | tf_op jit(solution)/shard_map/all_to_all | solution.py:264
  29.9 59.4 %copy-start = (bf16[3072,512]{1,0:T(8,128)(2,1)S(1)}, bf16[3072,512]{1,0:T(8,128)(2,1)}, u32[]{:S(2)}) copy-start(bf16[3072,512]{1,0:T(8,128)(2,1)} %ints_ref.1) | copy-start | bytes 9437188
  29.9 51.7 %collective-permute-start = (bf16[1536,512]{1,0:T(8,128)(2,1)}, bf16[1536,512]{1,0:T(8,128)(2,1)}, u32[]{:S(2)}, u32[]{:S(2)}) collective-permute-start(bf16[1536,512]{1,0:T(8,128)(2,1)} %constant_dynamic-slice_fusion), channel_id=1, source_target_pairs={{0,257},{1,256},{256,1},{257,0},{2,259},{3,258},{258,3},{259,2},{4... | collective-permute-start | bytes 4718600 | tf_op jit(solution)/shard_map/ppermute | solution.py:266
  81.6 12.5 %collective-permute-start.1 = (bf16[1536,512]{1,0:T(8,128)(2,1)}, bf16[1536,512]{1,0:T(8,128)(2,1)S(1)}, u32[]{:S(2)}, u32[]{:S(2)}) collective-permute-start(bf16[1536,512]{1,0:T(8,128)(2,1)} %collective-permute-done.mine_ref), channel_id=1, source_target_pairs={{0,32},{32,0},{1,33},{33,1},{2,34},{34,2},{3,35},{35,3},{4,36},{36... | collective-permute-start | bytes 4718600 | tf_op jit(solution)/shard_map/ppermute | solution.py:270
  97.3 36.6 %copy-start.2 = (bf16[1,32,32]{2,1,0:T(8,128)(2,1)S(1)}, bf16[1,32,32]{2,1,0:T(8,128)(2,1)}, u32[]{:S(2)}) copy-start(bf16[1,32,32]{2,1,0:T(8,128)(2,1)} %mix_ref.1) | copy-start | bytes 6148
  97.3 36.6 %copy-start.3 = (f32[512]{0:T(512)S(1)}, f32[512]{0:T(512)}, u32[]{:S(2)}) copy-start(f32[512]{0:T(512)} %param.14) | copy-start | bytes 6148

commit v4 on v3

--- a/solution.py
+++ b/solution.py
@@ -50,14 +50,14 @@
     tile_k, where, amps_ref, owners_ref, mask_ref, keep_ref, energy_ref, code_ref, slot_ref, meta_ref
 ):
     k_width, rows = amps_ref.shape
-    tiles, k_tiles = mask_ref.shape
+    k_tiles, tiles = mask_ref.shape
     owners = meta_ref.shape[0]
     tile_rows = rows // tiles
     half = rows // 2
-    own = owners_ref[...].astype(F32)
+    own_row = owners_ref[...].astype(F32)
     i = iota((tiles, tiles), 0)
     j = iota((tiles, tiles), 1)
-    own_row = jnp.sum(jnp.where(i == j, own, 0.0), axis=0, keepdims=True)
+    own = jnp.sum(jnp.where(i == j, own_row, 0.0), axis=1, keepdims=True)
     earlier = jnp.where((own_row == own) & (j < i), 1.0, 0.0)
     before = jnp.where(own_row < own, 1.0, 0.0)
     k = jnp.sum(earlier, axis=1, keepdims=True)
@@ -67,7 +67,7 @@
         jnp.where(rank == j.astype(F32), place, 0.0), axis=0, keepdims=True
     ).astype(I32)
     lane = iota((tiles, 128), 1)
-    keep = keep_ref[...].astype(F32)
+    keep = jnp.sum(jnp.where(i == j, keep_ref[...].astype(F32), 0.0), axis=1, keepdims=True)
     cols = jnp.where(
         lane == 0, rank, jnp.where(lane == 1, own, jnp.where(lane == 2, k, keep))
     ).astype(BF16)
@@ -76,16 +76,18 @@
     per_col = dot(cols, spread, 0, 1)
     column_tile = (where[2] + iota((k_width, k_tiles), 0)) // tile_k
     select = jnp.where(column_tile == iota((k_width, k_tiles), 1), 1.0, 0.0).astype(BF16)
-    present = dot(select, mask_ref[...].astype(F32).astype(BF16), 1, 1).astype(BF16)
+    present = dot(select, mask_ref[...].astype(F32).astype(BF16)).astype(BF16)
     present = dot(present, spread, 1, 1)
     masked = jnp.where(present > 0.5, amps_ref[...].astype(F32), 0.0).astype(BF16)
     r = per_row[:, 0:1].astype(I32)
-    target = (r % 2) * half + (r // 2) * tile_rows + iota((rows, 1), 0) % tile_rows
+    target = ((r + where[0]) % 2) * half + (r // 2) * tile_rows + iota((rows, 1), 0) % tile_rows
     moved = jnp.where(target == iota((rows, rows), 1), 1.0, 0.0).astype(BF16)
     code = encode(dot(masked, moved))
     code_ref[0] = code[:, :half].astype(jnp.int16)
     code_ref[1] = code[:, half:].astype(jnp.int16)
-    energy = jnp.where(per_col[3:4] > 0.5, energy_ref[...].astype(F32), 0.0)
+    energy = energy_ref[...].astype(F32)
+    energy = jnp.concatenate([energy[n : n + 1] for n in range(energy.shape[0])], axis=1)
+    energy = jnp.where(per_col[3:4] > 0.5, energy, 0.0)
     to = per_col[1:2].astype(I32) * tile_rows + iota((1, rows), 1) % tile_rows
     big = iota((owners * tile_rows, rows), 0)
     sent = jnp.where(big == to, energy, 0.0).astype(BF16)
@@ -103,7 +105,8 @@
 
 def prep(where, amps_t, owners, amp_mask, keep_mask, energy, tile_k, owner_count):
     k_width, rows = amps_t.shape
-    tile_rows = rows // amp_mask.shape[0]
+    tiles = amp_mask.shape[1]
+    tile_rows = rows // tiles
     vmem = pl.BlockSpec(memory_space=pltpu.VMEM)
 
     def kernel(*refs):
@@ -113,7 +116,7 @@
         kernel,
         out_shape=(
             jax.ShapeDtypeStruct((2, k_width, rows // 2), jnp.int16),
-            jax.ShapeDtypeStruct((1, amp_mask.shape[0]), I32),
+            jax.ShapeDtypeStruct((1, tiles), I32),
             jax.ShapeDtypeStruct((owner_count, tile_rows, 128), BF16),
         ),
         in_specs=[pl.BlockSpec(memory_space=pltpu.SMEM)] + [vmem] * 5,
@@ -163,36 +166,51 @@
     )(slot, where, code, ints)
 
 
-def far_kernel(slot, where, amps_ref, mine_ref, other_ref, _, out_ref):
-    rows = amps_ref.shape[0]
-    half = mine_ref.shape[0]
-    c = where[1]
-    first = pl.multiple_of(c * half, half)
-    second = pl.multiple_of((1 - c) * half, half)
-    tall = rows // 4
-    for r in range(0, rows, tall):
-        acc = dot(amps_ref[r : r + tall, pl.ds(first, half)], mine_ref[...])
-        acc += dot(amps_ref[r : r + tall, pl.ds(second, half)], other_ref[...])
-        place_tiles(slot, where[0], r // out_ref.shape[3], acc, out_ref, 1 - where[0])
-
-
-def far(slot, where, amps, mine, other, send):
+def far_kernel(slot, where, amps_ref, ints_hbm, _, out_ref, ints_ref, acc_ref, sems):
+    rows, depth = amps_ref.shape
+    parts = sems.shape[0]
+    block = depth // parts
+    reads = []
+    for n in range(parts):
+        at = pl.ds(n * block, block)
+        reads.append(pltpu.make_async_copy(ints_hbm.at[at], ints_ref.at[at], sems.at[n]))
+        reads[-1].start()
+    tall = rows // 2
+    for n in range(parts):
+        reads[n].wait()
+        at = pl.ds(n * block, block)
+        for r in range(0, rows, tall):
+            part = dot(amps_ref[r : r + tall, at], ints_ref[at])
+            if n > 0:
+                part += acc_ref[r : r + tall]
+            if n < parts - 1:
+                acc_ref[r : r + tall] = part
+            else:
+                place_tiles(slot, where[0], r // out_ref.shape[3], part, out_ref, 1 - where[0])
+
+
+def far(slot, where, amps, ints, send):
     rows, depth = amps.shape
-    width = mine.shape[1]
+    width = ints.shape[1]
     smem = pl.BlockSpec(memory_space=pltpu.SMEM)
     vmem = pl.BlockSpec(memory_space=pltpu.VMEM)
     return pl.pallas_call(
         far_kernel,
         out_shape=jax.ShapeDtypeStruct(send.shape, BF16),
-        in_specs=[smem, smem, vmem, vmem, vmem, vmem],
+        in_specs=[smem, smem, vmem, pl.BlockSpec(memory_space=pl.ANY), vmem],
         out_specs=vmem,
-        input_output_aliases={5: 0},
+        scratch_shapes=[
+            pltpu.VMEM(ints.shape, BF16),
+            pltpu.VMEM((rows, width), F32),
+            pltpu.SemaphoreType.DMA((3,)),
+        ],
+        input_output_aliases={4: 0},
         compiler_params=pltpu.CompilerParams(vmem_limit_bytes=FAR_LIMIT << 20),
         cost_estimate=pl.CostEstimate(
             flops=2 * rows * depth * width, bytes_accessed=8 << 20, transcendentals=0
         ),
         name="far",
-    )(slot, where, amps, mine, other, send)
+    )(slot, where, amps, ints, send)
 
 
 def update_kernel(recv_ref, meta_ref, mix_ref, vir_ref, out_ref, weight_ref, new_ref, sems):
@@ -256,20 +274,23 @@
     c = lax.axis_index("core").astype(I32)
     kfirst = (lax.axis_index(VIR) * k_width).astype(I32)
     where = jnp.stack([h, c, kfirst])
+    ints_far = lax.ppermute(ints, ("ylo", "yhi"), [(n, 3 - n) for n in range(4)])
     code, slot, meta = prep(
-        where, amps.T, owners, amp_mask, keep_mask, occ_energy.reshape(1, rows), depth // k_tiles, owner_count
+        where,
+        amps.T,
+        owners.T,
+        amp_mask.T,
+        keep_mask.T,
+        occ_energy.reshape(8, rows // 8),
+        depth // k_tiles,
+        owner_count,
     )
-    code, meta, ints_late = lax.optimization_barrier((code, meta, ints))
-    code = lax.all_to_all(code, "yhi", 0, 0, tiled=True)
+    partner = lax.ppermute(code[1], "yhi", [(0, 1), (1, 0)])
+    code = jnp.where(h == 0, jnp.concatenate([code[0], partner]), jnp.concatenate([partner, code[0]]))
     meta = lax.all_to_all(meta, OCC, 0, 0, tiled=True)
-    part = lax.dynamic_slice(ints_late, (c * (depth // 2), 0), (depth // 2, width))
-    mine = lax.ppermute(part, ("ylo", "yhi"), [(n, 3 - n) for n in range(4)])
-    code, meta = lax.optimization_barrier((code, meta))
-    code = lax.all_gather(code.reshape(2 * k_width, rows // 2), "z", axis=0, tiled=True)
-    mine, code = lax.optimization_barrier((mine, code))
-    other = lax.ppermute(mine, "core", [(0, 1), (1, 0)])
+    code = lax.all_gather(code, "z", axis=0, tiled=True)
     decoded, send = near(slot, where, code, ints, owner_count, tile_rows)
-    send = far(slot, where, decoded, mine, other, send)
+    send = far(slot, where, decoded, ints_far, send)
     recv = lax.all_to_all(
         send.reshape(2 * owner_count, 2, tile_rows, width), ("yhi",) + OCC, 0, 0, tiled=True
     )

time: 137 us -> 127 us (0.927)
  starting transfers between devices: 24.7 us -> 16.1 us
  blocking collectives: 84.7 us -> 92.2 us
  waiting for transfers between devices: 6.51 us -> 0.01 us
  local copies, waits for them, and re-layouts: 6.52 us -> 3.64 us
    all_to_all x1, blocking collectives: 36.6 us -> 42.8 us  [shards(): lax.all_to_all(send.reshape(2 * owner_count, 2, tile_rows, width), ('yhi'...]
    all_to_all x1 -> x0, waiting for transfers between devices: 5.18 us -> none  [shards(): code = lax.all_to_all(code, 'yhi', 0, 0, tiled=True)]
    all_to_all x1 -> x0, starting transfers between devices: 5.01 us -> none  [shards(): code = lax.all_to_all(code, 'yhi', 0, 0, tiled=True)]
    dynamic_slice x1 -> x0, local copies, waits for them, and re-layouts: 2.65 us -> none  [shards(): lax.dynamic_slice(ints_late, (c * (depth // 2), 0), (depth // 2, width))]
    ppermute x2, starting transfers between devices: 9.93 us -> 7.72 us  [the longest x1 5.46 us: shards(): lax.ppermute(ints, ('ylo', 'yhi'), [(n, 3 - n) for n in range(4)])]
    all_to_all x1, starting transfers between devices: 9.74 us -> 8.36 us  [shards(): meta = lax.all_to_all(meta, OCC, 0, 0, tiled=True)]
    unnamed x11 -> x16, local copies, waits for them, and re-layouts: 3.18 us -> 3.62 us
  transfers between devices with their start and end apart: 4 -> 3, of which waited for: 2 -> 0; matrix products, arithmetic and copies ran while one was open for 2% -> 0% of each run, Pallas kernels for 3% -> 9%
where the time goes in v4:
time: 127 us
  blocking collectives  92.2 us (73%)
  starting transfers between devices  16.1 us (13%)
  Pallas kernels  14.3 us (11%)
  local copies, waits for them, and re-layouts  3.64 us (3%)
    all_gather x1, blocking collectives, shards(): code = lax.all_gather(code, 'z', axis=0, tiled=True)  49.4 us
    all_to_all x1, blocking collectives, shards(): lax.all_to_all(send.reshape(2 * owner_count, 2, tile_rows, width), ('yhi'...  42.8 us
    all_to_all x1, starting transfers between devices, shards(): meta = lax.all_to_all(meta, OCC, 0, 0, tiled=True)  8.36 us
    ppermute x1, starting transfers between devices, shards(): lax.ppermute(ints, ('ylo', 'yhi'), [(n, 3 - n) for n in range(4)])  5.46 us
    pallas_call x1, Pallas kernels, near(): pl.pallas_call(near_kernel, out_shape=(jax.ShapeDtypeStruct((rows, depth)...  4.71 us
    pallas_call x1, Pallas kernels, far(): pl.pallas_call(far_kernel, out_shape=jax.ShapeDtypeStruct(send.shape, BF1...  3.69 us
    unnamed x16, local copies, waits for them, and re-layouts  3.62 us
    pallas_call x1, Pallas kernels, prep(): pl.pallas_call(kernel, out_shape=(jax.ShapeDtypeStruct((2, k_width, rows...  3.51 us
  transfers between devices with their start and end apart: 3, of which 0 were waited for; matrix products, arithmetic and copies ran while one was open for 0% of the time, Pallas kernels for 9%

profile of v4, /device:TPU:1, one launch (start us, length us, event | category | flops | bytes accessed | tf_op | source)
XLA Modules:
  0.0 126.5 jit_solution(6182583426428030118)
XLA Ops:
  0.0 5.5 %collective-permute-start.1 = (bf16[3072,512]{1,0:T(8,128)(2,1)}, bf16[3072,512]{1,0:T(8,128)(2,1)}, u32[]{:S(2)}, u32[]{:S(2)}) collective-permute-start(bf16[3072,512]{1,0:T(8,128)(2,1)} %ints_ref.1), channel_id=1, source_target_pairs={{0,257},{1,256},{256,1},{257,0},{2,259},{3,258},{258,3},{259,2},{4... | collective-permute-start | bytes 9437192 | tf_op jit(solution)/shard_map/ppermute | solution.py:277
  5.5 0.1 pad_add_fusion.refs_0_.where
  5.6 0.0 copy-start.1
  5.6 0.9 copy-done.1
  6.5 0.0 copy-start.3
  6.5 0.7 copy-done.3
  7.2 0.0 copy-start.4
  7.2 0.7 copy-done.4
  7.9 0.0 copy-start.6
  7.9 0.7 copy-done.6
  8.5 0.0 copy-start.7
  8.5 0.7 copy-done.7
  9.2 3.5 %prep.1 = (s16[2,96,512]{2,1,0:T(8,128)(2,1)S(1)}, s32[1,32]{1,0:T(1,128)S(1)}, bf16[16,32,128]{2,1,0:T(8,128)(2,1)}) custom-call(s32[3]{0:T(128)S(1)} %pad_add_fusion.refs_0_.where, bf16[96,1024]{1,0:T(8,128)(2,1)S(1)} %bitcast.17, s32[1,32]{1,0:T(1,128)S(1)} %bitcast.21, s32[6,32]{1,0:T(8,128)S(1)} %bitcast.18, s32[1,32]{1,0:T(1,128)S(1)} %bitcast.22, ...), custom_call_target="tpu_custom_call" | custom-call | tf_op jit(solution)/shard_map/prep/pallas_call | solution.py:115
  12.7 2.3 %collective-permute-start = (s16[96,512]{1,0:T(8,128)(2,1)S(1)}, s16[96,512]{1,0:T(8,128)(2,1)S(1)}, u32[]{:S(2)}, u32[]{:S(2)}) collective-permute-start(s16[96,512]{1,0:T(8,128)(2,1)S(1)} %get-tuple-element.16), channel_id=1, source_target_pairs={{0,1},{1,0},{2,3},{3,2},{4,5},{5,4},{6,7},{7,6},{8,9},{9,8},{10,11... | collective-permute-start | bytes 294920 | tf_op jit(solution)/shard_map/ppermute | solution.py:288
  15.0 8.4 %all-to-all-start.1 = ((bf16[16,32,128]{2,1,0:T(8,128)(2,1)}), bf16[16,32,128]{2,1,0:T(8,128)(2,1)S(1)}, u32[]{:S(2)}, u32[]{:S(2)}) async-start(bf16[16,32,128]{2,1,0:T(8,128)(2,1)} %get-tuple-element.14), calls=%async_computation.1 | async-start | bytes 262144 | tf_op jit(solution)/shard_map/all_to_all | solution.py:290
  23.3 0.0 copy-start
  23.3 0.0 collective-permute-done
  23.4 49.4 %all-gather.1.code_ref = s16[3072,512]{1,0:T(8,128)(2,1)S(1)} all-gather(s16[192,512]{1,0:T(8,128)(2,1)S(1)} %add_select_fusion), channel_id=1, replica_groups=mesh['ylo'=2,'x'=4,'core'=2,'z'=16,'yhi'=2] {'z'}, dimensions={0}, use_global_device_ids=true | all-gather | bytes 3342336 | tf_op jit(solution)/shard_map/all_gather | solution.py:291
  72.8 0.0 copy-done
  72.8 4.7 %near.1 = (bf16[512,3072]{1,0:T(8,128)(2,1)S(1)}, bf16[2,16,2,32,512]{4,3,2,1,0:T(8,128)(2,1)S(1)}) custom-call(s32[1,32]{1,0:T(1,128)S(1)} %get-tuple-element.10.slot, s32[3]{0:T(128)S(1)} %pad_add_fusion.refs_0_.where, s16[3072,512]{1,0:T(8,128)(2,1)S(1)} %all-gather.1.code_ref, bf16[3072,512]{1,0:T(8,128)(2,1)S(1)} %copy-done), custom_call_target="tpu_custom_call" | custom-call | flops 1610612736 | bytes 11534336 | tf_op jit(solution)/shard_map/near/pallas_call | solution.py:153
  77.5 0.0 collective-permute-done.1.ints_hbm
  77.6 3.7 %far.1 = bf16[2,16,2,32,512]{4,3,2,1,0:T(8,128)(2,1)S(1)} custom-call(s32[1,32]{1,0:T(1,128)S(1)} %get-tuple-element.10.slot, s32[3]{0:T(128)S(1)} %pad_add_fusion.refs_0_.where, bf16[512,3072]{1,0:T(8,128)(2,1)S(1)} %get-tuple-element.12.amps_ref, bf16[3072,512]{1,0:T(8,128)(2,1)} %collective-permute-done.1.ints_hbm, ...), custom_call_target="tpu_custom_call", output_to_operand_aliasing={{}: (4, {})} | custom-call | flops 1610612736 | bytes 8388608 | tf_op jit(solution)/shard_map/far/pallas_call | solution.py:197
  81.3 0.0 copy-start.2
  81.3 0.0 copy-start.5
  81.3 0.0 all-to-all-done.1.meta_ref
  81.3 42.8 %all_to_all.10 = bf16[32,2,32,512]{3,2,1,0:T(8,128)(2,1)S(1)} all-to-all(bf16[32,2,32,512]{3,2,1,0:T(8,128)(2,1)S(1)} %bitcast.16), channel_id=1, replica_groups=mesh['ylo'=2,'x'=4,'core'=2,'z'=16,'yhi'=2] {'yhi','ylo','x','core'}, dimensions={0} | all-to-all | bytes 4194304 | tf_op jit(solution)/shard_map/all_to_all | solution.py:294
  124.1 0.0 copy-done.2
  124.1 0.0 copy-done.5
  124.1 2.4 %update.1 = bf16[64,32,512]{2,1,0:T(8,128)(2,1)} custom-call(bf16[2,16,2,32,512]{4,3,2,1,0:T(8,128)(2,1)S(1)} %bitcast.15, bf16[16,32,128]{2,1,0:T(8,128)(2,1)S(1)} %all-to-all-done.1.meta_ref, bf16[1,32,32]{2,1,0:T(8,128)(2,1)S(1)} %copy-done.2, f32[1,512]{1,0:T(1,128)S(1)} %bitcast.20), custom_call_target="tpu_custom_call" | custom-call | tf_op jit(solution)/shard_map/update/pallas_call | solution.py:252
  (2 shorter events, 0.1 us)
Async XLA Ops:
  0.0 77.5 %collective-permute-start.1 = (bf16[3072,512]{1,0:T(8,128)(2,1)}, bf16[3072,512]{1,0:T(8,128)(2,1)}, u32[]{:S(2)}, u32[]{:S(2)}) collective-permute-start(bf16[3072,512]{1,0:T(8,128)(2,1)} %ints_ref.1), channel_id=1, source_target_pairs={{0,257},{1,256},{256,1},{257,0},{2,259},{3,258},{258,3},{259,2},{4... | collective-permute-start | bytes 9437192 | tf_op jit(solution)/shard_map/ppermute | solution.py:277
  5.6 0.9 copy-start.1
  6.5 0.7 copy-start.3
  7.2 0.7 copy-start.4
  7.9 0.7 copy-start.6
  8.5 0.7 copy-start.7
  12.7 10.6 %collective-permute-start = (s16[96,512]{1,0:T(8,128)(2,1)S(1)}, s16[96,512]{1,0:T(8,128)(2,1)S(1)}, u32[]{:S(2)}, u32[]{:S(2)}) collective-permute-start(s16[96,512]{1,0:T(8,128)(2,1)S(1)} %get-tuple-element.16), channel_id=1, source_target_pairs={{0,1},{1,0},{2,3},{3,2},{4,5},{5,4},{6,7},{7,6},{8,9},{9,8},{10,11... | collective-permute-start | bytes 294920 | tf_op jit(solution)/shard_map/ppermute | solution.py:288
  15.0 66.3 %all-to-all-start.1 = ((bf16[16,32,128]{2,1,0:T(8,128)(2,1)}), bf16[16,32,128]{2,1,0:T(8,128)(2,1)S(1)}, u32[]{:S(2)}, u32[]{:S(2)}) async-start(bf16[16,32,128]{2,1,0:T(8,128)(2,1)} %get-tuple-element.14), calls=%async_computation.1 | async-start | bytes 262144 | tf_op jit(solution)/shard_map/all_to_all | solution.py:290
  23.3 49.5 %copy-start = (bf16[3072,512]{1,0:T(8,128)(2,1)S(1)}, bf16[3072,512]{1,0:T(8,128)(2,1)}, u32[]{:S(2)}) copy-start(bf16[3072,512]{1,0:T(8,128)(2,1)} %ints_ref.1) | copy-start | bytes 9437188
  81.3 42.8 %copy-start.2 = (bf16[1,32,32]{2,1,0:T(8,128)(2,1)S(1)}, bf16[1,32,32]{2,1,0:T(8,128)(2,1)}, u32[]{:S(2)}) copy-start(bf16[1,32,32]{2,1,0:T(8,128)(2,1)} %mix_ref.1) | copy-start | bytes 6148
  81.3 42.8 %copy-start.5 = (f32[512]{0:T(512)S(1)}, f32[512]{0:T(512)}, u32[]{:S(2)}) copy-start(f32[512]{0:T(512)} %param.14) | copy-start | bytes 6148

commit v5 on v4

--- a/solution.py
+++ b/solution.py
@@ -11,6 +11,7 @@
 F32 = jnp.float32
 BF16 = jnp.bfloat16
 I32 = jnp.int32
+PREP_LIMIT = 62
 NEAR_LIMIT = 32
 FAR_LIMIT = 32
 
@@ -47,8 +48,17 @@
 
 
 def prep_kernel(
-    tile_k, where, amps_ref, owners_ref, mask_ref, keep_ref, energy_ref, code_ref, slot_ref, meta_ref
+    tile_k, where, amps_hbm, owners_hbm, mask_hbm, keep_hbm, energy_hbm, kept_ref, sent_ref, slot_ref, meta_ref,
+    amps_ref, owners_ref, mask_ref, keep_ref, energy_ref, sems
 ):
+    pairs = (
+        (owners_hbm, owners_ref), (keep_hbm, keep_ref), (mask_hbm, mask_ref), (energy_hbm, energy_ref), (amps_hbm, amps_ref)
+    )
+    reads = [pltpu.make_async_copy(a, b, sems.at[n]) for n, (a, b) in enumerate(pairs)]
+    for read in reads:
+        read.start()
+    for read in reads:
+        read.wait()
     k_width, rows = amps_ref.shape
     k_tiles, tiles = mask_ref.shape
     owners = meta_ref.shape[0]
@@ -83,8 +93,8 @@
     target = ((r + where[0]) % 2) * half + (r // 2) * tile_rows + iota((rows, 1), 0) % tile_rows
     moved = jnp.where(target == iota((rows, rows), 1), 1.0, 0.0).astype(BF16)
     code = encode(dot(masked, moved))
-    code_ref[0] = code[:, :half].astype(jnp.int16)
-    code_ref[1] = code[:, half:].astype(jnp.int16)
+    kept_ref[...] = code[:, :half].astype(jnp.int16)
+    sent_ref[...] = code[:, half:].astype(jnp.int16)
     energy = energy_ref[...].astype(F32)
     energy = jnp.concatenate([energy[n : n + 1] for n in range(energy.shape[0])], axis=1)
     energy = jnp.where(per_col[3:4] > 0.5, energy, 0.0)
@@ -115,13 +125,17 @@
     return pl.pallas_call(
         kernel,
         out_shape=(
-            jax.ShapeDtypeStruct((2, k_width, rows // 2), jnp.int16),
+            jax.ShapeDtypeStruct((k_width, rows // 2), jnp.int16),
+            jax.ShapeDtypeStruct((k_width, rows // 2), jnp.int16),
             jax.ShapeDtypeStruct((1, tiles), I32),
             jax.ShapeDtypeStruct((owner_count, tile_rows, 128), BF16),
         ),
-        in_specs=[pl.BlockSpec(memory_space=pltpu.SMEM)] + [vmem] * 5,
-        out_specs=(vmem, vmem, vmem),
-        compiler_params=pltpu.CompilerParams(vmem_limit_bytes=24 << 20),
+        in_specs=[pl.BlockSpec(memory_space=pltpu.SMEM)] + [pl.BlockSpec(memory_space=pl.ANY)] * 5,
+        out_specs=(vmem, vmem, vmem, vmem),
+        scratch_shapes=[
+            pltpu.VMEM(a.shape, a.dtype) for a in (amps_t, owners, amp_mask, keep_mask, energy)
+        ] + [pltpu.SemaphoreType.DMA((5,))],
+        compiler_params=pltpu.CompilerParams(vmem_limit_bytes=PREP_LIMIT << 20),
         name="prep",
     )(where, amps_t, owners, amp_mask, keep_mask, energy)
 
@@ -275,7 +289,7 @@
     kfirst = (lax.axis_index(VIR) * k_width).astype(I32)
     where = jnp.stack([h, c, kfirst])
     ints_far = lax.ppermute(ints, ("ylo", "yhi"), [(n, 3 - n) for n in range(4)])
-    code, slot, meta = prep(
+    code, partner, slot, meta = prep(
         where,
         amps.T,
         owners.T,
@@ -285,8 +299,8 @@
         depth // k_tiles,
         owner_count,
     )
-    partner = lax.ppermute(code[1], "yhi", [(0, 1), (1, 0)])
-    code = jnp.where(h == 0, jnp.concatenate([code[0], partner]), jnp.concatenate([partner, code[0]]))
+    partner = lax.ppermute(partner, "yhi", [(0, 1), (1, 0)])
+    code = jnp.where(h == 0, jnp.concatenate([code, partner]), jnp.concatenate([partner, code]))
     meta = lax.all_to_all(meta, OCC, 0, 0, tiled=True)
     code = lax.all_gather(code, "z", axis=0, tiled=True)
     decoded, send = near(slot, where, code, ints, owner_count, tile_rows)

time: 127 us -> 126 us (level)
  local copies, waits for them, and re-layouts: 3.64 us -> 0.02 us
  other arithmetic: 0.11 us -> 1.74 us
  Pallas kernels: 14.3 us -> 15.6 us
    unnamed x16 -> x10, local copies, waits for them, and re-layouts: 3.62 us -> 0.02 us
  transfers between devices with their start and end apart: 3 -> 3, of which waited for: 0 -> 0; matrix products, arithmetic and copies ran while one was open for 0% -> 1% of each run, Pallas kernels for 9% -> 10%
where the time goes in v5:
time: 126 us
  blocking collectives  92.1 us (73%)
  starting transfers between devices  16.1 us (13%)
  Pallas kernels  15.6 us (12%)
  other arithmetic  1.74 us (1%)
    all_gather x1, blocking collectives, shards(): code = lax.all_gather(code, 'z', axis=0, tiled=True)  49.9 us
    all_to_all x1, blocking collectives, shards(): lax.all_to_all(send.reshape(2 * owner_count, 2, tile_rows, width), ('yhi'...  42.2 us
    all_to_all x1, starting transfers between devices, shards(): meta = lax.all_to_all(meta, OCC, 0, 0, tiled=True)  8.35 us
    ppermute x1, starting transfers between devices, shards(): lax.ppermute(ints, ('ylo', 'yhi'), [(n, 3 - n) for n in range(4)])  5.46 us
    pallas_call x1, Pallas kernels, prep(): pl.pallas_call(kernel, out_shape=(jax.ShapeDtypeStruct((k_width, rows //...  4.72 us
    pallas_call x1, Pallas kernels, near(): pl.pallas_call(near_kernel, out_shape=(jax.ShapeDtypeStruct((rows, depth)...  4.71 us
    pallas_call x1, Pallas kernels, far(): pl.pallas_call(far_kernel, out_shape=jax.ShapeDtypeStruct(send.shape, BF1...  3.69 us
  transfers between devices with their start and end apart: 3, of which 0 were waited for; matrix products, arithmetic and copies ran while one was open for 1% of the time, Pallas kernels for 10%

profile of v5, /device:TPU:1, one launch (start us, length us, event | category | flops | bytes accessed | tf_op | source)
XLA Modules:
  0.0 125.6 jit_solution(497411543792428679)
XLA Ops:
  0.0 5.5 %collective-permute-start.1 = (bf16[3072,512]{1,0:T(8,128)(2,1)}, bf16[3072,512]{1,0:T(8,128)(2,1)}, u32[]{:S(2)}, u32[]{:S(2)}) collective-permute-start(bf16[3072,512]{1,0:T(8,128)(2,1)} %ints_ref.1), channel_id=1, source_target_pairs={{0,257},{1,256},{256,1},{257,0},{2,259},{3,258},{258,3},{259,2},{4... | collective-permute-start | bytes 9437192 | tf_op jit(solution)/shard_map/ppermute | solution.py:291
  5.5 0.6 pad_add_fusion.refs_0_.where
  6.1 0.0 copy-start.2
  6.1 4.7 %prep.1 = (s16[96,512]{1,0:T(8,128)(2,1)}, s16[96,512]{1,0:T(8,128)(2,1)}, s32[1,32]{1,0:T(1,128)}, bf16[16,32,128]{2,1,0:T(8,128)(2,1)}) custom-call(s32[3]{0:T(128)} %pad_add_fusion.refs_0_.where, bf16[96,1024]{1,0:T(8,128)(2,1)} %bitcast.14, s32[1,32]{1,0:T(1,128)} %bitcast.17, s32[6,32]{1,0:T(8,128)} %bitcast.15, s32[1,32]{1,0:T(1,128)} %bitcast.18, ...), custom_call_target="tpu_custom_call" | custom-call | tf_op jit(solution)/shard_map/prep/pallas_call | solution.py:125
  10.8 0.0 copy-start.4
  10.8 2.3 %collective-permute-start = (s16[96,512]{1,0:T(8,128)(2,1)}, s16[96,512]{1,0:T(8,128)(2,1)S(1)}, u32[]{:S(2)}, u32[]{:S(2)}) collective-permute-start(s16[96,512]{1,0:T(8,128)(2,1)} %get-tuple-element.13), channel_id=1, source_target_pairs={{0,1},{1,0},{2,3},{3,2},{4,5},{5,4},{6,7},{7,6},{8,9},{9,8},{10,11... | collective-permute-start | bytes 294920 | tf_op jit(solution)/shard_map/ppermute | solution.py:302
  13.1 8.4 %all-to-all-start.1 = ((bf16[16,32,128]{2,1,0:T(8,128)(2,1)}), bf16[16,32,128]{2,1,0:T(8,128)(2,1)S(1)}, u32[]{:S(2)}, u32[]{:S(2)}) async-start(bf16[16,32,128]{2,1,0:T(8,128)(2,1)} %get-tuple-element.16), calls=%async_computation.1 | async-start | bytes 262144 | tf_op jit(solution)/shard_map/all_to_all | solution.py:304
  21.5 0.0 copy-start
  21.5 0.0 collective-permute-done
  21.5 1.1 add_select_fusion
  22.6 49.9 %all-gather.1.code_ref = s16[3072,512]{1,0:T(8,128)(2,1)S(1)} all-gather(s16[192,512]{1,0:T(8,128)(2,1)S(1)} %add_select_fusion), channel_id=1, replica_groups=mesh['ylo'=2,'x'=4,'core'=2,'z'=16,'yhi'=2] {'z'}, dimensions={0}, use_global_device_ids=true | all-gather | bytes 3342336 | tf_op jit(solution)/shard_map/all_gather | solution.py:305
  72.5 0.0 copy-done.2
  72.5 0.0 copy-done.4
  72.5 0.0 copy-done
  72.5 4.7 %near.1 = (bf16[512,3072]{1,0:T(8,128)(2,1)S(1)}, bf16[2,16,2,32,512]{4,3,2,1,0:T(8,128)(2,1)S(1)}) custom-call(s32[1,32]{1,0:T(1,128)S(1)} %copy-done.4, s32[3]{0:T(128)S(1)} %copy-done.2, s16[3072,512]{1,0:T(8,128)(2,1)S(1)} %all-gather.1.code_ref, bf16[3072,512]{1,0:T(8,128)(2,1)S(1)} %copy-done), custom_call_target="tpu_custom_call" | custom-call | flops 1610612736 | bytes 11534336 | tf_op jit(solution)/shard_map/near/pallas_call | solution.py:167
  77.2 0.0 collective-permute-done.1.ints_hbm
  77.2 3.7 %far.1 = bf16[2,16,2,32,512]{4,3,2,1,0:T(8,128)(2,1)S(1)} custom-call(s32[1,32]{1,0:T(1,128)S(1)} %copy-done.4, s32[3]{0:T(128)S(1)} %copy-done.2, bf16[512,3072]{1,0:T(8,128)(2,1)S(1)} %get-tuple-element.14.amps_ref, bf16[3072,512]{1,0:T(8,128)(2,1)} %collective-permute-done.1.ints_hbm, ...), custom_call_target="tpu_custom_call", output_to_operand_aliasing={{}: (4, {})} | custom-call | flops 1610612736 | bytes 8388608 | tf_op jit(solution)/shard_map/far/pallas_call | solution.py:211
  80.9 0.0 copy-start.1
  80.9 0.0 copy-start.3
  80.9 0.0 all-to-all-done.1.meta_ref
  81.0 42.2 %all_to_all.10 = bf16[32,2,32,512]{3,2,1,0:T(8,128)(2,1)S(1)} all-to-all(bf16[32,2,32,512]{3,2,1,0:T(8,128)(2,1)S(1)} %bitcast.12), channel_id=1, replica_groups=mesh['ylo'=2,'x'=4,'core'=2,'z'=16,'yhi'=2] {'yhi','ylo','x','core'}, dimensions={0} | all-to-all | bytes 4194304 | tf_op jit(solution)/shard_map/all_to_all | solution.py:308
  123.2 0.0 copy-done.1
  123.2 0.0 copy-done.3
  123.2 2.4 %update.1 = bf16[64,32,512]{2,1,0:T(8,128)(2,1)} custom-call(bf16[2,16,2,32,512]{4,3,2,1,0:T(8,128)(2,1)S(1)} %bitcast.11, bf16[16,32,128]{2,1,0:T(8,128)(2,1)S(1)} %all-to-all-done.1.meta_ref, bf16[1,32,32]{2,1,0:T(8,128)(2,1)S(1)} %copy-done.1, f32[1,512]{1,0:T(1,128)S(1)} %bitcast.13), custom_call_target="tpu_custom_call" | custom-call | tf_op jit(solution)/shard_map/update/pallas_call | solution.py:266
Async XLA Ops:
  0.0 77.2 %collective-permute-start.1 = (bf16[3072,512]{1,0:T(8,128)(2,1)}, bf16[3072,512]{1,0:T(8,128)(2,1)}, u32[]{:S(2)}, u32[]{:S(2)}) collective-permute-start(bf16[3072,512]{1,0:T(8,128)(2,1)} %ints_ref.1), channel_id=1, source_target_pairs={{0,257},{1,256},{256,1},{257,0},{2,259},{3,258},{258,3},{259,2},{4... | collective-permute-start | bytes 9437192 | tf_op jit(solution)/shard_map/ppermute | solution.py:291
  6.1 66.4 %copy-start.2 = (s32[3]{0:T(128)S(1)}, s32[3]{0:T(128)}, u32[]{:S(2)}) copy-start(s32[3]{0:T(128)} %pad_add_fusion.refs_0_.where) | copy-start | bytes 40
  10.8 61.7 %copy-start.4 = (s32[1,32]{1,0:T(1,128)S(1)}, s32[1,32]{1,0:T(1,128)}, u32[]{:S(2)}) copy-start(s32[1,32]{1,0:T(1,128)} %get-tuple-element.11.slot) | copy-start | bytes 388
  10.8 10.6 %collective-permute-start = (s16[96,512]{1,0:T(8,128)(2,1)}, s16[96,512]{1,0:T(8,128)(2,1)S(1)}, u32[]{:S(2)}, u32[]{:S(2)}) collective-permute-start(s16[96,512]{1,0:T(8,128)(2,1)} %get-tuple-element.13), channel_id=1, source_target_pairs={{0,1},{1,0},{2,3},{3,2},{4,5},{5,4},{6,7},{7,6},{8,9},{9,8},{10,11... | collective-permute-start | bytes 294920 | tf_op jit(solution)/shard_map/ppermute | solution.py:302
  13.1 67.8 %all-to-all-start.1 = ((bf16[16,32,128]{2,1,0:T(8,128)(2,1)}), bf16[16,32,128]{2,1,0:T(8,128)(2,1)S(1)}, u32[]{:S(2)}, u32[]{:S(2)}) async-start(bf16[16,32,128]{2,1,0:T(8,128)(2,1)} %get-tuple-element.16), calls=%async_computation.1 | async-start | bytes 262144 | tf_op jit(solution)/shard_map/all_to_all | solution.py:304
  21.5 51.0 %copy-start = (bf16[3072,512]{1,0:T(8,128)(2,1)S(1)}, bf16[3072,512]{1,0:T(8,128)(2,1)}, u32[]{:S(2)}) copy-start(bf16[3072,512]{1,0:T(8,128)(2,1)} %ints_ref.1) | copy-start | bytes 9437188
  80.9 42.3 %copy-start.1 = (bf16[1,32,32]{2,1,0:T(8,128)(2,1)S(1)}, bf16[1,32,32]{2,1,0:T(8,128)(2,1)}, u32[]{:S(2)}) copy-start(bf16[1,32,32]{2,1,0:T(8,128)(2,1)} %mix_ref.1) | copy-start | bytes 6148
  80.9 42.2 %copy-start.3 = (f32[512]{0:T(512)S(1)}, f32[512]{0:T(512)}, u32[]{:S(2)}) copy-start(f32[512]{0:T(512)} %param.14) | copy-start | bytes 6148

commit v6 on v5

v6 whole, which is shorter than its diff:
```python
import jax
import jax.numpy as jnp
from jax import lax
from jax.experimental import pallas as pl
from jax.experimental.pallas import tpu as pltpu
from jax.sharding import Mesh
from jax.sharding import PartitionSpec as P

OCC = ("ylo", "x", "core")
VIR = ("z", "yhi")
F32 = jnp.float32
BF16 = jnp.bfloat16
I32 = jnp.int32
PREP_LIMIT = 62
NEAR_LIMIT = 32
FAR_LIMIT = 32


def iota(shape, dim):
    return lax.broadcasted_iota(I32, shape, dim)


def dot(a, b, da=1, db=0):
    return lax.dot_general(a, b, (((da,), (db,)), ((), ())), preferred_element_type=F32)


def encode(v):
    a = jnp.abs(v)
    small = a < 2.0**-60
    b = jnp.where(small, a * 2.0**60, a)
    e = jnp.floor(jnp.log2(jnp.maximum(b, 2.0**-70)))
    q = b * jnp.exp2(7.0 - e)
    up = q >= 255.5
    down = q < 127.5
    q = q * jnp.where(up, 0.5, jnp.where(down, 2.0, 1.0))
    e = e + jnp.where(up, 1.0, jnp.where(down, -1.0, 0.0)) - jnp.where(small, 60.0, 0.0)
    code = (e + 127.0) * 128.0 + (jnp.floor(q + 0.5) - 128.0)
    code = jnp.where(a < 2.0**-126, 0.0, code)
    return jnp.where(v < 0.0, code - 32768.0, code).astype(I32)


def decode(c):
    c = c.astype(I32)
    m = (c & 127) | 128
    f = jnp.where(c < 0, -m, m)
    return (f.astype(F32) * jnp.exp2(((c >> 7) & 255).astype(F32) - 127.0)).astype(BF16)


def fetch(pairs, sems):
    reads = [pltpu.make_async_copy(a, b, sems.at[n]) for n, (a, b) in enumerate(pairs)]
    for read in reads:
        read.start()
    for read in reads:
        read.wait()


def rows_of_tiles(rows, tiles):
    return jnp.where(iota((rows, tiles), 0) // (rows // tiles) == iota((rows, tiles), 1), 1.0, 0.0).astype(BF16)


def as_column(row):
    n = row.shape[1]
    return jnp.sum(jnp.where(iota((n, n), 0) == iota((n, n), 1), row, 0.0), axis=1, keepdims=True)


def route_kernel(
    owners_hbm, keep_hbm, energy_hbm, rank_ref, slot_ref, meta_ref, owners_ref, keep_ref, energy_ref, sems
):
    fetch(((owners_hbm, owners_ref), (keep_hbm, keep_ref), (energy_hbm, energy_ref)), sems)
    tiles = owners_ref.shape[1]
    owners, tile_rows, _ = meta_ref.shape
    rows = tiles * tile_rows
    own_row = owners_ref[...].astype(F32)
    own = as_column(own_row)
    i = iota((tiles, tiles), 0)
    j = iota((tiles, tiles), 1)
    k = jnp.sum(jnp.where((own_row == own) & (j < i), 1.0, 0.0), axis=1, keepdims=True)
    rank = jnp.sum(jnp.where(own_row < own, 1.0, 0.0), axis=1, keepdims=True) + k
    rank_ref[...] = jnp.sum(jnp.where(i == j, rank, 0.0), axis=0, keepdims=True).astype(I32)
    place = own * 2.0 + jnp.where(k >= 2.0, 1.0, 0.0)
    slot_ref[...] = jnp.sum(
        jnp.where(rank == j.astype(F32), place, 0.0), axis=0, keepdims=True
    ).astype(I32)
    lane = iota((tiles, 128), 1)
    keep = as_column(keep_ref[...].astype(F32))
    cols = jnp.where(lane == 0, own, jnp.where(lane == 1, k, keep)).astype(BF16)
    spread = rows_of_tiles(rows, tiles)
    per_row = dot(spread, cols)
    per_col = dot(cols, spread, 0, 1)
    energy = energy_ref[...].astype(F32)
    energy = jnp.concatenate([energy[n : n + 1] for n in range(energy.shape[0])], axis=1)
    energy = jnp.where(per_col[2:3] > 0.5, energy, 0.0)
    to = per_col[0:1].astype(I32) * tile_rows + iota((1, rows), 1) % tile_rows
    big = iota((owners * tile_rows, rows), 0)
    sent = jnp.where(big == to, energy, 0.0).astype(BF16)
    position = jnp.where(per_row[:, 1:2].astype(I32) == iota((rows, 128), 1), 1.0, 0.0).astype(BF16)
    meta = dot(sent, position)
    start = jnp.sum(
        jnp.where(own_row < (iota((owners * tile_rows, tiles), 0) // tile_rows).astype(F32), 1.0, 0.0),
        axis=1,
        keepdims=True,
    ).astype(I32)
    odd = (start % 2).astype(F32)
    meta = jnp.where(iota(meta.shape, 1) == 4, odd, meta)
    meta_ref[...] = meta.astype(BF16).reshape(meta_ref.shape)


def route(owners, keep_mask, energy, owner_count):
    tiles = owners.shape[1]
    tile_rows = energy.size // tiles
    vmem = pl.BlockSpec(memory_space=pltpu.VMEM)
    return pl.pallas_call(
        route_kernel,
        out_shape=(
            jax.ShapeDtypeStruct((1, tiles), I32),
            jax.ShapeDtypeStruct((1, tiles), I32),
            jax.ShapeDtypeStruct((owner_count, tile_rows, 128), BF16),
        ),
        in_specs=[pl.BlockSpec(memory_space=pl.ANY)] * 3,
        out_specs=(vmem, vmem, vmem),
        scratch_shapes=[pltpu.VMEM(a.shape, a.dtype) for a in (owners, keep_mask, energy)]
        + [pltpu.SemaphoreType.DMA((3,))],
        compiler_params=pltpu.CompilerParams(vmem_limit_bytes=PREP_LIMIT << 20),
        name="route",
    )(owners, keep_mask, energy)


def order_kernel(tile_k, own_hbm, partner_hbm, rank_hbm, mask_hbm, code_ref, amps_ref, rank_ref, mask_ref, sems):
    h = lax.axis_index("yhi").astype(I32)
    z = lax.axis_index("z").astype(I32)
    k_width, rows = own_hbm.shape
    depth = 2 * k_width
    k_tiles, tiles = mask_ref.shape
    tile_rows = rows // tiles
    half = rows // 2
    mine = amps_ref.at[pl.ds(pl.multiple_of(h * k_width, 16), k_width)]
    other = amps_ref.at[pl.ds(pl.multiple_of((1 - h) * k_width, 16), k_width)]
    fetch(((rank_hbm, rank_ref), (mask_hbm, mask_ref), (own_hbm, mine), (partner_hbm, other)), sems)
    lane = iota((tiles, 128), 1)
    cols = jnp.where(lane == 0, as_column(rank_ref[...].astype(F32)), 0.0).astype(BF16)
    spread = rows_of_tiles(rows, tiles)
    r = dot(spread, cols)[:, 0:1].astype(I32)
    column_tile = (z * depth + iota((depth, k_tiles), 0)) // tile_k
    select = jnp.where(column_tile == iota((depth, k_tiles), 1), 1.0, 0.0).astype(BF16)
    present = dot(select, mask_ref[...].astype(F32).astype(BF16)).astype(BF16)
    present = dot(present, spread, 1, 1)
    masked = jnp.where(present > 0.5, amps_ref[...].astype(F32), 0.0).astype(BF16)
    target = ((r + h) % 2) * half + (r // 2) * tile_rows + iota((rows, 1), 0) % tile_rows
    moved = jnp.where(target == iota((rows, half), 1), 1.0, 0.0).astype(BF16)
    code_ref[...] = encode(dot(masked, moved)).astype(jnp.int16)


def order(own, partner, rank, amp_mask, tile_k):
    k_width, rows = own.shape
    any_space = pl.BlockSpec(memory_space=pl.ANY)

    def kernel(*refs):
        order_kernel(tile_k, *refs)

    return pl.pallas_call(
        kernel,
        out_shape=jax.ShapeDtypeStruct((2 * k_width, rows // 2), jnp.int16),
        in_specs=[any_space] * 4,
        out_specs=pl.BlockSpec(memory_space=pltpu.VMEM),
        scratch_shapes=[
            pltpu.VMEM((2 * k_width, rows), BF16),
            pltpu.VMEM(rank.shape, I32),
            pltpu.VMEM(amp_mask.shape, I32),
            pltpu.SemaphoreType.DMA((4,)),
        ],
        compiler_params=pltpu.CompilerParams(vmem_limit_bytes=PREP_LIMIT << 20),
        name="order",
    )(own, partner, rank, amp_mask)


def place_tiles(slot, h, first, acc, out_ref, to):
    tile_rows = out_ref.shape[3]
    for n in range(acc.shape[0] // tile_rows):
        at = slot[0, 2 * (first + n) + h]
        tile = acc[n * tile_rows : (n + 1) * tile_rows] * (1.0 / 128.0)
        out_ref[to, at // 2, at % 2] = tile.astype(BF16)


def near_kernel(slot, code_ref, ints_ref, amps_ref, out_ref):
    depth, rows = code_ref.shape
    block = depth // 8
    for k in range(0, depth, block):
        amps_ref[:, k : k + block] = decode(code_ref[k : k + block]).T
    h = lax.axis_index("yhi").astype(I32)
    tall = rows // 4
    for r in range(0, rows, tall):
        acc = dot(amps_ref[r : r + tall], ints_ref[...])
        place_tiles(slot, h, r // out_ref.shape[3], acc, out_ref, h)


def near(slot, code, ints, owner_count, tile_rows):
    depth, rows = code.shape
    width = ints.shape[1]
    smem = pl.BlockSpec(memory_space=pltpu.SMEM)
    vmem = pl.BlockSpec(memory_space=pltpu.VMEM)
    return pl.pallas_call(
        near_kernel,
        out_shape=(
            jax.ShapeDtypeStruct((rows, depth), BF16),
            jax.ShapeDtypeStruct((2, owner_count, 2, tile_rows, width), BF16),
        ),
        in_specs=[smem, vmem, vmem],
        out_specs=(vmem, vmem),
        compiler_params=pltpu.CompilerParams(vmem_limit_bytes=NEAR_LIMIT << 20),
        cost_estimate=pl.CostEstimate(
            flops=2 * rows * depth * width, bytes_accessed=11 << 20, transcendentals=rows * depth
        ),
        name="near",
    )(slot, code, ints)


def far_kernel(slot, amps_ref, ints_hbm, _, out_ref, ints_ref, acc_ref, sems):
    h = lax.axis_index("yhi").astype(I32)
    rows, depth = amps_ref.shape
    parts = sems.shape[0]
    block = depth // parts
    reads = []
    for n in range(parts):
        at = pl.ds(n * block, block)
        reads.append(pltpu.make_async_copy(ints_hbm.at[at], ints_ref.at[at], sems.at[n]))
        reads[-1].start()
    tall = rows // 2
    for n in range(parts):
        reads[n].wait()
        at = pl.ds(n * block, block)
        for r in range(0, rows, tall):
            part = dot(amps_ref[r : r + tall, at], ints_ref[at])
            if n > 0:
                part += acc_ref[r : r + tall]
            if n < parts - 1:
                acc_ref[r : r + tall] = part
            else:
                place_tiles(slot, h, r // out_ref.shape[3], part, out_ref, 1 - h)


def far(slot, amps, ints, send):
    rows, depth = amps.shape
    width = ints.shape[1]
    smem = pl.BlockSpec(memory_space=pltpu.SMEM)
    vmem = pl.BlockSpec(memory_space=pltpu.VMEM)
    return pl.pallas_call(
        far_kernel,
        out_shape=jax.ShapeDtypeStruct(send.shape, BF16),
        in_specs=[smem, vmem, pl.BlockSpec(memory_space=pl.ANY), vmem],
        out_specs=vmem,
        scratch_shapes=[
            pltpu.VMEM(ints.shape, BF16),
            pltpu.VMEM((rows, width), F32),
            pltpu.SemaphoreType.DMA((3,)),
        ],
        input_output_aliases={3: 0},
        compiler_params=pltpu.CompilerParams(vmem_limit_bytes=FAR_LIMIT << 20),
        cost_estimate=pl.CostEstimate(
            flops=2 * rows * depth * width, bytes_accessed=8 << 20, transcendentals=0
        ),
        name="far",
    )(slot, amps, ints, send)


def update_kernel(recv_ref, meta_ref, mix_ref, vir_ref, out_ref, weight_ref, new_ref, sems):
    tile_rows = mix_ref.shape[1]
    tall = weight_ref.shape[0]
    batch = tall // (4 * tile_rows)
    copies = jnp.where(iota((tall, tile_rows), 0) % tile_rows == iota((tall, tile_rows), 1), 1.0, 0.0).astype(BF16)
    wide = dot(dot(copies, mix_ref[0]).astype(BF16), copies, 1, 1)
    same = iota((tall, tall), 0) // tile_rows == iota((tall, tall), 1) // tile_rows
    weight_ref[...] = jnp.where(same, wide, 0.0).astype(BF16)
    writes = []
    for step in range(meta_ref.shape[0] // batch):
        tiles, energies = [], []
        for s in range(step * batch, (step + 1) * batch):
            meta = meta_ref[s].astype(F32)
            odd = meta[0:1, 4:5] > 0.5
            for k in range(4):
                energy = meta[:, k : k + 1]
                even_tile = recv_ref[k % 2, s, k // 2].astype(F32)
                odd_tile = recv_ref[(k + 1) % 2, s, k // 2].astype(F32)
                tile = jnp.where(odd, odd_tile, even_tile)
                tiles.append(jnp.where(energy != 0.0, tile, 0.0).astype(BF16))
                energies.append(energy)
        mixed = dot(weight_ref[...], jnp.concatenate(tiles, axis=0))
        new = mixed / (vir_ref[...] - jnp.concatenate(energies, axis=0))
        at = pl.ds(step * batch * 4, batch * 4)
        new_ref[at] = new.astype(BF16).reshape((batch * 4,) + new_ref.shape[1:])
        write = pltpu.make_async_copy(new_ref.at[at], out_ref.at[at], sems.at[step])
        write.start()
        writes.append(write)
    for write in writes:
        write.wait()


def update(recv, meta, mix, vir_energy):
    _, owner_count, two, tile_rows, width = recv.shape
    batch = 2
    vmem = pl.BlockSpec(memory_space=pltpu.VMEM)
    return pl.pallas_call(
        update_kernel,
        out_shape=jax.ShapeDtypeStruct((owner_count * 4, tile_rows, width), BF16),
        in_specs=[vmem] * 4,
        out_specs=pl.BlockSpec(memory_space=pl.ANY),
        scratch_shapes=[
            pltpu.VMEM((batch * 4 * tile_rows, batch * 4 * tile_rows), BF16),
            pltpu.VMEM((owner_count * 4, tile_rows, width), BF16),
            pltpu.SemaphoreType.DMA((owner_count // batch,)),
        ],
        compiler_params=pltpu.CompilerParams(vmem_limit_bytes=24 << 20),
        name="update",
    )(recv, meta, mix, vir_energy)


def shards(amps, ints, amp_mask, keep_mask, owners, occ_energy, vir_energy, mix):
    tiles_dev, k_tiles = amp_mask.shape
    rows, k_width = amps.shape
    tile_rows = rows // tiles_dev
    depth, width = ints.shape
    owner_count = lax.axis_size(OCC)
    ints_far = lax.ppermute(ints, ("ylo", "yhi"), [(n, 3 - n) for n in range(4)])
    partner = lax.ppermute(amps, "yhi", [(0, 1), (1, 0)])
    rank, slot, meta = route(owners.T, keep_mask.T, occ_energy.reshape(8, rows // 8), owner_count)
    meta = lax.all_to_all(meta, OCC, 0, 0, tiled=True)
    code = order(amps.T, partner.T, rank, amp_mask.T, depth // k_tiles)
    code = lax.all_gather(code, "z", axis=0, tiled=True)
    decoded, send = near(slot, code, ints, owner_count, tile_rows)
    send = far(slot, decoded, ints_far, send)
    recv = lax.all_to_all(
        send.reshape(2 * owner_count, 2, tile_rows, width), ("yhi",) + OCC, 0, 0, tiled=True
    )
    recv = recv.reshape(2, owner_count, 2, tile_rows, width)
    return update(recv, meta, mix, vir_energy.reshape(1, width))


def solution(mesh):
    split = Mesh(mesh.devices.reshape(2, 4, 2, 16, 2), OCC + VIR)
    in_specs = (
        P(OCC, VIR),
        P(None, VIR),
        P(OCC, None),
        P(OCC, VIR),
        P(OCC, None),
        P(OCC),
        P(VIR),
        P(OCC, None, None),
    )
    return jax.shard_map(
        shards, mesh=split, in_specs=in_specs, out_specs=P(OCC, None, VIR), check_vma=False
    )
```

time: 126 us -> 126 us (level)
  other arithmetic: 1.74 us -> 0 us
    pallas_call x1 -> x2, Pallas kernels: 4.72 us -> 5.73 us  [the longest x1 3.45 us: order(): pl.pallas_call(kernel, out_shape=jax.ShapeDtypeStruct((2 * k_width, rows...]
  transfers between devices with their start and end apart: 3 -> 3, of which waited for: 0 -> 0; matrix products, arithmetic and copies ran while one was open for 1% -> 0% of each run, Pallas kernels for 10% -> 11%
where the time goes in v6:
time: 126 us; the launch traced here: 125 us
  blocking collectives  92.5 us (73%)
  starting transfers between devices  16.1 us (13%)
  Pallas kernels  16.1 us (13%)
    all_gather x1, blocking collectives, shards(): code = lax.all_gather(code, 'z', axis=0, tiled=True)  49.5 us
    all_to_all x1, blocking collectives, shards(): lax.all_to_all(send.reshape(2 * owner_count, 2, tile_rows, width), ('yhi'...  43.1 us
    all_to_all x1, starting transfers between devices, shards(): meta = lax.all_to_all(meta, OCC, 0, 0, tiled=True)  8.36 us
    ppermute x1, starting transfers between devices, shards(): lax.ppermute(ints, ('ylo', 'yhi'), [(n, 3 - n) for n in range(4)])  5.46 us
    pallas_call x1, Pallas kernels, near(): pl.pallas_call(near_kernel, out_shape=(jax.ShapeDtypeStruct((rows, depth)...  4.16 us
    pallas_call x1, Pallas kernels, far(): pl.pallas_call(far_kernel, out_shape=jax.ShapeDtypeStruct(send.shape, BF1...  3.73 us
    pallas_call x1, Pallas kernels, order(): pl.pallas_call(kernel, out_shape=jax.ShapeDtypeStruct((2 * k_width, rows...  3.45 us
  transfers between devices with their start and end apart: 3, of which 0 were waited for; matrix products, arithmetic and copies ran while one was open for 0% of the time, Pallas kernels for 11%

profile of v6, /device:TPU:1, one launch (start us, length us, event | category | flops | bytes accessed | tf_op | source)
XLA Modules:
  0.0 125.5 jit_solution(8971914303355116567)
XLA Ops:
  0.0 5.5 %collective-permute-start.1 = (bf16[3072,512]{1,0:T(8,128)(2,1)}, bf16[3072,512]{1,0:T(8,128)(2,1)}, u32[]{:S(2)}, u32[]{:S(2)}) collective-permute-start(bf16[3072,512]{1,0:T(8,128)(2,1)} %ints_ref.1), channel_id=1, source_target_pairs={{0,257},{1,256},{256,1},{257,0},{2,259},{3,258},{258,3},{259,2},{4... | collective-permute-start | bytes 9437192 | tf_op jit(solution)/shard_map/ppermute | solution.py:322
  5.5 2.3 %collective-permute-start = (bf16[1024,96]{0,1:T(8,128)(2,1)}, bf16[1024,96]{0,1:T(8,128)(2,1)S(1)}, u32[]{:S(2)}, u32[]{:S(2)}) collective-permute-start(bf16[1024,96]{0,1:T(8,128)(2,1)} %param.8), channel_id=1, source_target_pairs={{0,1},{1,0},{2,3},{3,2},{4,5},{5,4},{6,7},{7,6},{8,9},{9,8},{10,11... | collective-permute-start | bytes 589832 | tf_op jit(solution)/shard_map/ppermute | solution.py:323
  7.7 2.3 %route.1 = (s32[1,32]{1,0:T(1,128)}, s32[1,32]{1,0:T(1,128)}, bf16[16,32,128]{2,1,0:T(8,128)(2,1)}) custom-call(s32[1,32]{1,0:T(1,128)} %bitcast.16, s32[1,32]{1,0:T(1,128)} %bitcast.17, bf16[8,128]{1,0:T(8,128)(2,1)} %bitcast.15), custom_call_target="tpu_custom_call" | custom-call | tf_op jit(solution)/shard_map/route/pallas_call | solution.py:112
  10.0 0.0 copy-start.3
  10.0 8.4 %all-to-all-start.1 = ((bf16[16,32,128]{2,1,0:T(8,128)(2,1)}), bf16[16,32,128]{2,1,0:T(8,128)(2,1)S(1)}, u32[]{:S(2)}, u32[]{:S(2)}) async-start(bf16[16,32,128]{2,1,0:T(8,128)(2,1)} %get-tuple-element.14), calls=%async_computation.1 | async-start | bytes 262144 | tf_op jit(solution)/shard_map/all_to_all | solution.py:325
  18.4 0.0 collective-permute-done
  18.4 0.0 copy-start.4
  18.4 0.7 copy-done.4
  19.1 3.4 %order.1 = s16[192,512]{1,0:T(8,128)(2,1)} custom-call(bf16[96,1024]{1,0:T(8,128)(2,1)} %bitcast.12, bf16[96,1024]{1,0:T(8,128)(2,1)} %bitcast.13, s32[1,32]{1,0:T(1,128)} %get-tuple-element.11.refs_2_, s32[6,32]{1,0:T(8,128)} %bitcast.14), custom_call_target="tpu_custom_call" | custom-call | tf_op jit(solution)/shard_map/order/pallas_call | solution.py:160
  22.5 0.0 copy-start
  22.6 49.5 %all-gather.1.code_ref = s16[3072,512]{1,0:T(8,128)(2,1)S(1)} all-gather(s16[192,512]{1,0:T(8,128)(2,1)} %order.1), channel_id=1, replica_groups=mesh['ylo'=2,'x'=4,'core'=2,'z'=16,'yhi'=2] {'z'}, dimensions={0}, use_global_device_ids=true | all-gather | bytes 3342336 | tf_op jit(solution)/shard_map/all_gather | solution.py:327
  72.0 0.0 copy-done.3
  72.0 0.0 copy-done
  72.0 4.2 %near.1 = (bf16[512,3072]{1,0:T(8,128)(2,1)S(1)}, bf16[2,16,2,32,512]{4,3,2,1,0:T(8,128)(2,1)S(1)}) custom-call(s32[1,32]{1,0:T(1,128)S(1)} %copy-done.3, s16[3072,512]{1,0:T(8,128)(2,1)S(1)} %all-gather.1.code_ref, bf16[3072,512]{1,0:T(8,128)(2,1)S(1)} %copy-done), custom_call_target="tpu_custom_call" | custom-call | flops 1610612736 | bytes 11534336 | tf_op jit(solution)/shard_map/near/pallas_call | solution.py:201
  76.2 0.0 collective-permute-done.1.ints_hbm
  76.2 3.7 %far.1 = bf16[2,16,2,32,512]{4,3,2,1,0:T(8,128)(2,1)S(1)} custom-call(s32[1,32]{1,0:T(1,128)S(1)} %copy-done.3, bf16[512,3072]{1,0:T(8,128)(2,1)S(1)} %get-tuple-element.12.amps_ref, bf16[3072,512]{1,0:T(8,128)(2,1)} %collective-permute-done.1.ints_hbm, bf16[2,16,2,32,512]{4,3,2,1,0:T(8,128)(2,1)S(1)} %get-tuple-element.13._), custom_call_target="tpu_custom_call", output_to_operand_aliasing={{}: (3, {})} | custom-call | flops 1610612736 | bytes 8388608 | tf_op jit(solution)/shard_map/far/pallas_call | solution.py:246
  79.9 0.0 copy-start.1
  79.9 0.0 copy-start.2
  80.0 0.0 all-to-all-done.1.meta_ref
  80.0 43.1 %all_to_all.10 = bf16[32,2,32,512]{3,2,1,0:T(8,128)(2,1)S(1)} all-to-all(bf16[32,2,32,512]{3,2,1,0:T(8,128)(2,1)S(1)} %bitcast.10), channel_id=1, replica_groups=mesh['ylo'=2,'x'=4,'core'=2,'z'=16,'yhi'=2] {'yhi','ylo','x','core'}, dimensions={0} | all-to-all | bytes 4194304 | tf_op jit(solution)/shard_map/all_to_all | solution.py:330
  123.0 0.0 copy-done.1
  123.0 0.0 copy-done.2
  123.0 2.4 %update.1 = bf16[64,32,512]{2,1,0:T(8,128)(2,1)} custom-call(bf16[2,16,2,32,512]{4,3,2,1,0:T(8,128)(2,1)S(1)} %bitcast.9, bf16[16,32,128]{2,1,0:T(8,128)(2,1)S(1)} %all-to-all-done.1.meta_ref, bf16[1,32,32]{2,1,0:T(8,128)(2,1)S(1)} %copy-done.1, f32[1,512]{1,0:T(1,128)S(1)} %bitcast.11), custom_call_target="tpu_custom_call" | custom-call | tf_op jit(solution)/shard_map/update/pallas_call | solution.py:301
Async XLA Ops:
  0.0 76.2 %collective-permute-start.1 = (bf16[3072,512]{1,0:T(8,128)(2,1)}, bf16[3072,512]{1,0:T(8,128)(2,1)}, u32[]{:S(2)}, u32[]{:S(2)}) collective-permute-start(bf16[3072,512]{1,0:T(8,128)(2,1)} %ints_ref.1), channel_id=1, source_target_pairs={{0,257},{1,256},{256,1},{257,0},{2,259},{3,258},{258,3},{259,2},{4... | collective-permute-start | bytes 9437192 | tf_op jit(solution)/shard_map/ppermute | solution.py:322
  5.5 12.9 %collective-permute-start = (bf16[1024,96]{0,1:T(8,128)(2,1)}, bf16[1024,96]{0,1:T(8,128)(2,1)S(1)}, u32[]{:S(2)}, u32[]{:S(2)}) collective-permute-start(bf16[1024,96]{0,1:T(8,128)(2,1)} %param.8), channel_id=1, source_target_pairs={{0,1},{1,0},{2,3},{3,2},{4,5},{5,4},{6,7},{7,6},{8,9},{9,8},{10,11... | collective-permute-start | bytes 589832 | tf_op jit(solution)/shard_map/ppermute | solution.py:323
  10.0 62.0 %copy-start.3 = (s32[1,32]{1,0:T(1,128)S(1)}, s32[1,32]{1,0:T(1,128)}, u32[]{:S(2)}) copy-start(s32[1,32]{1,0:T(1,128)} %get-tuple-element.10.slot) | copy-start | bytes 388
  10.0 69.9 %all-to-all-start.1 = ((bf16[16,32,128]{2,1,0:T(8,128)(2,1)}), bf16[16,32,128]{2,1,0:T(8,128)(2,1)S(1)}, u32[]{:S(2)}, u32[]{:S(2)}) async-start(bf16[16,32,128]{2,1,0:T(8,128)(2,1)} %get-tuple-element.14), calls=%async_computation.1 | async-start | bytes 262144 | tf_op jit(solution)/shard_map/all_to_all | solution.py:325
  18.4 0.7 copy-start.4
  22.5 49.5 %copy-start = (bf16[3072,512]{1,0:T(8,128)(2,1)S(1)}, bf16[3072,512]{1,0:T(8,128)(2,1)}, u32[]{:S(2)}) copy-start(bf16[3072,512]{1,0:T(8,128)(2,1)} %ints_ref.1) | copy-start | bytes 9437188
  79.9 43.1 %copy-start.1 = (bf16[1,32,32]{2,1,0:T(8,128)(2,1)S(1)}, bf16[1,32,32]{2,1,0:T(8,128)(2,1)}, u32[]{:S(2)}) copy-start(bf16[1,32,32]{2,1,0:T(8,128)(2,1)} %mix_ref.1) | copy-start | bytes 6148
  79.9 43.1 %copy-start.2 = (f32[512]{0:T(512)S(1)}, f32[512]{0:T(512)}, u32[]{:S(2)}) copy-start(f32[512]{0:T(512)} %param.14) | copy-start | bytes 6148

commit v7 on v6

--- a/solution.py
+++ b/solution.py
@@ -34,15 +34,14 @@
     down = q < 127.5
     q = q * jnp.where(up, 0.5, jnp.where(down, 2.0, 1.0))
     e = e + jnp.where(up, 1.0, jnp.where(down, -1.0, 0.0)) - jnp.where(small, 60.0, 0.0)
-    code = (e + 127.0) * 128.0 + (jnp.floor(q + 0.5) - 128.0)
-    code = jnp.where(a < 2.0**-126, 0.0, code)
-    return jnp.where(v < 0.0, code - 32768.0, code).astype(I32)
+    q = jnp.floor(q + 0.5)
+    code = (e + 127.0) * 128.0 + jnp.where(v < 0.0, 255.0 - q - 32768.0, q - 128.0)
+    return jnp.where(a < 2.0**-126, 0.0, code).astype(I32)
 
 
 def decode(c):
     c = c.astype(I32)
-    m = (c & 127) | 128
-    f = jnp.where(c < 0, -m, m)
+    f = jnp.where(c < 0, -255, 128) + (c & 127)
     return (f.astype(F32) * jnp.exp2(((c >> 7) & 255).astype(F32) - 127.0)).astype(BF16)
 
 
@@ -64,8 +63,14 @@
 
 
 def route_kernel(
-    owners_hbm, keep_hbm, energy_hbm, rank_ref, slot_ref, meta_ref, owners_ref, keep_ref, energy_ref, sems
+    owners_hbm, keep_hbm, energy_hbm, ints_hbm, rank_ref, slot_ref, meta_ref, part_hbm,
+    owners_ref, keep_ref, energy_ref, part_ref, sems
 ):
+    part_rows = part_ref.shape[0]
+    first = pl.multiple_of(lax.axis_index("core").astype(I32) * part_rows, part_rows)
+    cut = pltpu.make_async_copy(ints_hbm.at[pl.ds(first, part_rows)], part_ref, sems.at[3])
+    put = pltpu.make_async_copy(part_ref, part_hbm, sems.at[4])
+    cut.start()
     fetch(((owners_hbm, owners_ref), (keep_hbm, keep_ref), (energy_hbm, energy_ref)), sems)
     tiles = owners_ref.shape[1]
     owners, tile_rows, _ = meta_ref.shape
@@ -87,6 +92,8 @@
     spread = rows_of_tiles(rows, tiles)
     per_row = dot(spread, cols)
     per_col = dot(cols, spread, 0, 1)
+    cut.wait()
+    put.start()
     energy = energy_ref[...].astype(F32)
     energy = jnp.concatenate([energy[n : n + 1] for n in range(energy.shape[0])], axis=1)
     energy = jnp.where(per_col[2:3] > 0.5, energy, 0.0)
@@ -103,9 +110,12 @@
     odd = (start % 2).astype(F32)
     meta = jnp.where(iota(meta.shape, 1) == 4, odd, meta)
     meta_ref[...] = meta.astype(BF16).reshape(meta_ref.shape)
-
-
-def route(owners, keep_mask, energy, owner_count):
+    put.wait()
+
+
+def route(owners, keep_mask, energy, ints, owner_count):
+    part = (ints.shape[0] // 2, ints.shape[1])
+    any_space = pl.BlockSpec(memory_space=pl.ANY)
     tiles = owners.shape[1]
     tile_rows = energy.size // tiles
     vmem = pl.BlockSpec(memory_space=pltpu.VMEM)
@@ -115,14 +125,15 @@
             jax.ShapeDtypeStruct((1, tiles), I32),
             jax.ShapeDtypeStruct((1, tiles), I32),
             jax.ShapeDtypeStruct((owner_count, tile_rows, 128), BF16),
+            jax.ShapeDtypeStruct(part, BF16),
         ),
-        in_specs=[pl.BlockSpec(memory_space=pl.ANY)] * 3,
-        out_specs=(vmem, vmem, vmem),
+        in_specs=[any_space] * 4,
+        out_specs=(vmem, vmem, vmem, any_space),
         scratch_shapes=[pltpu.VMEM(a.shape, a.dtype) for a in (owners, keep_mask, energy)]
-        + [pltpu.SemaphoreType.DMA((3,))],
+        + [pltpu.VMEM(part, BF16), pltpu.SemaphoreType.DMA((5,))],
         compiler_params=pltpu.CompilerParams(vmem_limit_bytes=PREP_LIMIT << 20),
         name="route",
-    )(owners, keep_mask, energy)
+    )(owners, keep_mask, energy, ints)
 
 
 def order_kernel(tile_k, own_hbm, partner_hbm, rank_hbm, mask_hbm, code_ref, amps_ref, rank_ref, mask_ref, sems):
@@ -135,7 +146,12 @@
     half = rows // 2
     mine = amps_ref.at[pl.ds(pl.multiple_of(h * k_width, 16), k_width)]
     other = amps_ref.at[pl.ds(pl.multiple_of((1 - h) * k_width, 16), k_width)]
-    fetch(((rank_hbm, rank_ref), (mask_hbm, mask_ref), (own_hbm, mine), (partner_hbm, other)), sems)
+    large = [
+        pltpu.make_async_copy(own_hbm, mine, sems.at[2]), pltpu.make_async_copy(partner_hbm, other, sems.at[3])
+    ]
+    for read in large:
+        read.start()
+    fetch(((rank_hbm, rank_ref), (mask_hbm, mask_ref)), sems)
     lane = iota((tiles, 128), 1)
     cols = jnp.where(lane == 0, as_column(rank_ref[...].astype(F32)), 0.0).astype(BF16)
     spread = rows_of_tiles(rows, tiles)
@@ -144,9 +160,11 @@
     select = jnp.where(column_tile == iota((depth, k_tiles), 1), 1.0, 0.0).astype(BF16)
     present = dot(select, mask_ref[...].astype(F32).astype(BF16)).astype(BF16)
     present = dot(present, spread, 1, 1)
-    masked = jnp.where(present > 0.5, amps_ref[...].astype(F32), 0.0).astype(BF16)
     target = ((r + h) % 2) * half + (r // 2) * tile_rows + iota((rows, 1), 0) % tile_rows
     moved = jnp.where(target == iota((rows, half), 1), 1.0, 0.0).astype(BF16)
+    for read in large:
+        read.wait()
+    masked = jnp.where(present > 0.5, amps_ref[...].astype(F32), 0.0).astype(BF16)
     code_ref[...] = encode(dot(masked, moved)).astype(jnp.int16)
 
 
@@ -214,52 +232,46 @@
     )(slot, code, ints)
 
 
-def far_kernel(slot, amps_ref, ints_hbm, _, out_ref, ints_ref, acc_ref, sems):
+def far_kernel(slot, amps_ref, mine_hbm, other_ref, _, out_ref, mine_ref, acc_ref, sem):
+    read = pltpu.make_async_copy(mine_hbm, mine_ref, sem)
+    read.start()
     h = lax.axis_index("yhi").astype(I32)
-    rows, depth = amps_ref.shape
-    parts = sems.shape[0]
-    block = depth // parts
-    reads = []
-    for n in range(parts):
-        at = pl.ds(n * block, block)
-        reads.append(pltpu.make_async_copy(ints_hbm.at[at], ints_ref.at[at], sems.at[n]))
-        reads[-1].start()
+    c = lax.axis_index("core").astype(I32)
+    rows = amps_ref.shape[0]
+    half = other_ref.shape[0]
     tall = rows // 2
-    for n in range(parts):
-        reads[n].wait()
-        at = pl.ds(n * block, block)
-        for r in range(0, rows, tall):
-            part = dot(amps_ref[r : r + tall, at], ints_ref[at])
-            if n > 0:
-                part += acc_ref[r : r + tall]
-            if n < parts - 1:
-                acc_ref[r : r + tall] = part
-            else:
-                place_tiles(slot, h, r // out_ref.shape[3], part, out_ref, 1 - h)
-
-
-def far(slot, amps, ints, send):
+    for r in range(0, rows, tall):
+        at = pl.ds(pl.multiple_of((1 - c) * half, half), half)
+        acc_ref[r : r + tall] = dot(amps_ref[r : r + tall, at], other_ref[...])
+    read.wait()
+    for r in range(0, rows, tall):
+        at = pl.ds(pl.multiple_of(c * half, half), half)
+        acc = acc_ref[r : r + tall] + dot(amps_ref[r : r + tall, at], mine_ref[...])
+        place_tiles(slot, h, r // out_ref.shape[3], acc, out_ref, 1 - h)
+
+
+def far(slot, amps, mine, other, send):
     rows, depth = amps.shape
-    width = ints.shape[1]
+    width = mine.shape[1]
     smem = pl.BlockSpec(memory_space=pltpu.SMEM)
     vmem = pl.BlockSpec(memory_space=pltpu.VMEM)
     return pl.pallas_call(
         far_kernel,
         out_shape=jax.ShapeDtypeStruct(send.shape, BF16),
-        in_specs=[smem, vmem, pl.BlockSpec(memory_space=pl.ANY), vmem],
+        in_specs=[smem, vmem, pl.BlockSpec(memory_space=pl.ANY), vmem, vmem],
         out_specs=vmem,
         scratch_shapes=[
-            pltpu.VMEM(ints.shape, BF16),
+            pltpu.VMEM(mine.shape, BF16),
             pltpu.VMEM((rows, width), F32),
-            pltpu.SemaphoreType.DMA((3,)),
+            pltpu.SemaphoreType.DMA,
         ],
-        input_output_aliases={3: 0},
+        input_output_aliases={4: 0},
         compiler_params=pltpu.CompilerParams(vmem_limit_bytes=FAR_LIMIT << 20),
         cost_estimate=pl.CostEstimate(
             flops=2 * rows * depth * width, bytes_accessed=8 << 20, transcendentals=0
         ),
         name="far",
-    )(slot, amps, ints, send)
+    )(slot, amps, mine, other, send)
 
 
 def update_kernel(recv_ref, meta_ref, mix_ref, vir_ref, out_ref, weight_ref, new_ref, sems):
@@ -319,14 +331,19 @@
     tile_rows = rows // tiles_dev
     depth, width = ints.shape
     owner_count = lax.axis_size(OCC)
-    ints_far = lax.ppermute(ints, ("ylo", "yhi"), [(n, 3 - n) for n in range(4)])
     partner = lax.ppermute(amps, "yhi", [(0, 1), (1, 0)])
-    rank, slot, meta = route(owners.T, keep_mask.T, occ_energy.reshape(8, rows // 8), owner_count)
+    rank, slot, meta, part = route(
+        owners.T, keep_mask.T, occ_energy.reshape(8, rows // 8), ints, owner_count
+    )
     meta = lax.all_to_all(meta, OCC, 0, 0, tiled=True)
+    mine = lax.ppermute(part, ("ylo", "yhi"), [(n, 3 - n) for n in range(4)])
     code = order(amps.T, partner.T, rank, amp_mask.T, depth // k_tiles)
+    code, meta = lax.optimization_barrier((code, meta))
     code = lax.all_gather(code, "z", axis=0, tiled=True)
+    mine, code = lax.optimization_barrier((mine, code))
+    other = lax.ppermute(mine, "core", [(0, 1), (1, 0)])
     decoded, send = near(slot, code, ints, owner_count, tile_rows)
-    send = far(slot, decoded, ints_far, send)
+    send = far(slot, decoded, mine, other, send)
     recv = lax.all_to_all(
         send.reshape(2 * owner_count, 2, tile_rows, width), ("yhi",) + OCC, 0, 0, tiled=True
     )

time: 126 us -> 129 us (1.024)
  starting transfers between devices: 16.1 us -> 26.4 us
  blocking collectives: 92.5 us -> 83.9 us
    ppermute x1 -> x2, starting transfers between devices: 5.46 us -> 14.3 us  [the longest x1 8.95 us: shards(): other = lax.ppermute(mine, 'core', [(0, 1), (1, 0)])]
    all_to_all x1, blocking collectives: 43.1 us -> 34.9 us  [shards(): lax.all_to_all(send.reshape(2 * owner_count, 2, tile_rows, width), ('yhi'...]
    ppermute x1, starting transfers between devices: 2.26 us -> 5.64 us  [shards(): partner = lax.ppermute(amps, 'yhi', [(0, 1), (1, 0)])]
    all_to_all x1, starting transfers between devices: 8.36 us -> 6.46 us  [shards(): meta = lax.all_to_all(meta, OCC, 0, 0, tiled=True)]
  transfers between devices with their start and end apart: 3 -> 4, of which waited for: 0 -> 0; matrix products, arithmetic and copies ran while one was open for 0% -> 0% of each run, Pallas kernels for 11% -> 8%
where the time goes in v7:
time: 129 us; the launch traced here: 128 us
  blocking collectives  83.9 us (65%)
  starting transfers between devices  26.4 us (20%)
  Pallas kernels  17 us (13%)
    all_gather x1, blocking collectives, shards(): code = lax.all_gather(code, 'z', axis=0, tiled=True)  48.9 us
    all_to_all x1, blocking collectives, shards(): lax.all_to_all(send.reshape(2 * owner_count, 2, tile_rows, width), ('yhi'...  34.9 us
    ppermute x1, starting transfers between devices, shards(): other = lax.ppermute(mine, 'core', [(0, 1), (1, 0)])  8.95 us
    all_to_all x1, starting transfers between devices, shards(): meta = lax.all_to_all(meta, OCC, 0, 0, tiled=True)  6.46 us
    ppermute x1, starting transfers between devices, shards(): partner = lax.ppermute(amps, 'yhi', [(0, 1), (1, 0)])  5.64 us
    ppermute x1, starting transfers between devices, shards(): mine = lax.ppermute(part, ('ylo', 'yhi'), [(n, 3 - n) for n in range(4)])  5.39 us
    pallas_call x1, Pallas kernels, near(): pl.pallas_call(near_kernel, out_shape=(jax.ShapeDtypeStruct((rows, depth)...  3.89 us
    pallas_call x1, Pallas kernels, far(): pl.pallas_call(far_kernel, out_shape=jax.ShapeDtypeStruct(send.shape, BF1...  3.71 us
  transfers between devices with their start and end apart: 4, of which 0 were waited for; matrix products, arithmetic and copies ran while one was open for 0% of the time, Pallas kernels for 8%

profile of v7, /device:TPU:1, one launch (start us, length us, event | category | flops | bytes accessed | tf_op | source)
XLA Modules:
  0.0 128.2 jit_solution(6670523327368781292)
XLA Ops:
  0.0 5.6 %collective-permute-start.1 = (bf16[1024,96]{0,1:T(8,128)(2,1)}, bf16[1024,96]{0,1:T(8,128)(2,1)S(1)}, u32[]{:S(2)}, u32[]{:S(2)}) collective-permute-start(bf16[1024,96]{0,1:T(8,128)(2,1)} %param.8), channel_id=1, source_target_pairs={{0,1},{1,0},{2,3},{3,2},{4,5},{5,4},{6,7},{7,6},{8,9},{9,8},{10,11... | collective-permute-start | bytes 589832 | tf_op jit(solution)/shard_map/ppermute | solution.py:334
  5.7 3.5 %route.1 = (s32[1,32]{1,0:T(1,128)}, s32[1,32]{1,0:T(1,128)}, bf16[16,32,128]{2,1,0:T(8,128)(2,1)}, bf16[1536,512]{1,0:T(8,128)(2,1)}) custom-call(s32[1,32]{1,0:T(1,128)} %bitcast.16, s32[1,32]{1,0:T(1,128)} %bitcast.17, bf16[8,128]{1,0:T(8,128)(2,1)} %bitcast.15, bf16[3072,512]{1,0:T(8,128)(2,1)} %ints_ref.1), custom_call_target="tpu_custom_call" | custom-call | tf_op jit(solution)/shard_map/route/pallas_call | solution.py:122
  9.2 0.0 copy-start.3
  9.2 6.5 %all-to-all-start = ((bf16[16,32,128]{2,1,0:T(8,128)(2,1)}), bf16[16,32,128]{2,1,0:T(8,128)(2,1)S(1)}, u32[]{:S(2)}, u32[]{:S(2)}) async-start(bf16[16,32,128]{2,1,0:T(8,128)(2,1)} %get-tuple-element.18), calls=%async_computation | async-start | bytes 262144 | tf_op jit(solution)/shard_map/all_to_all | solution.py:338
  15.6 5.4 %collective-permute-start = (bf16[1536,512]{1,0:T(8,128)(2,1)}, bf16[1536,512]{1,0:T(8,128)(2,1)}, u32[]{:S(2)}, u32[]{:S(2)}) collective-permute-start(bf16[1536,512]{1,0:T(8,128)(2,1)} %get-tuple-element.16), channel_id=1, source_target_pairs={{0,257},{1,256},{256,1},{257,0},{2,259},{3,258},{258,3},{259,2},{4... | collective-permute-start | bytes 4718600 | tf_op jit(solution)/shard_map/ppermute | solution.py:339
  21.0 0.0 collective-permute-done.1
  21.0 0.0 copy-start.4
  21.0 0.7 copy-done.4
  21.7 3.5 %order.1 = s16[192,512]{1,0:T(8,128)(2,1)} custom-call(bf16[96,1024]{1,0:T(8,128)(2,1)} %bitcast.12, bf16[96,1024]{1,0:T(8,128)(2,1)} %bitcast.13, s32[1,32]{1,0:T(1,128)} %get-tuple-element.17.refs_2_, s32[6,32]{1,0:T(8,128)} %bitcast.14), custom_call_target="tpu_custom_call" | custom-call | tf_op jit(solution)/shard_map/order/pallas_call | solution.py:178
  25.2 0.0 copy-start
  25.2 0.0 all-to-all-done.meta_ref
  25.2 48.9 %all-gather.1.code_ref = s16[3072,512]{1,0:T(8,128)(2,1)S(1)} all-gather(s16[192,512]{1,0:T(8,128)(2,1)} %order.1), channel_id=1, replica_groups=mesh['ylo'=2,'x'=4,'core'=2,'z'=16,'yhi'=2] {'z'}, dimensions={0}, use_global_device_ids=true | all-gather | bytes 3342336 | tf_op jit(solution)/shard_map/all_gather | solution.py:342
  74.1 0.0 collective-permute-done.mine_hbm
  74.1 9.0 %collective-permute-start.2 = (bf16[1536,512]{1,0:T(8,128)(2,1)}, bf16[1536,512]{1,0:T(8,128)(2,1)S(1)}, u32[]{:S(2)}, u32[]{:S(2)}) collective-permute-start(bf16[1536,512]{1,0:T(8,128)(2,1)} %collective-permute-done.mine_hbm), channel_id=1, source_target_pairs={{0,32},{32,0},{1,33},{33,1},{2,34},{34,2},{3,35},{35,3},{4,36},{36... | collective-permute-start | bytes 4718600 | tf_op jit(solution)/shard_map/ppermute | solution.py:344
  83.1 0.0 copy-done.3
  83.1 0.0 copy-done
  83.1 3.9 %near.1 = (bf16[512,3072]{1,0:T(8,128)(2,1)S(1)}, bf16[2,16,2,32,512]{4,3,2,1,0:T(8,128)(2,1)S(1)}) custom-call(s32[1,32]{1,0:T(1,128)S(1)} %copy-done.3, s16[3072,512]{1,0:T(8,128)(2,1)S(1)} %all-gather.1.code_ref, bf16[3072,512]{1,0:T(8,128)(2,1)S(1)} %copy-done), custom_call_target="tpu_custom_call" | custom-call | flops 1610612736 | bytes 11534336 | tf_op jit(solution)/shard_map/near/pallas_call | solution.py:219
  87.0 0.0 collective-permute-done.2.other_ref
  87.0 3.7 %far.1 = bf16[2,16,2,32,512]{4,3,2,1,0:T(8,128)(2,1)S(1)} custom-call(s32[1,32]{1,0:T(1,128)S(1)} %copy-done.3, bf16[512,3072]{1,0:T(8,128)(2,1)S(1)} %get-tuple-element.21.amps_ref, bf16[1536,512]{1,0:T(8,128)(2,1)} %collective-permute-done.mine_hbm, bf16[1536,512]{1,0:T(8,128)(2,1)S(1)} %collective-permute-done.2.other_ref, ...), custom_call_target="tpu_custom_call", output_to_operand_aliasing={{}: (4, {})} | custom-call | flops 1610612736 | bytes 8388608 | tf_op jit(solution)/shard_map/far/pallas_call | solution.py:258
  90.8 0.0 copy-start.1
  90.8 0.0 copy-start.2
  90.8 34.9 %all_to_all.10 = bf16[32,2,32,512]{3,2,1,0:T(8,128)(2,1)S(1)} all-to-all(bf16[32,2,32,512]{3,2,1,0:T(8,128)(2,1)S(1)} %bitcast.10), channel_id=1, replica_groups=mesh['ylo'=2,'x'=4,'core'=2,'z'=16,'yhi'=2] {'yhi','ylo','x','core'}, dimensions={0} | all-to-all | bytes 4194304 | tf_op jit(solution)/shard_map/all_to_all | solution.py:347
  125.7 0.0 copy-done.1
  125.7 0.0 copy-done.2
  125.7 2.5 %update.1 = bf16[64,32,512]{2,1,0:T(8,128)(2,1)} custom-call(bf16[2,16,2,32,512]{4,3,2,1,0:T(8,128)(2,1)S(1)} %bitcast.9, bf16[16,32,128]{2,1,0:T(8,128)(2,1)S(1)} %all-to-all-done.meta_ref, bf16[1,32,32]{2,1,0:T(8,128)(2,1)S(1)} %copy-done.1, f32[1,512]{1,0:T(1,128)S(1)} %bitcast.11), custom_call_target="tpu_custom_call" | custom-call | tf_op jit(solution)/shard_map/update/pallas_call | solution.py:313
Async XLA Ops:
  0.0 21.0 %collective-permute-start.1 = (bf16[1024,96]{0,1:T(8,128)(2,1)}, bf16[1024,96]{0,1:T(8,128)(2,1)S(1)}, u32[]{:S(2)}, u32[]{:S(2)}) collective-permute-start(bf16[1024,96]{0,1:T(8,128)(2,1)} %param.8), channel_id=1, source_target_pairs={{0,1},{1,0},{2,3},{3,2},{4,5},{5,4},{6,7},{7,6},{8,9},{9,8},{10,11... | collective-permute-start | bytes 589832 | tf_op jit(solution)/shard_map/ppermute | solution.py:334
  9.2 73.9 %copy-start.3 = (s32[1,32]{1,0:T(1,128)S(1)}, s32[1,32]{1,0:T(1,128)}, u32[]{:S(2)}) copy-start(s32[1,32]{1,0:T(1,128)} %get-tuple-element.15.slot) | copy-start | bytes 388
  9.2 16.0 %all-to-all-start = ((bf16[16,32,128]{2,1,0:T(8,128)(2,1)}), bf16[16,32,128]{2,1,0:T(8,128)(2,1)S(1)}, u32[]{:S(2)}, u32[]{:S(2)}) async-start(bf16[16,32,128]{2,1,0:T(8,128)(2,1)} %get-tuple-element.18), calls=%async_computation | async-start | bytes 262144 | tf_op jit(solution)/shard_map/all_to_all | solution.py:338
  15.6 58.5 %collective-permute-start = (bf16[1536,512]{1,0:T(8,128)(2,1)}, bf16[1536,512]{1,0:T(8,128)(2,1)}, u32[]{:S(2)}, u32[]{:S(2)}) collective-permute-start(bf16[1536,512]{1,0:T(8,128)(2,1)} %get-tuple-element.16), channel_id=1, source_target_pairs={{0,257},{1,256},{256,1},{257,0},{2,259},{3,258},{258,3},{259,2},{4... | collective-permute-start | bytes 4718600 | tf_op jit(solution)/shard_map/ppermute | solution.py:339
  21.0 0.7 copy-start.4
  25.2 57.9 %copy-start = (bf16[3072,512]{1,0:T(8,128)(2,1)S(1)}, bf16[3072,512]{1,0:T(8,128)(2,1)}, u32[]{:S(2)}) copy-start(bf16[3072,512]{1,0:T(8,128)(2,1)} %ints_ref.1) | copy-start | bytes 9437188
  74.1 12.9 %collective-permute-start.2 = (bf16[1536,512]{1,0:T(8,128)(2,1)}, bf16[1536,512]{1,0:T(8,128)(2,1)S(1)}, u32[]{:S(2)}, u32[]{:S(2)}) collective-permute-start(bf16[1536,512]{1,0:T(8,128)(2,1)} %collective-permute-done.mine_hbm), channel_id=1, source_target_pairs={{0,32},{32,0},{1,33},{33,1},{2,34},{34,2},{3,35},{35,3},{4,36},{36... | collective-permute-start | bytes 4718600 | tf_op jit(solution)/shard_map/ppermute | solution.py:344
  90.8 35.0 %copy-start.1 = (bf16[1,32,32]{2,1,0:T(8,128)(2,1)S(1)}, bf16[1,32,32]{2,1,0:T(8,128)(2,1)}, u32[]{:S(2)}) copy-start(bf16[1,32,32]{2,1,0:T(8,128)(2,1)} %mix_ref.1) | copy-start | bytes 6148
  90.8 35.0 %copy-start.2 = (f32[512]{0:T(512)S(1)}, f32[512]{0:T(512)}, u32[]{:S(2)}) copy-start(f32[512]{0:T(512)} %param.14) | copy-start | bytes 6148

commit v8 on v6

--- a/solution.py
+++ b/solution.py
@@ -13,7 +13,6 @@
 I32 = jnp.int32
 PREP_LIMIT = 62
 NEAR_LIMIT = 32
-FAR_LIMIT = 32
 
 
 def iota(shape, dim):
@@ -34,15 +33,14 @@
     down = q < 127.5
     q = q * jnp.where(up, 0.5, jnp.where(down, 2.0, 1.0))
     e = e + jnp.where(up, 1.0, jnp.where(down, -1.0, 0.0)) - jnp.where(small, 60.0, 0.0)
-    code = (e + 127.0) * 128.0 + (jnp.floor(q + 0.5) - 128.0)
-    code = jnp.where(a < 2.0**-126, 0.0, code)
-    return jnp.where(v < 0.0, code - 32768.0, code).astype(I32)
+    q = jnp.floor(q + 0.5)
+    code = (e + 127.0) * 128.0 + jnp.where(v < 0.0, 255.0 - q - 32768.0, q - 128.0)
+    return jnp.where(a < 2.0**-126, 0.0, code).astype(I32)
 
 
 def decode(c):
     c = c.astype(I32)
-    m = (c & 127) | 128
-    f = jnp.where(c < 0, -m, m)
+    f = jnp.where(c < 0, -255, 128) + (c & 127)
     return (f.astype(F32) * jnp.exp2(((c >> 7) & 255).astype(F32) - 127.0)).astype(BF16)
 
 
@@ -135,7 +133,12 @@
     half = rows // 2
     mine = amps_ref.at[pl.ds(pl.multiple_of(h * k_width, 16), k_width)]
     other = amps_ref.at[pl.ds(pl.multiple_of((1 - h) * k_width, 16), k_width)]
-    fetch(((rank_hbm, rank_ref), (mask_hbm, mask_ref), (own_hbm, mine), (partner_hbm, other)), sems)
+    large = [
+        pltpu.make_async_copy(own_hbm, mine, sems.at[2]), pltpu.make_async_copy(partner_hbm, other, sems.at[3])
+    ]
+    for read in large:
+        read.start()
+    fetch(((rank_hbm, rank_ref), (mask_hbm, mask_ref)), sems)
     lane = iota((tiles, 128), 1)
     cols = jnp.where(lane == 0, as_column(rank_ref[...].astype(F32)), 0.0).astype(BF16)
     spread = rows_of_tiles(rows, tiles)
@@ -144,9 +147,11 @@
     select = jnp.where(column_tile == iota((depth, k_tiles), 1), 1.0, 0.0).astype(BF16)
     present = dot(select, mask_ref[...].astype(F32).astype(BF16)).astype(BF16)
     present = dot(present, spread, 1, 1)
-    masked = jnp.where(present > 0.5, amps_ref[...].astype(F32), 0.0).astype(BF16)
     target = ((r + h) % 2) * half + (r // 2) * tile_rows + iota((rows, 1), 0) % tile_rows
     moved = jnp.where(target == iota((rows, half), 1), 1.0, 0.0).astype(BF16)
+    for read in large:
+        read.wait()
+    masked = jnp.where(present > 0.5, amps_ref[...].astype(F32), 0.0).astype(BF16)
     code_ref[...] = encode(dot(masked, moved)).astype(jnp.int16)
 
 
@@ -181,85 +186,46 @@
         out_ref[to, at // 2, at % 2] = tile.astype(BF16)
 
 
-def near_kernel(slot, code_ref, ints_ref, amps_ref, out_ref):
+def ladder_kernel(slot, code_ref, ints_ref, far_hbm, out_ref, amps_ref, far_ref, sem):
+    read = pltpu.make_async_copy(far_hbm, far_ref, sem)
+    read.start()
+    h = lax.axis_index("yhi").astype(I32)
     depth, rows = code_ref.shape
-    block = depth // 8
+    tile_rows = out_ref.shape[3]
+    block = depth // 4
     for k in range(0, depth, block):
         amps_ref[:, k : k + block] = decode(code_ref[k : k + block]).T
-    h = lax.axis_index("yhi").astype(I32)
-    tall = rows // 4
+    tall = rows // 2
     for r in range(0, rows, tall):
         acc = dot(amps_ref[r : r + tall], ints_ref[...])
-        place_tiles(slot, h, r // out_ref.shape[3], acc, out_ref, h)
-
-
-def near(slot, code, ints, owner_count, tile_rows):
+        place_tiles(slot, h, r // tile_rows, acc, out_ref, h)
+    read.wait()
+    for r in range(0, rows, tall):
+        acc = dot(amps_ref[r : r + tall], far_ref[...])
+        place_tiles(slot, h, r // tile_rows, acc, out_ref, 1 - h)
+
+
+def ladder(slot, code, ints, ints_far, owner_count, tile_rows):
     depth, rows = code.shape
     width = ints.shape[1]
     smem = pl.BlockSpec(memory_space=pltpu.SMEM)
     vmem = pl.BlockSpec(memory_space=pltpu.VMEM)
     return pl.pallas_call(
-        near_kernel,
-        out_shape=(
-            jax.ShapeDtypeStruct((rows, depth), BF16),
-            jax.ShapeDtypeStruct((2, owner_count, 2, tile_rows, width), BF16),
-        ),
-        in_specs=[smem, vmem, vmem],
-        out_specs=(vmem, vmem),
+        ladder_kernel,
+        out_shape=jax.ShapeDtypeStruct((2, owner_count, 2, tile_rows, width), BF16),
+        in_specs=[smem, vmem, vmem, pl.BlockSpec(memory_space=pl.ANY)],
+        out_specs=vmem,
+        scratch_shapes=[
+            pltpu.VMEM((rows, depth), BF16),
+            pltpu.VMEM(ints.shape, BF16),
+            pltpu.SemaphoreType.DMA,
+        ],
         compiler_params=pltpu.CompilerParams(vmem_limit_bytes=NEAR_LIMIT << 20),
         cost_estimate=pl.CostEstimate(
-            flops=2 * rows * depth * width, bytes_accessed=11 << 20, transcendentals=rows * depth
+            flops=4 * rows * depth * width, bytes_accessed=11 << 20, transcendentals=rows * depth
         ),
-        name="near",
-    )(slot, code, ints)
-
-
-def far_kernel(slot, amps_ref, ints_hbm, _, out_ref, ints_ref, acc_ref, sems):
-    h = lax.axis_index("yhi").astype(I32)
-    rows, depth = amps_ref.shape
-    parts = sems.shape[0]
-    block = depth // parts
-    reads = []
-    for n in range(parts):
-        at = pl.ds(n * block, block)
-        reads.append(pltpu.make_async_copy(ints_hbm.at[at], ints_ref.at[at], sems.at[n]))
-        reads[-1].start()
-    tall = rows // 2
-    for n in range(parts):
-        reads[n].wait()
-        at = pl.ds(n * block, block)
-        for r in range(0, rows, tall):
-            part = dot(amps_ref[r : r + tall, at], ints_ref[at])
-            if n > 0:
-                part += acc_ref[r : r + tall]
-            if n < parts - 1:
-                acc_ref[r : r + tall] = part
-            else:
-                place_tiles(slot, h, r // out_ref.shape[3], part, out_ref, 1 - h)
-
-
-def far(slot, amps, ints, send):
-    rows, depth = amps.shape
-    width = ints.shape[1]
-    smem = pl.BlockSpec(memory_space=pltpu.SMEM)
-    vmem = pl.BlockSpec(memory_space=pltpu.VMEM)
-    return pl.pallas_call(
-        far_kernel,
-        out_shape=jax.ShapeDtypeStruct(send.shape, BF16),
-        in_specs=[smem, vmem, pl.BlockSpec(memory_space=pl.ANY), vmem],
-        out_specs=vmem,
-        scratch_shapes=[
-            pltpu.VMEM(ints.shape, BF16),
-            pltpu.VMEM((rows, width), F32),
-            pltpu.SemaphoreType.DMA((3,)),
-        ],
-        input_output_aliases={3: 0},
-        compiler_params=pltpu.CompilerParams(vmem_limit_bytes=FAR_LIMIT << 20),
-        cost_estimate=pl.CostEstimate(
-            flops=2 * rows * depth * width, bytes_accessed=8 << 20, transcendentals=0
-        ),
-        name="far",
-    )(slot, amps, ints, send)
+        name="ladder",
+    )(slot, code, ints, ints_far)
 
 
 def update_kernel(recv_ref, meta_ref, mix_ref, vir_ref, out_ref, weight_ref, new_ref, sems):
@@ -325,8 +291,7 @@
     meta = lax.all_to_all(meta, OCC, 0, 0, tiled=True)
     code = order(amps.T, partner.T, rank, amp_mask.T, depth // k_tiles)
     code = lax.all_gather(code, "z", axis=0, tiled=True)
-    decoded, send = near(slot, code, ints, owner_count, tile_rows)
-    send = far(slot, decoded, ints_far, send)
+    send = ladder(slot, code, ints, ints_far, owner_count, tile_rows)
     recv = lax.all_to_all(
         send.reshape(2 * owner_count, 2, tile_rows, width), ("yhi",) + OCC, 0, 0, tiled=True
     )

time: 126 us -> 126 us (level)
  waiting for transfers between devices: 0.01 us -> 3.53 us
  blocking collectives: 92.5 us -> 89 us
    ppermute x1, waiting for transfers between devices: 0.01 us -> 3.52 us  [shards(): lax.ppermute(ints, ('ylo', 'yhi'), [(n, 3 - n) for n in range(4)])]
    all_to_all x1, blocking collectives: 43.1 us -> 39.6 us  [shards(): lax.all_to_all(send.reshape(2 * owner_count, 2, tile_rows, width), ('yhi'...]
    pallas_call x2 -> x1, Pallas kernels: 7.9 us -> 7.72 us  [ladder(): pl.pallas_call(ladder_kernel, out_shape=jax.ShapeDtypeStruct((2, owner_co...]
  transfers between devices with their start and end apart: 3 -> 3, of which waited for: 0 -> 1; matrix products, arithmetic and copies ran while one was open for 0% -> 0% of each run, Pallas kernels for 11% -> 11%
where the time goes in v8:
time: 126 us; the launch traced here: 125 us
  blocking collectives  89 us (71%)
  starting transfers between devices  16.1 us (13%)
  Pallas kernels  15.9 us (13%)
  waiting for transfers between devices  3.53 us (3%)
    all_gather x1, blocking collectives, shards(): code = lax.all_gather(code, 'z', axis=0, tiled=True)  49.4 us
    all_to_all x1, blocking collectives, shards(): lax.all_to_all(send.reshape(2 * owner_count, 2, tile_rows, width), ('yhi'...  39.6 us
    all_to_all x1, starting transfers between devices, shards(): meta = lax.all_to_all(meta, OCC, 0, 0, tiled=True)  8.36 us
    pallas_call x1, Pallas kernels, ladder(): pl.pallas_call(ladder_kernel, out_shape=jax.ShapeDtypeStruct((2, owner_co...  7.72 us
    ppermute x1, starting transfers between devices, shards(): lax.ppermute(ints, ('ylo', 'yhi'), [(n, 3 - n) for n in range(4)])  5.46 us
    ppermute x1, waiting for transfers between devices, shards(): lax.ppermute(ints, ('ylo', 'yhi'), [(n, 3 - n) for n in range(4)])  3.52 us
    pallas_call x1, Pallas kernels, order(): pl.pallas_call(kernel, out_shape=jax.ShapeDtypeStruct((2 * k_width, rows...  3.48 us
  transfers between devices with their start and end apart: 3, of which 1 were waited for; matrix products, arithmetic and copies ran while one was open for 0% of the time, Pallas kernels for 11%

profile of v8, /device:TPU:1, one launch (start us, length us, event | category | flops | bytes accessed | tf_op | source)
XLA Modules:
  0.0 125.3 jit_solution(13090543173431844197)
XLA Ops:
  0.0 5.5 %collective-permute-start.1 = (bf16[3072,512]{1,0:T(8,128)(2,1)}, bf16[3072,512]{1,0:T(8,128)(2,1)}, u32[]{:S(2)}, u32[]{:S(2)}) collective-permute-start(bf16[3072,512]{1,0:T(8,128)(2,1)} %ints_ref.1), channel_id=1, source_target_pairs={{0,257},{1,256},{256,1},{257,0},{2,259},{3,258},{258,3},{259,2},{4... | collective-permute-start | bytes 9437192 | tf_op jit(solution)/shard_map/ppermute | solution.py:288
  5.5 2.3 %collective-permute-start = (bf16[1024,96]{0,1:T(8,128)(2,1)}, bf16[1024,96]{0,1:T(8,128)(2,1)S(1)}, u32[]{:S(2)}, u32[]{:S(2)}) collective-permute-start(bf16[1024,96]{0,1:T(8,128)(2,1)} %param.8), channel_id=1, source_target_pairs={{0,1},{1,0},{2,3},{3,2},{4,5},{5,4},{6,7},{7,6},{8,9},{9,8},{10,11... | collective-permute-start | bytes 589832 | tf_op jit(solution)/shard_map/ppermute | solution.py:289
  7.7 2.3 %route.1 = (s32[1,32]{1,0:T(1,128)}, s32[1,32]{1,0:T(1,128)}, bf16[16,32,128]{2,1,0:T(8,128)(2,1)}) custom-call(s32[1,32]{1,0:T(1,128)} %bitcast.16, s32[1,32]{1,0:T(1,128)} %bitcast.17, bf16[8,128]{1,0:T(8,128)(2,1)} %bitcast.15), custom_call_target="tpu_custom_call" | custom-call | tf_op jit(solution)/shard_map/route/pallas_call | solution.py:110
  10.0 0.0 copy-start.3
  10.0 8.4 %all-to-all-start.1 = ((bf16[16,32,128]{2,1,0:T(8,128)(2,1)}), bf16[16,32,128]{2,1,0:T(8,128)(2,1)S(1)}, u32[]{:S(2)}, u32[]{:S(2)}) async-start(bf16[16,32,128]{2,1,0:T(8,128)(2,1)} %get-tuple-element.10), calls=%async_computation.1 | async-start | bytes 262144 | tf_op jit(solution)/shard_map/all_to_all | solution.py:291
  18.4 0.0 collective-permute-done
  18.4 0.0 copy-start.4
  18.4 0.7 copy-done.4
  19.1 3.5 %order.1 = s16[192,512]{1,0:T(8,128)(2,1)} custom-call(bf16[96,1024]{1,0:T(8,128)(2,1)} %bitcast.12, bf16[96,1024]{1,0:T(8,128)(2,1)} %bitcast.13, s32[1,32]{1,0:T(1,128)} %get-tuple-element.9.refs_2_, s32[6,32]{1,0:T(8,128)} %bitcast.14), custom_call_target="tpu_custom_call" | custom-call | tf_op jit(solution)/shard_map/order/pallas_call | solution.py:165
  22.6 0.0 copy-start.2
  22.6 49.4 %all-gather.1.code_ref = s16[3072,512]{1,0:T(8,128)(2,1)S(1)} all-gather(s16[192,512]{1,0:T(8,128)(2,1)} %order.1), channel_id=1, replica_groups=mesh['ylo'=2,'x'=4,'core'=2,'z'=16,'yhi'=2] {'z'}, dimensions={0}, use_global_device_ids=true | all-gather | bytes 3342336 | tf_op jit(solution)/shard_map/all_gather | solution.py:293
  72.0 3.5 %collective-permute-done.1.far_hbm = bf16[3072,512]{1,0:T(8,128)(2,1)} collective-permute-done((bf16[3072,512]{1,0:T(8,128)(2,1)}, bf16[3072,512]{1,0:T(8,128)(2,1)}, u32[]{:S(2)}, u32[]{:S(2)}) %collective-permute-start.1) | collective-permute-done | bytes 3145760 | tf_op jit(solution)/shard_map/ppermute | solution.py:288
  75.5 0.0 copy-done.3
  75.5 0.0 copy-done.2
  75.5 7.7 %ladder.1 = bf16[2,16,2,32,512]{4,3,2,1,0:T(8,128)(2,1)S(1)} custom-call(s32[1,32]{1,0:T(1,128)S(1)} %copy-done.3, s16[3072,512]{1,0:T(8,128)(2,1)S(1)} %all-gather.1.code_ref, bf16[3072,512]{1,0:T(8,128)(2,1)S(1)} %copy-done.2, bf16[3072,512]{1,0:T(8,128)(2,1)} %collective-permute-done.1.far_hbm), custom_call_target="tpu_custom_call" | custom-call | flops 3221225472 | bytes 11534336 | tf_op jit(solution)/shard_map/ladder/pallas_call | solution.py:213
  83.2 0.0 copy-start
  83.3 0.0 copy-start.1
  83.3 0.0 all-to-all-done.1.meta_ref
  83.3 39.6 %all_to_all.10 = bf16[32,2,32,512]{3,2,1,0:T(8,128)(2,1)S(1)} all-to-all(bf16[32,2,32,512]{3,2,1,0:T(8,128)(2,1)S(1)} %bitcast.10), channel_id=1, replica_groups=mesh['ylo'=2,'x'=4,'core'=2,'z'=16,'yhi'=2] {'yhi','ylo','x','core'}, dimensions={0} | all-to-all | bytes 4194304 | tf_op jit(solution)/shard_map/all_to_all | solution.py:295
  122.9 0.0 copy-done
  122.9 0.0 copy-done.1
  122.9 2.4 %update.1 = bf16[64,32,512]{2,1,0:T(8,128)(2,1)} custom-call(bf16[2,16,2,32,512]{4,3,2,1,0:T(8,128)(2,1)S(1)} %bitcast.9, bf16[16,32,128]{2,1,0:T(8,128)(2,1)S(1)} %all-to-all-done.1.meta_ref, bf16[1,32,32]{2,1,0:T(8,128)(2,1)S(1)} %copy-done, f32[1,512]{1,0:T(1,128)S(1)} %bitcast.11), custom_call_target="tpu_custom_call" | custom-call | tf_op jit(solution)/shard_map/update/pallas_call | solution.py:267
Async XLA Ops:
  0.0 75.5 %collective-permute-start.1 = (bf16[3072,512]{1,0:T(8,128)(2,1)}, bf16[3072,512]{1,0:T(8,128)(2,1)}, u32[]{:S(2)}, u32[]{:S(2)}) collective-permute-start(bf16[3072,512]{1,0:T(8,128)(2,1)} %ints_ref.1), channel_id=1, source_target_pairs={{0,257},{1,256},{256,1},{257,0},{2,259},{3,258},{258,3},{259,2},{4... | collective-permute-start | bytes 9437192 | tf_op jit(solution)/shard_map/ppermute | solution.py:288
  5.5 12.9 %collective-permute-start = (bf16[1024,96]{0,1:T(8,128)(2,1)}, bf16[1024,96]{0,1:T(8,128)(2,1)S(1)}, u32[]{:S(2)}, u32[]{:S(2)}) collective-permute-start(bf16[1024,96]{0,1:T(8,128)(2,1)} %param.8), channel_id=1, source_target_pairs={{0,1},{1,0},{2,3},{3,2},{4,5},{5,4},{6,7},{7,6},{8,9},{9,8},{10,11... | collective-permute-start | bytes 589832 | tf_op jit(solution)/shard_map/ppermute | solution.py:289
  10.0 65.5 %copy-start.3 = (s32[1,32]{1,0:T(1,128)S(1)}, s32[1,32]{1,0:T(1,128)}, u32[]{:S(2)}) copy-start(s32[1,32]{1,0:T(1,128)} %get-tuple-element.8.slot) | copy-start | bytes 388
  10.0 73.2 %all-to-all-start.1 = ((bf16[16,32,128]{2,1,0:T(8,128)(2,1)}), bf16[16,32,128]{2,1,0:T(8,128)(2,1)S(1)}, u32[]{:S(2)}, u32[]{:S(2)}) async-start(bf16[16,32,128]{2,1,0:T(8,128)(2,1)} %get-tuple-element.10), calls=%async_computation.1 | async-start | bytes 262144 | tf_op jit(solution)/shard_map/all_to_all | solution.py:291
  18.4 0.7 copy-start.4
  22.6 53.0 %copy-start.2 = (bf16[3072,512]{1,0:T(8,128)(2,1)S(1)}, bf16[3072,512]{1,0:T(8,128)(2,1)}, u32[]{:S(2)}) copy-start(bf16[3072,512]{1,0:T(8,128)(2,1)} %ints_ref.1) | copy-start | bytes 9437188
  83.2 39.6 %copy-start = (bf16[1,32,32]{2,1,0:T(8,128)(2,1)S(1)}, bf16[1,32,32]{2,1,0:T(8,128)(2,1)}, u32[]{:S(2)}) copy-start(bf16[1,32,32]{2,1,0:T(8,128)(2,1)} %mix_ref.1) | copy-start | bytes 6148
  83.3 39.6 %copy-start.1 = (f32[512]{0:T(512)S(1)}, f32[512]{0:T(512)}, u32[]{:S(2)}) copy-start(f32[512]{0:T(512)} %param.14) | copy-start | bytes 6148

commit v9 on v6

--- a/solution.py
+++ b/solution.py
@@ -34,15 +34,14 @@
     down = q < 127.5
     q = q * jnp.where(up, 0.5, jnp.where(down, 2.0, 1.0))
     e = e + jnp.where(up, 1.0, jnp.where(down, -1.0, 0.0)) - jnp.where(small, 60.0, 0.0)
-    code = (e + 127.0) * 128.0 + (jnp.floor(q + 0.5) - 128.0)
-    code = jnp.where(a < 2.0**-126, 0.0, code)
-    return jnp.where(v < 0.0, code - 32768.0, code).astype(I32)
+    q = jnp.floor(q + 0.5)
+    code = (e + 127.0) * 128.0 + jnp.where(v < 0.0, 255.0 - q - 32768.0, q - 128.0)
+    return jnp.where(a < 2.0**-126, 0.0, code).astype(I32)
 
 
 def decode(c):
     c = c.astype(I32)
-    m = (c & 127) | 128
-    f = jnp.where(c < 0, -m, m)
+    f = jnp.where(c < 0, -255, 128) + (c & 127)
     return (f.astype(F32) * jnp.exp2(((c >> 7) & 255).astype(F32) - 127.0)).astype(BF16)
 
 
@@ -135,7 +134,12 @@
     half = rows // 2
     mine = amps_ref.at[pl.ds(pl.multiple_of(h * k_width, 16), k_width)]
     other = amps_ref.at[pl.ds(pl.multiple_of((1 - h) * k_width, 16), k_width)]
-    fetch(((rank_hbm, rank_ref), (mask_hbm, mask_ref), (own_hbm, mine), (partner_hbm, other)), sems)
+    large = [
+        pltpu.make_async_copy(own_hbm, mine, sems.at[2]), pltpu.make_async_copy(partner_hbm, other, sems.at[3])
+    ]
+    for read in large:
+        read.start()
+    fetch(((rank_hbm, rank_ref), (mask_hbm, mask_ref)), sems)
     lane = iota((tiles, 128), 1)
     cols = jnp.where(lane == 0, as_column(rank_ref[...].astype(F32)), 0.0).astype(BF16)
     spread = rows_of_tiles(rows, tiles)
@@ -144,9 +148,11 @@
     select = jnp.where(column_tile == iota((depth, k_tiles), 1), 1.0, 0.0).astype(BF16)
     present = dot(select, mask_ref[...].astype(F32).astype(BF16)).astype(BF16)
     present = dot(present, spread, 1, 1)
-    masked = jnp.where(present > 0.5, amps_ref[...].astype(F32), 0.0).astype(BF16)
     target = ((r + h) % 2) * half + (r // 2) * tile_rows + iota((rows, 1), 0) % tile_rows
     moved = jnp.where(target == iota((rows, half), 1), 1.0, 0.0).astype(BF16)
+    for read in large:
+        read.wait()
+    masked = jnp.where(present > 0.5, amps_ref[...].astype(F32), 0.0).astype(BF16)
     code_ref[...] = encode(dot(masked, moved)).astype(jnp.int16)
 
 

time: 126 us -> 125 us (level)
  no operation moved by 1% of the time
where the time goes in v9:
time: 125 us
  blocking collectives  92.5 us (74%)
  starting transfers between devices  16.1 us (13%)
  Pallas kernels  15.8 us (13%)
    all_gather x1, blocking collectives, shards(): code = lax.all_gather(code, 'z', axis=0, tiled=True)  49.5 us
    all_to_all x1, blocking collectives, shards(): lax.all_to_all(send.reshape(2 * owner_count, 2, tile_rows, width), ('yhi'...  43 us
    all_to_all x1, starting transfers between devices, shards(): meta = lax.all_to_all(meta, OCC, 0, 0, tiled=True)  8.36 us
    ppermute x1, starting transfers between devices, shards(): lax.ppermute(ints, ('ylo', 'yhi'), [(n, 3 - n) for n in range(4)])  5.46 us
    pallas_call x1, Pallas kernels, near(): pl.pallas_call(near_kernel, out_shape=(jax.ShapeDtypeStruct((rows, depth)...  3.87 us
    pallas_call x1, Pallas kernels, far(): pl.pallas_call(far_kernel, out_shape=jax.ShapeDtypeStruct(send.shape, BF1...  3.75 us
    pallas_call x1, Pallas kernels, order(): pl.pallas_call(kernel, out_shape=jax.ShapeDtypeStruct((2 * k_width, rows...  3.48 us
  transfers between devices with their start and end apart: 3, of which 0 were waited for; matrix products, arithmetic and copies ran while one was open for 0% of the time, Pallas kernels for 11%

profile of v9, /device:TPU:1, one launch (start us, length us, event | category | flops | bytes accessed | tf_op | source)
XLA Modules:
  0.0 125.2 jit_solution(3171326070198457508)
XLA Ops:
  0.0 5.5 %collective-permute-start.1 = (bf16[3072,512]{1,0:T(8,128)(2,1)}, bf16[3072,512]{1,0:T(8,128)(2,1)}, u32[]{:S(2)}, u32[]{:S(2)}) collective-permute-start(bf16[3072,512]{1,0:T(8,128)(2,1)} %ints_ref.1), channel_id=1, source_target_pairs={{0,257},{1,256},{256,1},{257,0},{2,259},{3,258},{258,3},{259,2},{4... | collective-permute-start | bytes 9437192 | tf_op jit(solution)/shard_map/ppermute | solution.py:328
  5.5 2.3 %collective-permute-start = (bf16[1024,96]{0,1:T(8,128)(2,1)}, bf16[1024,96]{0,1:T(8,128)(2,1)S(1)}, u32[]{:S(2)}, u32[]{:S(2)}) collective-permute-start(bf16[1024,96]{0,1:T(8,128)(2,1)} %param.8), channel_id=1, source_target_pairs={{0,1},{1,0},{2,3},{3,2},{4,5},{5,4},{6,7},{7,6},{8,9},{9,8},{10,11... | collective-permute-start | bytes 589832 | tf_op jit(solution)/shard_map/ppermute | solution.py:329
  7.7 2.3 %route.1 = (s32[1,32]{1,0:T(1,128)}, s32[1,32]{1,0:T(1,128)}, bf16[16,32,128]{2,1,0:T(8,128)(2,1)}) custom-call(s32[1,32]{1,0:T(1,128)} %bitcast.16, s32[1,32]{1,0:T(1,128)} %bitcast.17, bf16[8,128]{1,0:T(8,128)(2,1)} %bitcast.15), custom_call_target="tpu_custom_call" | custom-call | tf_op jit(solution)/shard_map/route/pallas_call | solution.py:111
  10.0 0.0 copy-start.3
  10.0 8.4 %all-to-all-start.1 = ((bf16[16,32,128]{2,1,0:T(8,128)(2,1)}), bf16[16,32,128]{2,1,0:T(8,128)(2,1)S(1)}, u32[]{:S(2)}, u32[]{:S(2)}) async-start(bf16[16,32,128]{2,1,0:T(8,128)(2,1)} %get-tuple-element.14), calls=%async_computation.1 | async-start | bytes 262144 | tf_op jit(solution)/shard_map/all_to_all | solution.py:331
  18.4 0.0 collective-permute-done
  18.4 0.0 copy-start.4
  18.4 0.7 copy-done.4
  19.1 3.5 %order.1 = s16[192,512]{1,0:T(8,128)(2,1)} custom-call(bf16[96,1024]{1,0:T(8,128)(2,1)} %bitcast.12, bf16[96,1024]{1,0:T(8,128)(2,1)} %bitcast.13, s32[1,32]{1,0:T(1,128)} %get-tuple-element.11.refs_2_, s32[6,32]{1,0:T(8,128)} %bitcast.14), custom_call_target="tpu_custom_call" | custom-call | tf_op jit(solution)/shard_map/order/pallas_call | solution.py:166
  22.6 0.0 copy-start
  22.6 49.5 %all-gather.1.code_ref = s16[3072,512]{1,0:T(8,128)(2,1)S(1)} all-gather(s16[192,512]{1,0:T(8,128)(2,1)} %order.1), channel_id=1, replica_groups=mesh['ylo'=2,'x'=4,'core'=2,'z'=16,'yhi'=2] {'z'}, dimensions={0}, use_global_device_ids=true | all-gather | bytes 3342336 | tf_op jit(solution)/shard_map/all_gather | solution.py:333
  72.1 0.0 copy-done.3
  72.1 0.0 copy-done
  72.1 3.9 %near.1 = (bf16[512,3072]{1,0:T(8,128)(2,1)S(1)}, bf16[2,16,2,32,512]{4,3,2,1,0:T(8,128)(2,1)S(1)}) custom-call(s32[1,32]{1,0:T(1,128)S(1)} %copy-done.3, s16[3072,512]{1,0:T(8,128)(2,1)S(1)} %all-gather.1.code_ref, bf16[3072,512]{1,0:T(8,128)(2,1)S(1)} %copy-done), custom_call_target="tpu_custom_call" | custom-call | flops 1610612736 | bytes 11534336 | tf_op jit(solution)/shard_map/near/pallas_call | solution.py:207
  75.9 0.0 collective-permute-done.1.ints_hbm
  75.9 3.7 %far.1 = bf16[2,16,2,32,512]{4,3,2,1,0:T(8,128)(2,1)S(1)} custom-call(s32[1,32]{1,0:T(1,128)S(1)} %copy-done.3, bf16[512,3072]{1,0:T(8,128)(2,1)S(1)} %get-tuple-element.12.amps_ref, bf16[3072,512]{1,0:T(8,128)(2,1)} %collective-permute-done.1.ints_hbm, bf16[2,16,2,32,512]{4,3,2,1,0:T(8,128)(2,1)S(1)} %get-tuple-element.13._), custom_call_target="tpu_custom_call", output_to_operand_aliasing={{}: (3, {})} | custom-call | flops 1610612736 | bytes 8388608 | tf_op jit(solution)/shard_map/far/pallas_call | solution.py:252
  79.7 0.0 copy-start.1
  79.7 0.0 copy-start.2
  79.7 0.0 all-to-all-done.1.meta_ref
  79.7 43.0 %all_to_all.10 = bf16[32,2,32,512]{3,2,1,0:T(8,128)(2,1)S(1)} all-to-all(bf16[32,2,32,512]{3,2,1,0:T(8,128)(2,1)S(1)} %bitcast.10), channel_id=1, replica_groups=mesh['ylo'=2,'x'=4,'core'=2,'z'=16,'yhi'=2] {'yhi','ylo','x','core'}, dimensions={0} | all-to-all | bytes 4194304 | tf_op jit(solution)/shard_map/all_to_all | solution.py:336
  122.7 0.0 copy-done.1
  122.7 0.0 copy-done.2
  122.7 2.4 %update.1 = bf16[64,32,512]{2,1,0:T(8,128)(2,1)} custom-call(bf16[2,16,2,32,512]{4,3,2,1,0:T(8,128)(2,1)S(1)} %bitcast.9, bf16[16,32,128]{2,1,0:T(8,128)(2,1)S(1)} %all-to-all-done.1.meta_ref, bf16[1,32,32]{2,1,0:T(8,128)(2,1)S(1)} %copy-done.1, f32[1,512]{1,0:T(1,128)S(1)} %bitcast.11), custom_call_target="tpu_custom_call" | custom-call | tf_op jit(solution)/shard_map/update/pallas_call | solution.py:307
Async XLA Ops:
  0.0 75.9 %collective-permute-start.1 = (bf16[3072,512]{1,0:T(8,128)(2,1)}, bf16[3072,512]{1,0:T(8,128)(2,1)}, u32[]{:S(2)}, u32[]{:S(2)}) collective-permute-start(bf16[3072,512]{1,0:T(8,128)(2,1)} %ints_ref.1), channel_id=1, source_target_pairs={{0,257},{1,256},{256,1},{257,0},{2,259},{3,258},{258,3},{259,2},{4... | collective-permute-start | bytes 9437192 | tf_op jit(solution)/shard_map/ppermute | solution.py:328
  5.5 12.9 %collective-permute-start = (bf16[1024,96]{0,1:T(8,128)(2,1)}, bf16[1024,96]{0,1:T(8,128)(2,1)S(1)}, u32[]{:S(2)}, u32[]{:S(2)}) collective-permute-start(bf16[1024,96]{0,1:T(8,128)(2,1)} %param.8), channel_id=1, source_target_pairs={{0,1},{1,0},{2,3},{3,2},{4,5},{5,4},{6,7},{7,6},{8,9},{9,8},{10,11... | collective-permute-start | bytes 589832 | tf_op jit(solution)/shard_map/ppermute | solution.py:329
  10.0 62.0 %copy-start.3 = (s32[1,32]{1,0:T(1,128)S(1)}, s32[1,32]{1,0:T(1,128)}, u32[]{:S(2)}) copy-start(s32[1,32]{1,0:T(1,128)} %get-tuple-element.10.slot) | copy-start | bytes 388
  10.0 69.7 %all-to-all-start.1 = ((bf16[16,32,128]{2,1,0:T(8,128)(2,1)}), bf16[16,32,128]{2,1,0:T(8,128)(2,1)S(1)}, u32[]{:S(2)}, u32[]{:S(2)}) async-start(bf16[16,32,128]{2,1,0:T(8,128)(2,1)} %get-tuple-element.14), calls=%async_computation.1 | async-start | bytes 262144 | tf_op jit(solution)/shard_map/all_to_all | solution.py:331
  18.4 0.7 copy-start.4
  22.6 49.5 %copy-start = (bf16[3072,512]{1,0:T(8,128)(2,1)S(1)}, bf16[3072,512]{1,0:T(8,128)(2,1)}, u32[]{:S(2)}) copy-start(bf16[3072,512]{1,0:T(8,128)(2,1)} %ints_ref.1) | copy-start | bytes 9437188
  79.7 43.0 %copy-start.1 = (bf16[1,32,32]{2,1,0:T(8,128)(2,1)S(1)}, bf16[1,32,32]{2,1,0:T(8,128)(2,1)}, u32[]{:S(2)}) copy-start(bf16[1,32,32]{2,1,0:T(8,128)(2,1)} %mix_ref.1) | copy-start | bytes 6148
  79.7 43.0 %copy-start.2 = (f32[512]{0:T(512)S(1)}, f32[512]{0:T(512)}, u32[]{:S(2)}) copy-start(f32[512]{0:T(512)} %param.14) | copy-start | bytes 6148
